TPU v7x, 32 devices: a whole 2x2x4 slice. The times are simulated.
32 devices in a mesh: dp: 8 (over z, y), mp: 4 (over x, core).
Axes of the slice: x: 2, y: 2, z: 4, core: 2. Of those that a mesh axis runs over, the one named last changes fastest.
Arguments:
- features: bfloat16 [8192, 9216], P('dp', 'mp'), may hold values from -18 to 18
- labels: int32 [8192], P('dp'), may hold values from 0 to 999
- noise_six: bfloat16 [73728, 4096], P('dp', 'mp'), may hold values from 0 to 1
- noise_seven: bfloat16 [32768, 4096], P('dp', 'mp'), may hold values from 0 to 1
- noise_eight: bfloat16 [32768, 1000], P(('dp', 'mp')), may hold values from 0 to 1
- w_six: float32 [9216, 4096], P('dp', 'mp'), may hold values from -0.0625 to 0.0625
- w_seven: float32 [4096, 4096], P('dp', 'mp'), may hold values from -0.125 to 0.125
- w_eight: float32 [4096, 1000], P(('mp', 'dp')), may hold values from -0.1875 to 0.1875
- m_six: float32 [9216, 4096], P('dp', 'mp'), may hold values from -2.6119556e-05 to 2.6119556e-05
- m_seven: float32 [4096, 4096], P('dp', 'mp'), may hold values from -2.6119556e-05 to 2.6119556e-05
- m_eight: float32 [4096, 1000], P(('mp', 'dp')), may hold values from -2.6119556e-05 to 2.6119556e-05
- v_six: float32 [9216, 4096], P('dp', 'mp'), may hold values from 4.2639454e-11 to 1.7055782e-10
- v_seven: float32 [4096, 4096], P('dp', 'mp'), may hold values from 4.2639454e-11 to 1.7055782e-10
- v_eight: float32 [4096, 1000], P(('mp', 'dp')), may hold values from 4.2639454e-11 to 1.7055782e-10
- biases: float32 [2, 4096], P(None, 'mp'), may hold values from -0.5 to 0.5
- bias_out: float32 [1000], replicated, may hold values from -0.5 to 0.5
- m_biases: float32 [2, 4096], P(None, 'mp'), may hold values from -5.2239113e-05 to 5.2239113e-05
- v_biases: float32 [2, 4096], P(None, 'mp'), may hold values from 1.3644626e-10 to 6.8223127e-10
- m_bias_out: float32 [1000], replicated, may hold values from -0.0002611956 to 0.0002611956
- v_bias_out: float32 [1000], replicated, may hold values from 2.1319728e-09 to 3.4111565e-08
Outputs:
- loss: float32 [], replicated
- grad_norm: float32 [], replicated
- new_six: float32 [9216, 4096], P('dp', 'mp')
- new_seven: float32 [4096, 4096], P('dp', 'mp')
- new_eight: float32 [4096, 1000], P(('mp', 'dp'))
- new_m_six: float32 [9216, 4096], P('dp', 'mp')
- new_m_seven: float32 [4096, 4096], P('dp', 'mp')
- new_m_eight: float32 [4096, 1000], P(('mp', 'dp'))
- new_v_six: float32 [9216, 4096], P('dp', 'mp')
- new_v_seven: float32 [4096, 4096], P('dp', 'mp')
- new_v_eight: float32 [4096, 1000], P(('mp', 'dp'))
- copy_six: bfloat16 [9216, 4096], P('dp', 'mp')
- copy_seven: bfloat16 [4096, 4096], P('dp', 'mp')
- copy_eight: bfloat16 [4096, 1000], P(('mp', 'dp'))
- new_biases: float32 [2, 4096], P(None, 'mp')
- new_bias_out: float32 [1000], replicated
- new_m_biases: float32 [2, 4096], P(None, 'mp')
- new_v_biases: float32 [2, 4096], P(None, 'mp')
- new_m_bias_out: float32 [1000], replicated
- new_v_bias_out: float32 [1000], replicated
All inputs are finite; a program needn't handle non-finite values.
Results may differ from a plain program's by a relative error of at most 0.006.
The roundings to bfloat16 on the way count: a program that leaves them out, or rounds other values in their place, can miss the bound.
Values may be sent and summed in bfloat16 or wider, within the bound.
No kernel may reach another device: no remote copies, remote signals or barrier semaphores. Data moves between devices by JAX's collectives and lax.ppermute only.
A program may use at most 320 MiB of HBM per device.

v0:
```python
import jax
import jax.numpy as jnp
from jax import lax
from jax.sharding import PartitionSpec as P

STEP = 3


beta_one = 0.5
beta_two = 0.5
learn_rate = 0.01
bias_rate = 0.05
decay_rate = 0.1
adam_eps = 1e-08
clip_norm = 0.05
tiny_eps = 1e-12


def matmul(left, right):
    return jnp.dot(left, right, preferred_element_type=jnp.float32)


def contract_rows(left, right):
    return lax.dot_general(
        left, right, (((0,), (0,)), ((), ())), preferred_element_type=jnp.float32
    )


def against_rows(left, right):
    return lax.dot_general(
        left, right, (((1,), (1,)), ((), ())), preferred_element_type=jnp.float32
    )


def layer_forward(pre_sum, bias_row):
    pre_act = pre_sum + bias_row
    return (pre_act, jax.nn.silu(pre_act).astype(jnp.bfloat16))


def layer_backward(inputs, pre_act, upstream):
    sigmoid_val = jax.nn.sigmoid(pre_act)
    slope = sigmoid_val * (1.0 + pre_act * (1.0 - sigmoid_val))
    delta_act = (upstream * slope).astype(jnp.bfloat16)
    weight_grad = contract_rows(inputs, delta_act)
    bias_grad = jnp.sum(delta_act.astype(jnp.float32), axis=0)
    return (weight_grad, bias_grad, delta_act)


def clip_shard(grad_block):
    spread = jnp.sqrt(jnp.mean(grad_block * grad_block))
    clipped = jnp.clip(grad_block, -2.5 * spread, 2.5 * spread)
    return (clipped, jnp.max(jnp.abs(clipped)))


def soft_ternary(clipped, peak_val, noise_val):
    ratio = clipped / (peak_val + tiny_eps)
    value = jnp.clip(4.0 * ratio, -1.0, 1.0) * jnp.clip(
        2.0 * (jnp.abs(ratio) - noise_val.astype(jnp.float32)) + 0.5, 0.0, 1.0
    )
    return value.astype(jnp.bfloat16)


def adam_step(weight, moment, second, grad_val, decay, rate):
    moment_new = beta_one * moment + (1.0 - beta_one) * grad_val
    second_new = beta_two * second + (1.0 - beta_two) * grad_val * grad_val
    first_fix = 1.0 - beta_one**STEP
    second_fix = 1.0 - beta_two**STEP
    weight_new = weight - rate * (
        moment_new / first_fix / (jnp.sqrt(second_new / second_fix) + adam_eps) + decay * weight
    )
    return (weight_new, moment_new, second_new)


def shards(
    features,
    labels,
    noise_six,
    noise_seven,
    noise_eight,
    w_six,
    w_seven,
    w_eight,
    m_six,
    m_seven,
    m_eight,
    v_six,
    v_seven,
    v_eight,
    biases,
    bias_out,
    m_biases,
    v_biases,
    m_bias_out,
    v_bias_out,
):
    batch_rows = features.shape[0]
    replicas = lax.axis_size("dp")
    tokens = batch_rows * replicas
    cast_six = w_six.astype(jnp.bfloat16)
    cast_seven = w_seven.astype(jnp.bfloat16)
    cast_eight = w_eight.astype(jnp.bfloat16)
    inputs = lax.all_gather(features, "mp", axis=1, tiled=True)
    kept_six, kept_seven, kept_eight = (
        lax.all_gather(cast_six, "dp", axis=0, tiled=True),
        lax.all_gather(cast_seven, "dp", axis=0, tiled=True),
        lax.all_gather(cast_eight, "dp", axis=0, tiled=True),
    )
    first_sum = matmul(inputs, kept_six)
    pre_six, out_six = layer_forward(first_sum, biases[0])
    hidden = lax.all_gather(out_six, "mp", axis=1, tiled=True)
    pre_seven, out_seven = layer_forward(matmul(hidden, kept_seven), biases[1])
    logits = lax.psum(matmul(out_seven, kept_eight), "mp") + bias_out
    top_logit = jnp.max(logits, axis=1, keepdims=True)
    shifted = jnp.exp(logits - top_logit)
    row_total = jnp.sum(shifted, axis=1, keepdims=True)
    log_total = top_logit[:, 0] + jnp.log(row_total[:, 0])
    classes = lax.broadcasted_iota(jnp.int32, logits.shape, 1)
    onehot = (classes == labels[:, None]).astype(jnp.float32)
    loss_part = jnp.sum(log_total - jnp.sum(onehot * logits, axis=1)) / tokens
    dlogits = ((shifted / row_total - onehot) / tokens).astype(jnp.bfloat16)
    grad_eight = contract_rows(out_seven, dlogits)
    grad_last = jnp.sum(dlogits.astype(jnp.float32), axis=0)
    upstream = against_rows(dlogits, kept_eight)
    grad_seven, grad_bias_seven, delta_seven = layer_backward(hidden, pre_seven, upstream)
    upstream_six = lax.psum_scatter(
        against_rows(delta_seven, kept_seven), "mp", scatter_dimension=1, tiled=True
    )
    grad_six, grad_bias_six, delta_six = layer_backward(inputs, pre_six, upstream_six)
    clip_six, peak_six = clip_shard(grad_six)
    clip_seven, peak_seven = clip_shard(grad_seven)
    clip_eight, peak_eight = clip_shard(grad_eight)
    top_six, top_seven, top_eight = lax.pmax((peak_six, peak_seven, peak_eight), "dp")
    tern_six = soft_ternary(clip_six, top_six, noise_six)
    tern_seven = soft_ternary(clip_seven, top_seven, noise_seven)
    tern_eight = soft_ternary(clip_eight, top_eight, noise_eight)
    count_six, count_seven, count_eight = (
        lax.psum_scatter(tern_six.astype(jnp.float32), "dp", scatter_dimension=0, tiled=True),
        lax.psum_scatter(tern_seven.astype(jnp.float32), "dp", scatter_dimension=0, tiled=True),
        lax.psum_scatter(tern_eight.astype(jnp.float32), "dp", scatter_dimension=0, tiled=True),
    )
    reduced_six = top_six * count_six
    reduced_seven = top_seven * count_seven
    reduced_eight = top_eight * count_eight
    grad_pair, grad_out, loss = lax.psum(
        (jnp.stack([grad_bias_six, grad_bias_seven]), grad_last, loss_part), "dp"
    )
    squares = (
        jnp.sum(reduced_six * reduced_six)
        + jnp.sum(reduced_seven * reduced_seven)
        + jnp.sum(reduced_eight * reduced_eight)
        + jnp.sum(grad_pair * grad_pair) / replicas
        + jnp.sum(grad_out * grad_out) / (replicas * lax.axis_size("mp"))
    )
    total_squares = lax.psum(squares, ("dp", "mp"))
    grad_norm = jnp.sqrt(total_squares)
    factor = clip_norm / jnp.maximum(grad_norm, clip_norm)
    new_six, new_m_six, new_v_six = adam_step(
        w_six, m_six, v_six, factor * reduced_six, decay_rate, learn_rate
    )
    new_seven, new_m_seven, new_v_seven = adam_step(
        w_seven, m_seven, v_seven, factor * reduced_seven, decay_rate, learn_rate
    )
    new_eight, new_m_eight, new_v_eight = adam_step(
        w_eight, m_eight, v_eight, factor * reduced_eight, decay_rate, learn_rate
    )
    new_biases, new_m_biases, new_v_biases = adam_step(
        biases, m_biases, v_biases, factor * grad_pair, 0.0, bias_rate
    )
    new_bias_out, new_m_bias_out, new_v_bias_out = adam_step(
        bias_out, m_bias_out, v_bias_out, factor * grad_out, 0.0, bias_rate
    )
    return (
        loss,
        grad_norm,
        new_six,
        new_seven,
        new_eight,
        new_m_six,
        new_m_seven,
        new_m_eight,
        new_v_six,
        new_v_seven,
        new_v_eight,
        new_six.astype(jnp.bfloat16),
        new_seven.astype(jnp.bfloat16),
        new_eight.astype(jnp.bfloat16),
        new_biases,
        new_bias_out,
        new_m_biases,
        new_v_biases,
        new_m_bias_out,
        new_v_bias_out,
    )


def solution(mesh):
    return jax.shard_map(
        shards,
        mesh=mesh,
        in_specs=(
            P("dp", "mp"),
            P("dp"),
            P("dp", "mp"),
            P("dp", "mp"),
            P(("dp", "mp"), None),
            P("dp", "mp"),
            P("dp", "mp"),
            P(("mp", "dp"), None),
            P("dp", "mp"),
            P("dp", "mp"),
            P(("mp", "dp"), None),
            P("dp", "mp"),
            P("dp", "mp"),
            P(("mp", "dp"), None),
            P(None, "mp"),
            P(),
            P(None, "mp"),
            P(None, "mp"),
            P(),
            P(),
        ),
        out_specs=(
            P(),
            P(),
            P("dp", "mp"),
            P("dp", "mp"),
            P(("mp", "dp"), None),
            P("dp", "mp"),
            P("dp", "mp"),
            P(("mp", "dp"), None),
            P("dp", "mp"),
            P("dp", "mp"),
            P(("mp", "dp"), None),
            P("dp", "mp"),
            P("dp", "mp"),
            P(("mp", "dp"), None),
            P(None, "mp"),
            P(),
            P(None, "mp"),
            P(None, "mp"),
            P(),
            P(),
        ),
        check_vma=False,
    )
```

profile of v0, /device:TPU:0, one launch (start us, length us, event | category | flops | bytes accessed | tf_op | source)
XLA Modules:
  0.0 2140.9 jit_solution(12045034476656626308)
XLA Ops:
  13.6 118.7 %all-gather.6.cloned.1.call-done = bf16[1024,9216]{1,0:T(8,128)(2,1)} async-done(((bf16[1024,2304]{1,0:T(8,128)(2,1)}), bf16[1024,9216]{1,0:T(8,128)(2,1)}) %all-gather.6.cloned.1.call-update) | async-done | bytes 18874384 | tf_op jit(solution)/shard_map/all_gather | solution.py:102
  132.3 364.6 %all-gather.8.cloned.1.call-done = bf16[9216,1024]{1,0:T(8,128)(2,1)} async-done(((bf16[1152,1024]{1,0:T(8,128)(2,1)}), bf16[9216,1024]{1,0:T(8,128)(2,1)}) %all-gather.8.cloned.1.call-update) | async-done | bytes 18874384 | tf_op jit(solution)/shard_map/all_gather | solution.py:104
  496.9 27.9 %multiply_convert_fusion.4 = (bf16[1024,1024]{1,0:T(8,128)(2,1)}, f32[1024,1024]{1,0:T(8,128)}) fusion(f32[1024]{0:T(1024)S(1)} %bitcast.38, bf16[1024,9216]{1,0:T(8,128)(2,1)} %all-gather.6.cloned.1.call-done, bf16[9216,1024]{1,0:T(8,128)(2,1)} %all-gather.8.cloned.1.call-done), kind=kOutput, calls=%fused_computation.26 | convolution fusion | flops 19333644288 | bytes 44044288 | tf_op jit(solution)/shard_map/dot_general | solution.py:20
  525.7 98.9 %all-gather.12.cloned.1.call-done = bf16[4096,1024]{1,0:T(8,128)(2,1)} async-done(((bf16[512,1024]{1,0:T(8,128)(2,1)}), bf16[4096,1024]{1,0:T(8,128)(2,1)}) %all-gather.12.cloned.1.call-update) | async-done | bytes 8388624 | tf_op jit(solution)/shard_map/all_gather | solution.py:105
  624.6 58.5 %all-gather.10.cloned.1.call-done = bf16[1024,4096]{1,0:T(8,128)(2,1)} async-done(((bf16[1024,1024]{1,0:T(8,128)(2,1)}), bf16[1024,4096]{1,0:T(8,128)(2,1)}) %all-gather.10.cloned.1.call-update) | async-done | bytes 8388624 | tf_op jit(solution)/shard_map/all_gather | solution.py:110
  683.1 15.8 multiply_convert_fusion.3
  698.9 37.1 %all-gather.14.cloned.1.call-done = bf16[1024,1000]{0,1:T(8,128)(2,1)} async-done(((bf16[128,1000]{0,1:T(8,128)(2,1)}), bf16[1024,1000]{0,1:T(8,128)(2,1)}) %all-gather.14.cloned.1.call-update) | async-done | bytes 2048016 | tf_op jit(solution)/shard_map/all_gather | solution.py:106
  742.8 82.0 %all-reduce.4.cloned.1.call-done = f32[1024,1000]{0,1:T(8,128)} async-done(((f32[1024,1000]{0,1:T(8,128)}), f32[1024,1000]{0,1:T(8,128)}) %all-reduce.4.cloned.1.call-update) | async-done | bytes 4096016 | tf_op jit(solution)/shard_map/psum | solution.py:112
  837.9 13.5 fusion.24
  859.2 20.1 multiply_reduce_fusion.1
  883.2 9.2 abs_reduce_fusion.1
  892.3 85.6 %reduce-scatter.5.cloned.1.call-done = f32[1024,1024]{1,0:T(8,128)} async-done(((f32[1024,4096]{1,0:T(8,128)}), f32[1024,1024]{1,0:T(8,128)}) %reduce-scatter.5.cloned.1.call-update) | async-done | bytes 4194320 | tf_op jit(solution)/shard_map/reduce_scatter | solution.py:125
  982.2 31.8 %multiply_reduce_fusion = (f32[]{:T(128)}, f32[1024,9216]{1,0:T(8,128)}) fusion(bf16[1024,1024]{1,0:T(8,128)(2,1)S(1)} %get-tuple-element.69, bf16[1024,9216]{1,0:T(8,128)(2,1)} %all-gather.6.cloned.1.call-done), kind=kOutput, calls=%fused_computation.8 | convolution fusion | flops 19346227200 | bytes 58720260 | tf_op jit(solution)/shard_map/dot_general | solution.py:24
  1014.7 14.9 abs_reduce_fusion
  1029.6 22.0 %all-reduce.1 = (f32[]{:T(128)}, f32[]{:T(128)}, f32[]{:T(128)}) all-reduce(f32[]{:T(128)} %abs_reduce_fusion, f32[]{:T(128)} %abs_reduce_fusion.1, f32[]{:T(128)} %abs_reduce_fusion.2), channel_id=1, replica_groups=mesh['dp'=8,'mp'=4] {'dp'}, use_global_device_ids=true, to_apply=%region_9.10 | all-reduce | flops 3 | bytes 24 | tf_op jit(solution)/shard_map/pmax | solution.py:132
  1058.7 16.2 fusion.6
  1074.9 24.9 %copy.40 = bf16[9216,1024]{0,1:T(8,128)(2,1)} copy(bf16[9216,1024]{1,0:T(8,128)(2,1)} %param.22) | data formatting | bytes 37748736 | tf_op args[2]
  1100.5 33.2 %fusion.5 = f32[9216,1024]{0,1:T(8,128)} fusion(bf16[9216,1024]{0,1:T(8,128)(2,1)} %copy.40, f32[]{:T(128)S(6)} %add.191, f32[1024,9216]{1,0:T(8,128)} %get-tuple-element.79, f32[]{:T(128)S(6)} %mul.303, f32[]{:T(128)S(6)} %mul.302), kind=kLoop, calls=%fused_computation.9 | loop fusion | flops 132120576 | bytes 94371856 | tf_op jit(solution)/shard_map/convert_element_type | solution.py:137
  1147.1 34.9 %all-reduce = (f32[]{:T(128)}, f32[2,1024]{1,0:T(2,128)S(1)}, f32[1000]{0:T(1024)S(1)}) all-reduce(f32[]{:T(128)S(6)} %div.110, f32[2,1024]{1,0:T(2,128)S(1)} %pad_maximum_fusion, f32[1000]{0:T(1024)S(1)} %copy-done.17), channel_id=1, replica_groups=mesh['dp'=8,'mp'=4] {'dp'}, use_global_device_ids=true, to_apply=%region_5.6 | all-reduce | flops 3049 | bytes 24392 | tf_op jit(solution)/shard_map/psum | solution.py:144
  1187.0 238.8 %reduce-scatter.9.cloned.1.call-done = f32[512,1024]{1,0:T(8,128)} async-done(((f32[4096,1024]{1,0:T(8,128)}), f32[512,1024]{1,0:T(8,128)}) %reduce-scatter.9.cloned.1.call-update) | async-done | bytes 2097168 | tf_op jit(solution)/shard_map/reduce_scatter | solution.py:138
  1429.3 603.9 %reduce-scatter.7.cloned.1.call-done = f32[1152,1024]{0,1:T(8,128)} async-done(((f32[9216,1024]{0,1:T(8,128)}), f32[1152,1024]{0,1:T(8,128)}) %reduce-scatter.7.cloned.1.call-update) | async-done | bytes 4718608 | tf_op jit(solution)/shard_map/reduce_scatter | solution.py:137
  2046.0 39.6 %psum.39 = f32[]{:T(128)} all-reduce(f32[]{:T(128)S(6)} %add.203), channel_id=1, replica_groups=mesh['dp'=8,'mp'=4] {'dp','mp'}, use_global_device_ids=true, to_apply=%region_29.30 | all-reduce | flops 1 | bytes 8 | tf_op jit(solution)/shard_map/psum | solution.py:154
  2086.3 12.9 fusion.20
  2124.6 8.0 fusion.18
  (106 shorter events, 103.4 us)
Async XLA Ops:
  7.2 125.1 %all-gather.6.cloned.1.call-start = ((), (), s32[]{:S(2)}) async-start(), calls=%async_computation.4 | async-start | bytes 23592960 | tf_op jit(solution)/shard_map/all_gather | solution.py:102
  7.9 4.4 copy-start.1
  7.9 489.0 %all-gather.8.cloned.1.call-start = ((), (), s32[]{:S(2)}) async-start(), calls=%async_computation.5 | async-start | bytes 21233664 | tf_op jit(solution)/shard_map/all_gather | solution.py:104
  12.3 612.3 %all-gather.12.cloned.1.call-start = ((), (), s32[]{:S(2)}) async-start(), calls=%async_computation.7 | async-start | bytes 9437184 | tf_op jit(solution)/shard_map/all_gather | solution.py:105
  13.5 669.6 %all-gather.10.cloned.1.call-start = ((), (), s32[]{:S(2)}) async-start(), calls=%async_computation.6 | async-start | bytes 10485760 | tf_op jit(solution)/shard_map/all_gather | solution.py:110
  496.9 28.0 %copy-start.3 = (f32[128,1000]{0,1:T(8,128)S(1)}, f32[128,1000]{0,1:T(8,128)}, u32[]{:S(2)}) copy-start(f32[128,1000]{0,1:T(8,128)} %param.27) | copy-start | bytes 1536004
  524.8 211.2 %all-gather.14.cloned.1.call-start = ((), (), s32[]{:S(2)}) async-start(), calls=%async_computation.8 | async-start | bytes 2304000 | tf_op jit(solution)/shard_map/all_gather | solution.py:106
  525.6 299.2 %all-reduce.4.cloned.1.call-start = ((), (), s32[]{:S(2)}) async-start(), calls=%async_computation.9 | async-start | bytes 8192000 | tf_op jit(solution)/shard_map/psum | solution.py:112
  736.0 88.8 %copy-start.7 = (f32[1000]{0:T(1024)S(1)}, f32[1000]{0:T(1024)}, u32[]{:S(2)}) copy-start(f32[1000]{0:T(1024)} %param.35) | copy-start | bytes 12004
  742.5 84.9 %copy-start.16 = (s32[1024]{0:T(1024)S(1)}, s32[1024]{0:T(1024)}, u32[]{:S(2)}) copy-start(s32[1024]{0:T(1024)} %param.21) | copy-start | bytes 12292
  742.6 235.3 %reduce-scatter.5.cloned.1.call-start = ((), (), s32[]{:S(2)}) async-start(), calls=%async_computation.10 | async-start | bytes 20971520 | tf_op jit(solution)/shard_map/reduce_scatter | solution.py:125
  830.0 7.9 copy-start.11
  830.0 7.9 slice-start
  832.2 5.7 slice-start.1
  851.5 333.1 %reduce-scatter.11.cloned.1.call-start = ((), (), s32[]{:S(2)}) async-start(), calls=%async_computation.13 | async-start | bytes 4608000 | tf_op jit(solution)/shard_map/reduce_scatter | solution.py:139
  1014.6 37.6 %copy-start.6 = (bf16[1024,1000]{0,1:T(8,128)(2,1)S(1)}, bf16[1024,1000]{0,1:T(8,128)(2,1)}, u32[]{:S(2)}) copy-start(bf16[1024,1000]{0,1:T(8,128)(2,1)} %param.24) | copy-start | bytes 6144004
  1058.0 367.9 %reduce-scatter.9.cloned.1.call-start = ((), (), s32[]{:S(2)}) async-start(), calls=%async_computation.12 | async-start | bytes 18874368 | tf_op jit(solution)/shard_map/reduce_scatter | solution.py:138
  1074.9 958.3 %reduce-scatter.7.cloned.1.call-start = ((), (), s32[]{:S(2)}) async-start(), calls=%async_computation.11 | async-start | bytes 42467328 | tf_op jit(solution)/shard_map/reduce_scatter | solution.py:137
  1139.7 6.1 copy-start.10
  1139.7 6.1 copy-start.12
  1139.7 6.1 copy-start.15
  1139.7 7.4 copy-start.22
  1139.7 7.4 copy-start.17
  2119.9 4.7 copy-start.2
  (13 other events, 41.6 us)
Sparse Core Ops, SparseCore 0:
  9.6 122.6 all-gather.5
  134.4 362.4 all-gather.7
  499.6 124.8 all-gather.11
  626.6 56.4 all-gather.9
  685.5 50.4 all-gather.13
  742.7 82.0 all-reduce.3
  851.6 126.2 reduce-scatter.4
  1058.1 81.4 reduce-scatter.10
  1143.5 282.3 reduce-scatter.8
  1430.1 603.0 reduce-scatter.6
where the time goes:
time: 2150 us; the launch traced here: 2140 us
  waiting for transfers between devices  1690 us (79%)
  other arithmetic  137 us (6%)
  matrix products  128 us (6%)
  blocking collectives  96.5 us (4%)
  local copies, waits for them, and re-layouts  64.5 us (3%)
  between operations  24.7 us (1%)
    reduce_scatter x1, waiting for transfers between devices, shards(): lax.psum_scatter(tern_six.astype(jnp.float32), 'dp', scatter_dimension=0,...  604 us
    all_gather x1, waiting for transfers between devices, shards(): lax.all_gather(cast_six, 'dp', axis=0, tiled=True)  365 us
    reduce_scatter x1, waiting for transfers between devices, shards(): lax.psum_scatter(tern_seven.astype(jnp.float32), 'dp', scatter_dimension=...  239 us
    all_gather x1, waiting for transfers between devices, shards(): inputs = lax.all_gather(features, 'mp', axis=1, tiled=True)  119 us
    all_gather x1, waiting for transfers between devices, shards(): lax.all_gather(cast_seven, 'dp', axis=0, tiled=True)  98.9 us
    reduce_scatter x1, waiting for transfers between devices, shards(): lax.psum_scatter(against_rows(delta_seven, kept_seven), 'mp', scatter_dim...  85.6 us
    psum x1, waiting for transfers between devices, shards(): logits = lax.psum(matmul(out_seven, kept_eight), 'mp') + bias_out  82 us
    unnamed x62, local copies, waits for them, and re-layouts  64.5 us
  transfers between devices with their start and end apart: 10, of which 9 were waited for; matrix products, arithmetic and copies ran while one was open for 9% of the time, Pallas kernels for 0%

commit v1 on v0

--- a/solution.py
+++ b/solution.py
@@ -37,22 +37,75 @@
     return (pre_act, jax.nn.silu(pre_act).astype(jnp.bfloat16))
 
 
-def layer_backward(inputs, pre_act, upstream):
+def layer_delta(pre_act, upstream):
     sigmoid_val = jax.nn.sigmoid(pre_act)
     slope = sigmoid_val * (1.0 + pre_act * (1.0 - sigmoid_val))
-    delta_act = (upstream * slope).astype(jnp.bfloat16)
-    weight_grad = contract_rows(inputs, delta_act)
-    bias_grad = jnp.sum(delta_act.astype(jnp.float32), axis=0)
-    return (weight_grad, bias_grad, delta_act)
-
-
-def clip_shard(grad_block):
-    spread = jnp.sqrt(jnp.mean(grad_block * grad_block))
-    clipped = jnp.clip(grad_block, -2.5 * spread, 2.5 * spread)
-    return (clipped, jnp.max(jnp.abs(clipped)))
-
-
-def soft_ternary(clipped, peak_val, noise_val):
+    return (upstream * slope).astype(jnp.bfloat16)
+
+
+def grad_limits(grad_block):
+    limit = 2.5 * jnp.sqrt(jnp.mean(grad_block * grad_block))
+    return (limit, jnp.minimum(jnp.max(jnp.abs(grad_block)), limit))
+
+
+def swap(value, axis, bit):
+    size = lax.axis_size(axis)
+    return lax.ppermute(value, axis, [(i, i ^ bit) for i in range(size)])
+
+
+def turn(value):
+    size = lax.axis_size("dp")
+    return lax.ppermute(value, "dp", [(i, (i + 2) % size) for i in range(size)])
+
+
+def spread_bits(axis):
+    bit = 1
+    while bit < lax.axis_size(axis):
+        yield bit
+        bit *= 2
+
+
+def fold(value, combine, axes):
+    for axis in axes:
+        for bit in spread_bits(axis):
+            value = combine(value, swap(value, axis, bit))
+    return value
+
+
+def after(value, *earlier):
+    return lax.optimization_barrier((value, earlier))[0]
+
+
+def place(row, block_rows):
+    if block_rows is None:
+        return row
+    mine = lax.axis_index("mp")
+    return ((row // block_rows) ^ mine) * block_rows + row % block_rows
+
+
+def owner(step, flip):
+    size = lax.axis_size("dp")
+    here = lax.axis_index("dp")
+    return ((here + size - 2 * step) % size) ^ flip
+
+
+def put(whole, piece, row):
+    return lax.dynamic_update_slice(whole, piece, (row, 0))
+
+
+def take(whole, row, rows):
+    return lax.dynamic_slice_in_dim(whole, row, rows, 0)
+
+
+def xor_columns(value):
+    blocks = {0: value}
+    for bit in reversed(list(spread_bits("mp"))):
+        blocks |= {step ^ bit: swap(item, "mp", bit) for step, item in blocks.items()}
+    return jnp.concatenate([blocks[step] for step in sorted(blocks)], axis=1)
+
+
+def soft_ternary(grad_block, limit, peak_val, noise_val):
+    clipped = jnp.clip(grad_block, -limit, limit)
     ratio = clipped / (peak_val + tiny_eps)
     value = jnp.clip(4.0 * ratio, -1.0, 1.0) * jnp.clip(
         2.0 * (jnp.abs(ratio) - noise_val.astype(jnp.float32)) + 0.5, 0.0, 1.0
@@ -93,65 +146,136 @@
     m_bias_out,
     v_bias_out,
 ):
+    mine = lax.axis_index("mp")
+    here = lax.axis_index("dp")
+    replicas = lax.axis_size("dp")
+    ways = lax.axis_size("mp")
+    rings = replicas // 2
     batch_rows = features.shape[0]
-    replicas = lax.axis_size("dp")
     tokens = batch_rows * replicas
+    part_rows = batch_rows // ways
+
+    def gather(shard, block_rows):
+        rows = shard.shape[0]
+        whole = jnp.zeros((rows * replicas, shard.shape[1]), shard.dtype)
+        for step in range(rings):
+            other = swap(shard, "dp", 1)
+            whole = put(whole, shard, place(owner(step, 0) * rows, block_rows))
+            whole = put(whole, other, place(owner(step, 1) * rows, block_rows))
+            last = shard
+            if step < rings - 1:
+                shard = turn(shard)
+        return whole, last
+
     cast_six = w_six.astype(jnp.bfloat16)
     cast_seven = w_seven.astype(jnp.bfloat16)
     cast_eight = w_eight.astype(jnp.bfloat16)
-    inputs = lax.all_gather(features, "mp", axis=1, tiled=True)
-    kept_six, kept_seven, kept_eight = (
-        lax.all_gather(cast_six, "dp", axis=0, tiled=True),
-        lax.all_gather(cast_seven, "dp", axis=0, tiled=True),
-        lax.all_gather(cast_eight, "dp", axis=0, tiled=True),
-    )
-    first_sum = matmul(inputs, kept_six)
-    pre_six, out_six = layer_forward(first_sum, biases[0])
-    hidden = lax.all_gather(out_six, "mp", axis=1, tiled=True)
+    inputs = xor_columns(features)
+    kept_six, last_six = gather(cast_six, features.shape[1])
+    cast_seven = after(cast_seven, last_six)
+    kept_seven, last_seven = gather(cast_seven, biases.shape[1])
+    cast_eight = after(cast_eight, last_seven)
+    kept_eight, _ = gather(cast_eight, None)
+    pre_six, out_six = layer_forward(matmul(inputs, kept_six), biases[0])
+    hidden = xor_columns(out_six)
     pre_seven, out_seven = layer_forward(matmul(hidden, kept_seven), biases[1])
-    logits = lax.psum(matmul(out_seven, kept_eight), "mp") + bias_out
+
+    def part(step):
+        return matmul(take(out_seven, (mine ^ step) * part_rows, part_rows), kept_eight)
+
+    parts = {step: part(step) for step in range(ways)}
+    for bit in spread_bits("mp"):
+        for step in range(0, ways, 2 * bit):
+            parts[step] = parts[step] + swap(parts[step + bit], "mp", bit)
+    logits = parts[0] + bias_out
+    labels_part = lax.dynamic_slice_in_dim(labels, mine * part_rows, part_rows, 0)
     top_logit = jnp.max(logits, axis=1, keepdims=True)
     shifted = jnp.exp(logits - top_logit)
     row_total = jnp.sum(shifted, axis=1, keepdims=True)
     log_total = top_logit[:, 0] + jnp.log(row_total[:, 0])
     classes = lax.broadcasted_iota(jnp.int32, logits.shape, 1)
-    onehot = (classes == labels[:, None]).astype(jnp.float32)
+    onehot = (classes == labels_part[:, None]).astype(jnp.float32)
     loss_part = jnp.sum(log_total - jnp.sum(onehot * logits, axis=1)) / tokens
-    dlogits = ((shifted / row_total - onehot) / tokens).astype(jnp.bfloat16)
+    dz_part = ((shifted / row_total - onehot) / tokens).astype(jnp.bfloat16)
+    dz_parts = [dz_part]
+    for bit in spread_bits("mp"):
+        dz_parts = dz_parts + [swap(item, "mp", bit) for item in dz_parts]
+    dlogits = jnp.zeros((batch_rows, logits.shape[1]), jnp.bfloat16)
+    for step, item in enumerate(dz_parts):
+        dlogits = put(dlogits, item, (mine ^ step) * part_rows)
+
+    delta_seven = layer_delta(pre_seven, against_rows(dlogits, kept_eight))
+    width = biases.shape[1]
+    ups = {
+        step: against_rows(delta_seven, kept_seven[step * width : (step + 1) * width])
+        for step in range(ways)
+    }
+    for bit in spread_bits("mp"):
+        for step in range(0, ways, 2 * bit):
+            ups[step] = ups[step] + swap(ups[step + bit], "mp", bit)
+    delta_six = layer_delta(pre_six, ups[0])
     grad_eight = contract_rows(out_seven, dlogits)
-    grad_last = jnp.sum(dlogits.astype(jnp.float32), axis=0)
-    upstream = against_rows(dlogits, kept_eight)
-    grad_seven, grad_bias_seven, delta_seven = layer_backward(hidden, pre_seven, upstream)
-    upstream_six = lax.psum_scatter(
-        against_rows(delta_seven, kept_seven), "mp", scatter_dimension=1, tiled=True
-    )
-    grad_six, grad_bias_six, delta_six = layer_backward(inputs, pre_six, upstream_six)
-    clip_six, peak_six = clip_shard(grad_six)
-    clip_seven, peak_seven = clip_shard(grad_seven)
-    clip_eight, peak_eight = clip_shard(grad_eight)
-    top_six, top_seven, top_eight = lax.pmax((peak_six, peak_seven, peak_eight), "dp")
-    tern_six = soft_ternary(clip_six, top_six, noise_six)
-    tern_seven = soft_ternary(clip_seven, top_seven, noise_seven)
-    tern_eight = soft_ternary(clip_eight, top_eight, noise_eight)
-    count_six, count_seven, count_eight = (
-        lax.psum_scatter(tern_six.astype(jnp.float32), "dp", scatter_dimension=0, tiled=True),
-        lax.psum_scatter(tern_seven.astype(jnp.float32), "dp", scatter_dimension=0, tiled=True),
-        lax.psum_scatter(tern_eight.astype(jnp.float32), "dp", scatter_dimension=0, tiled=True),
-    )
-    reduced_six = top_six * count_six
-    reduced_seven = top_seven * count_seven
-    reduced_eight = top_eight * count_eight
-    grad_pair, grad_out, loss = lax.psum(
-        (jnp.stack([grad_bias_six, grad_bias_seven]), grad_last, loss_part), "dp"
-    )
+    grad_seven = contract_rows(hidden, delta_seven)
+    limit_seven, peak_seven = grad_limits(grad_seven)
+    limit_eight, peak_eight = grad_limits(grad_eight)
+    tops = fold(jnp.stack([peak_seven, peak_eight]), jnp.maximum, ("dp",))
+    top_seven, top_eight = tops[0], tops[1]
+    grad_six = contract_rows(inputs, delta_six)
+    limit_six, peak_six = grad_limits(grad_six)
+    top_six = fold(peak_six, jnp.maximum, ("dp",))
+
+    def reduce(grad, limit, top, noise, rows, block_rows, hold):
+        def tern(step, flip):
+            row = owner(step, flip) * rows
+            return soft_ternary(
+                take(grad, place(row, block_rows), rows), limit, top, take(noise, row, rows)
+            )
+
+        total = None
+        first = None
+        for step in list(range(1, rings)) + [0]:
+            away = tern(step, 1)
+            if hold is not None:
+                away = after(away, hold)
+            near = swap(away, "dp", 1)
+            pair = tern(step, 0).astype(jnp.float32) + near.astype(jnp.float32)
+            if total is not None:
+                pair = pair + turn(total).astype(jnp.float32)
+            total = pair.astype(jnp.bfloat16)
+            first = near if step == rings - 1 else first
+        return top * pair, first
+
+    reduced_eight, mark = reduce(
+        grad_eight, limit_eight, top_eight, noise_eight, w_eight.shape[0], None, None
+    )
+    reduced_seven, mark = reduce(
+        grad_seven, limit_seven, top_seven, noise_seven, w_seven.shape[0], width, None
+    )
+    reduced_six, mark = reduce(
+        grad_six, limit_six, top_six, noise_six, w_six.shape[0], features.shape[1], None
+    )
+    bias_sums = fold(
+        jnp.concatenate(
+            [
+                jnp.sum(delta_six.astype(jnp.float32), axis=0),
+                jnp.sum(delta_seven.astype(jnp.float32), axis=0),
+                jnp.sum(dlogits.astype(jnp.float32), axis=0),
+            ]
+        ),
+        jnp.add,
+        ("dp",),
+    )
+    grad_pair = bias_sums[: 2 * width].reshape(2, width)
+    grad_out = bias_sums[2 * width :]
     squares = (
         jnp.sum(reduced_six * reduced_six)
         + jnp.sum(reduced_seven * reduced_seven)
         + jnp.sum(reduced_eight * reduced_eight)
         + jnp.sum(grad_pair * grad_pair) / replicas
-        + jnp.sum(grad_out * grad_out) / (replicas * lax.axis_size("mp"))
-    )
-    total_squares = lax.psum(squares, ("dp", "mp"))
+        + jnp.sum(grad_out * grad_out) / (replicas * ways)
+    )
+    totals = fold(jnp.stack([squares, loss_part]), jnp.add, ("dp", "mp"))
+    total_squares, loss = totals[0], totals[1]
     grad_norm = jnp.sqrt(total_squares)
     factor = clip_norm / jnp.maximum(grad_norm, clip_norm)
     new_six, new_m_six, new_v_six = adam_step(

time: 2150 us -> 1140 us (0.53)
  waiting for transfers between devices: 1690 us -> 622 us
  local copies, waits for them, and re-layouts: 64.5 us -> 187 us
  blocking collectives: 96.5 us -> 0 us
  starting transfers between devices: 1.03 us -> 67.1 us
  other arithmetic: 137 us -> 106 us
    reduce_scatter x4 -> x0, waiting for transfers between devices: 928 us -> none  [the longest x1 604 us: shards(): lax.psum_scatter(tern_six.astype(jnp.float32), 'dp', scatter_dimension=0,...]
    all_gather x5 -> x0, waiting for transfers between devices: 678 us -> none  [the longest x1 365 us: shards(): lax.all_gather(cast_six, 'dp', axis=0, tiled=True)]
    ppermute x0 -> x71, waiting for transfers between devices: none -> 622 us  [the longest x53 470 us: swap(): return lax.ppermute(value, axis, [(i, i ^ bit) for i in range(size)])]
    dynamic_update_slice x0 -> x27, local copies, waits for them, and re-layouts: none -> 150 us  [put(): return lax.dynamic_update_slice(whole, piece, (row, 0))]
    psum x1 -> x0, waiting for transfers between devices: 82 us -> none  [shards(): logits = lax.psum(matmul(out_seven, kept_eight), 'mp') + bias_out]
    psum x2 -> x0, blocking collectives: 74.5 us -> none  [the longest x1 39.6 us: shards(): total_squares = lax.psum(squares, ('dp', 'mp'))]
    ppermute x0 -> x71, starting transfers between devices: none -> 67.1 us  [the longest x53 52 us: swap(): return lax.ppermute(value, axis, [(i, i ^ bit) for i in range(size)])]
    unnamed x62 -> x79, local copies, waits for them, and re-layouts: 64.5 us -> 18.8 us
  transfers between devices with their start and end apart: 10 -> 71, of which waited for: 9 -> 39; matrix products, arithmetic and copies ran while one was open for 9% -> 27% of each run, Pallas kernels for 0% -> 0%
where the time goes in v1:
time: 1140 us; the launch traced here: 1130 us
  waiting for transfers between devices  622 us (55%)
  local copies, waits for them, and re-layouts  187 us (16%)
  matrix products  137 us (12%)
  other arithmetic  106 us (9%)
  starting transfers between devices  67.1 us (6%)
  between operations  14.9 us (1%)
    ppermute x53, waiting for transfers between devices, swap(): return lax.ppermute(value, axis, [(i, i ^ bit) for i in range(size)])  470 us
    ppermute x18, waiting for transfers between devices, turn(): return lax.ppermute(value, 'dp', [(i, (i + 2) % size) for i in range(size)])  152 us
    dynamic_update_slice x27, local copies, waits for them, and re-layouts, put(): return lax.dynamic_update_slice(whole, piece, (row, 0))  150 us
    dot_general x3, matrix products, contract_rows(): lax.dot_general(left, right, (((0,), (0,)), ((), ())), preferred_element_...  59.3 us
    dot_general x6, matrix products, matmul(): return jnp.dot(left, right, preferred_element_type=jnp.float32)  53.4 us
    ppermute x53, starting transfers between devices, swap(): return lax.ppermute(value, axis, [(i, i ^ bit) for i in range(size)])  52 us
    convert_element_type x6, other arithmetic, soft_ternary(): return value.astype(jnp.bfloat16)  36.6 us
    convert_element_type x6, other arithmetic, reduce(): total = pair.astype(jnp.bfloat16)  25.7 us
  transfers between devices with their start and end apart: 71, of which 39 were waited for; matrix products, arithmetic and copies ran while one was open for 27% of the time, Pallas kernels for 0%

profile of v1, /device:TPU:0, one launch (start us, length us, event | category | flops | bytes accessed | tf_op | source)
XLA Modules:
  0.0 1133.7 jit_solution(15639075030236787472)
XLA Ops:
  8.0 53.0 %collective-permute-done.4 = bf16[1152,1024]{1,0:T(8,128)(2,1)S(1)} collective-permute-done((bf16[1152,1024]{1,0:T(8,128)(2,1)S(1)}, bf16[1152,1024]{1,0:T(8,128)(2,1)S(1)}, u32[]{:S(2)}, u32[]{:S(2)}) %collective-permute-start.4) | collective-permute-done | bytes 2359328 | tf_op jit(solution)/shard_map/ppermute | solution.py:58
  62.6 43.2 %collective-permute-done.1 = bf16[1024,2304]{1,0:T(8,128)(2,1)} collective-permute-done((bf16[1024,2304]{1,0:T(8,128)(2,1)}, bf16[1024,2304]{1,0:T(8,128)(2,1)}, u32[]{:S(2)}, u32[]{:S(2)}) %collective-permute-start.1) | collective-permute-done | bytes 4718624 | tf_op jit(solution)/shard_map/ppermute | solution.py:53
  116.8 51.0 %collective-permute-done.8 = bf16[1152,1024]{1,0:T(8,128)(2,1)} collective-permute-done((bf16[1152,1024]{1,0:T(8,128)(2,1)}, bf16[1152,1024]{1,0:T(8,128)(2,1)}, u32[]{:S(2)}, u32[]{:S(2)}) %collective-permute-start.8) | collective-permute-done | bytes 2359328 | tf_op jit(solution)/shard_map/ppermute | solution.py:58
  194.6 12.4 %dynamic_update_slice.85 = bf16[9216,1024]{1,0:T(8,128)(2,1)} dynamic-update-slice(bf16[9216,1024]{1,0:T(8,128)(2,1)} %dynamic_update_slice.84, bf16[1152,1024]{1,0:T(8,128)(2,1)} %copy-done.8, s32[]{:T(128)S(6)} %select_n.443, s32[]{:T(128)} %constant.412.clone.1) | dynamic-update-slice | bytes 4718596 | tf_op jit(solution)/shard_map/dynamic_update_slice | solution.py:93
  230.4 12.3 %dynamic_update_slice.88 = bf16[9216,1024]{1,0:T(8,128)(2,1)} dynamic-update-slice(bf16[9216,1024]{1,0:T(8,128)(2,1)} %dynamic_update_slice.87, bf16[1152,1024]{1,0:T(8,128)(2,1)} %collective-permute-done.6, s32[]{:T(128)S(6)} %select_n.454, s32[]{:T(128)} %constant.412.clone.1) | dynamic-update-slice | bytes 4718596 | tf_op jit(solution)/shard_map/dynamic_update_slice | solution.py:93
  252.3 12.3 %dynamic_update_slice.89 = bf16[9216,1024]{1,0:T(8,128)(2,1)} dynamic-update-slice(bf16[9216,1024]{1,0:T(8,128)(2,1)} %dynamic_update_slice.88, bf16[1152,1024]{1,0:T(8,128)(2,1)} %collective-permute-done.7, s32[]{:T(128)S(6)} %select_n.457, s32[]{:T(128)} %constant.412.clone.1) | dynamic-update-slice | bytes 4718596 | tf_op jit(solution)/shard_map/dynamic_update_slice | solution.py:93
  264.6 12.3 %dynamic_update_slice.90 = bf16[9216,1024]{1,0:T(8,128)(2,1)} dynamic-update-slice(bf16[9216,1024]{1,0:T(8,128)(2,1)} %dynamic_update_slice.89, bf16[1152,1024]{1,0:T(8,128)(2,1)} %collective-permute-done.8, s32[]{:T(128)S(6)} %select_n.461, s32[]{:T(128)} %constant.412.clone.1) | dynamic-update-slice | bytes 4718596 | tf_op jit(solution)/shard_map/dynamic_update_slice | solution.py:93
  281.7 12.3 %dynamic_update_slice.91 = bf16[9216,1024]{1,0:T(8,128)(2,1)} dynamic-update-slice(bf16[9216,1024]{1,0:T(8,128)(2,1)} %dynamic_update_slice.90, bf16[1152,1024]{1,0:T(8,128)(2,1)} %collective-permute-done.9, s32[]{:T(128)S(6)} %select_n.464, s32[]{:T(128)} %constant.412.clone.1) | dynamic-update-slice | bytes 4718596 | tf_op jit(solution)/shard_map/dynamic_update_slice | solution.py:93
  294.0 27.9 %multiply_convert_fusion.11 = (bf16[1024,1024]{1,0:T(8,128)(2,1)}, f32[1024,1024]{1,0:T(8,128)}) fusion(f32[1024]{0:T(1024)S(1)} %bitcast.34, bf16[1024,9216]{1,0:T(8,128)(2,1)} %constant_dynamic-update-slice_fusion.12, bf16[9216,1024]{1,0:T(8,128)(2,1)} %dynamic_update_slice.91), kind=kOutput, calls=%fused_computation.28 | convolution fusion | flops 19333644288 | bytes 44044288 | tf_op jit(solution)/shard_map/dot_general | solution.py:20
  326.4 19.9 %collective-permute-done.18 = bf16[512,1024]{1,0:T(8,128)(2,1)} collective-permute-done((bf16[512,1024]{1,0:T(8,128)(2,1)S(1)}, bf16[512,1024]{1,0:T(8,128)(2,1)}, u32[]{:S(2)}, u32[]{:S(2)}) %collective-permute-start.18) | collective-permute-done | bytes 1048608 | tf_op jit(solution)/shard_map/ppermute | solution.py:58
  346.3 20.0 %collective-permute-done.11 = bf16[1024,1024]{1,0:T(8,128)(2,1)} collective-permute-done((bf16[1024,1024]{1,0:T(8,128)(2,1)}, bf16[1024,1024]{1,0:T(8,128)(2,1)}, u32[]{:S(2)}, u32[]{:S(2)}) %collective-permute-start.11) | collective-permute-done | bytes 2097184 | tf_op jit(solution)/shard_map/ppermute | solution.py:53
  377.5 17.1 %collective-permute-done.17 = bf16[512,1024]{1,0:T(8,128)(2,1)S(1)} collective-permute-done((bf16[512,1024]{1,0:T(8,128)(2,1)S(1)}, bf16[512,1024]{1,0:T(8,128)(2,1)S(1)}, u32[]{:S(2)}, u32[]{:S(2)}) %collective-permute-start.17) | collective-permute-done | bytes 1048608 | tf_op jit(solution)/shard_map/ppermute | solution.py:53
  470.9 15.8 %multiply_convert_fusion.10 = (bf16[1024,1024]{1,0:T(8,128)(2,1)S(1)}, f32[1024,1024]{1,0:T(8,128)}) fusion(f32[1024]{0:T(1024)S(1)} %bitcast.36, bf16[4096,1024]{1,0:T(8,128)(2,1)} %dynamic_update_slice.99, bf16[1024,1024]{1,0:T(8,128)(2,1)} %collective-permute-done.12, bf16[1024,1024]{1,0:T(8,128)(2,1)} %collective-permute-done.11, ...), kind=kOutput, calls=%fused_computation.26 | convolution fusion | flops 8629780480 | bytes 23072768 | tf_op jit(solution)/shard_map/dot_general | solution.py:20
  497.4 23.5 %collective-permute-done.29 = f32[256,1000]{0,1:T(8,128)} collective-permute-done((f32[256,1000]{0,1:T(8,128)}, f32[256,1000]{0,1:T(8,128)}, u32[]{:S(2)}, u32[]{:S(2)}) %collective-permute-start.29) | collective-permute-done | bytes 1024032 | tf_op jit(solution)/shard_map/ppermute | solution.py:53
  568.8 91.2 %collective-permute-done.35 = f32[1024,1024]{1,0:T(8,128)} collective-permute-done((f32[1024,1024]{1,0:T(8,128)}, f32[1024,1024]{1,0:T(8,128)}, u32[]{:S(2)}, u32[]{:S(2)}) %collective-permute-start.35) | collective-permute-done | bytes 4194336 | tf_op jit(solution)/shard_map/ppermute | solution.py:53
  669.3 32.1 %multiply_reduce_fusion = (f32[]{:T(128)}, f32[]{:T(128)}, f32[9216,1024]{1,0:T(8,128)}) fusion(bf16[1024,9216]{1,0:T(8,128)(2,1)} %constant_dynamic-update-slice_fusion.12, bf16[1024,1024]{1,0:T(8,128)(2,1)S(1)} %get-tuple-element.88), kind=kOutput, calls=%fused_computation | convolution fusion | flops 19365101568 | bytes 58720264 | tf_op jit(solution)/shard_map/dot_general | solution.py:24
  723.4 47.9 %collective-permute-done.42 = bf16[1152,1024]{1,0:T(8,128)(2,1)S(1)} collective-permute-done((bf16[1152,1024]{1,0:T(8,128)(2,1)}, bf16[1152,1024]{1,0:T(8,128)(2,1)S(1)}, u32[]{:S(2)}, u32[]{:S(2)}) %collective-permute-start.42) | collective-permute-done | bytes 2359328 | tf_op jit(solution)/shard_map/ppermute | solution.py:53
  771.3 16.9 %multiply_convert_fusion.6 = (bf16[1152,1024]{1,0:T(8,128)(2,1)}, bf16[1152,1024]{1,0:T(8,128)(2,1)}, bf16[1152,1024]{1,0:T(8,128)(2,1)}, bf16[1152,1024]{1,0:T(8,128)(2,1)}) fusion(f32[9216,1024]{1,0:T(8,128)} %get-tuple-element.82, s32[]{:T(128)S(6)} %select_n.443, bf16[9216,1024]{1,0:T(8,128)(2,1)} %param.22, s32[]{:T(128)S(6)} %select_n.502, ...), kind=kLoop, calls=%fused_computation.20 | loop fusion | flops 66060288 | bytes 40108076 | tf_op jit(solution)/shard_map/convert_element_type | solution.py:113
  791.1 20.7 %multiply_reduce_fusion.1 = (f32[]{:T(128)}, f32[]{:T(128)}, f32[4096,1024]{1,0:T(8,128)}) fusion(bf16[1024,1024]{1,0:T(8,128)(2,1)S(1)} %copy-done.30, bf16[1024,1024]{1,0:T(8,128)(2,1)} %collective-permute-done.12, bf16[1024,1024]{1,0:T(8,128)(2,1)} %collective-permute-done.11, bf16[1024,1024]{1,0:T(8,128)(2,1)} %collective-permute-done.10, ...), kind=kOutput, calls=%fused_computation.2 | convolution fusion | flops 8640266240 | bytes 27262984 | tf_op jit(solution)/shard_map/dot_general | solution.py:24
  822.1 14.4 %collective-permute-done.46 = f32[2]{0:T(128)S(1)} collective-permute-done((f32[2]{0:T(128)S(1)}, f32[2]{0:T(128)S(1)}, u32[]{:S(2)}, u32[]{:S(2)}) %collective-permute-start.46) | collective-permute-done | bytes 40 | tf_op jit(solution)/shard_map/ppermute | solution.py:53
  863.2 15.7 %collective-permute-done.52 = bf16[512,1024]{1,0:T(8,128)(2,1)S(1)} collective-permute-done((bf16[512,1024]{1,0:T(8,128)(2,1)S(1)}, bf16[512,1024]{1,0:T(8,128)(2,1)S(1)}, u32[]{:S(2)}, u32[]{:S(2)}) %collective-permute-start.52) | collective-permute-done | bytes 1048608 | tf_op jit(solution)/shard_map/ppermute | solution.py:53
  892.3 58.4 %collective-permute-done.58 = bf16[128,1000]{0,1:T(8,128)(2,1)S(1)} collective-permute-done((bf16[128,1000]{0,1:T(8,128)(2,1)S(1)}, bf16[128,1000]{0,1:T(8,128)(2,1)S(1)}, u32[]{:S(2)}, u32[]{:S(2)}) %collective-permute-start.58) | collective-permute-done | bytes 256032 | tf_op jit(solution)/shard_map/ppermute | solution.py:53
  976.4 17.8 %collective-permute-done.50 = bf16[512,1024]{1,0:T(8,128)(2,1)S(1)} collective-permute-done((bf16[512,1024]{1,0:T(8,128)(2,1)S(1)}, bf16[512,1024]{1,0:T(8,128)(2,1)S(1)}, u32[]{:S(2)}, u32[]{:S(2)}) %collective-permute-start.50) | collective-permute-done | bytes 1048608 | tf_op jit(solution)/shard_map/ppermute | solution.py:53
  1004.2 59.2 %collective-permute-done.63 = f32[3048]{0:T(1024)S(1)} collective-permute-done((f32[3048]{0:T(1024)S(1)}, f32[3048]{0:T(1024)S(1)}, u32[]{:S(2)}, u32[]{:S(2)}) %collective-permute-start.63) | collective-permute-done | bytes 12224 | tf_op jit(solution)/shard_map/ppermute | solution.py:53
  (295 shorter events, 411.6 us)
Async XLA Ops:
  0.7 105.1 %collective-permute-start.1 = (bf16[1024,2304]{1,0:T(8,128)(2,1)}, bf16[1024,2304]{1,0:T(8,128)(2,1)}, u32[]{:S(2)}, u32[]{:S(2)}) collective-permute-start(bf16[1024,2304]{1,0:T(8,128)(2,1)} %param.20), channel_id=1, source_target_pairs={{0,2},{1,3},{2,0},{3,1},{4,6},{5,7},{6,4},{7,5},{8,10},{9,11},{10,... | collective-permute-start | bytes 14155784 | tf_op jit(solution)/shard_map/ppermute | solution.py:53
  61.0 181.7 %collective-permute-start = (bf16[1024,2304]{1,0:T(8,128)(2,1)}, bf16[1024,2304]{1,0:T(8,128)(2,1)}, u32[]{:S(2)}, u32[]{:S(2)}) collective-permute-start(bf16[1024,2304]{1,0:T(8,128)(2,1)} %param.20), channel_id=1, source_target_pairs={{0,1},{1,0},{2,3},{3,2},{4,5},{5,4},{6,7},{7,6},{8,9},{9,8},{10,11... | collective-permute-start | bytes 14155784 | tf_op jit(solution)/shard_map/ppermute | solution.py:53
  105.8 171.1 %collective-permute-start.2 = (bf16[1024,2304]{1,0:T(8,128)(2,1)}, bf16[1024,2304]{1,0:T(8,128)(2,1)}, u32[]{:S(2)}, u32[]{:S(2)}) collective-permute-start(bf16[1024,2304]{1,0:T(8,128)(2,1)} %collective-permute-done.1), channel_id=1, source_target_pairs={{0,1},{1,0},{2,3},{3,2},{4,5},{5,4},{6,7},{7,6},{8,9},{9,8},{10,11... | collective-permute-start | bytes 14155784 | tf_op jit(solution)/shard_map/ppermute | solution.py:53
  114.8 59.7 %collective-permute-start.5 = (bf16[1152,1024]{1,0:T(8,128)(2,1)S(1)}, bf16[1152,1024]{1,0:T(8,128)(2,1)S(1)}, u32[]{:S(2)}, u32[]{:S(2)}) collective-permute-start(bf16[1152,1024]{1,0:T(8,128)(2,1)S(1)} %collective-permute-done.4), channel_id=1, source_target_pairs={{0,4},{4,0},{8,12},{12,8},{16,20},{20,16},{24,28},{28,24},{1,5},{5... | collective-permute-start | bytes 7077896 | tf_op jit(solution)/shard_map/ppermute | solution.py:53
  116.3 136.0 %collective-permute-start.7 = (bf16[1152,1024]{1,0:T(8,128)(2,1)}, bf16[1152,1024]{1,0:T(8,128)(2,1)}, u32[]{:S(2)}, u32[]{:S(2)}) collective-permute-start(bf16[1152,1024]{1,0:T(8,128)(2,1)} %collective-permute-done.6), channel_id=1, source_target_pairs={{0,4},{4,0},{8,12},{12,8},{16,20},{20,16},{24,28},{28,24},{1,5},{5... | collective-permute-start | bytes 7077896 | tf_op jit(solution)/shard_map/ppermute | solution.py:53
  167.8 113.9 %collective-permute-start.9 = (bf16[1152,1024]{1,0:T(8,128)(2,1)}, bf16[1152,1024]{1,0:T(8,128)(2,1)}, u32[]{:S(2)}, u32[]{:S(2)}) collective-permute-start(bf16[1152,1024]{1,0:T(8,128)(2,1)} %collective-permute-done.8), channel_id=1, source_target_pairs={{0,4},{4,0},{8,12},{12,8},{16,20},{20,16},{24,28},{28,24},{1,5},{5... | collective-permute-start | bytes 7077896 | tf_op jit(solution)/shard_map/ppermute | solution.py:53
  175.8 101.0 %collective-permute-start.14 = (bf16[512,1024]{1,0:T(8,128)(2,1)S(1)}, bf16[512,1024]{1,0:T(8,128)(2,1)}, u32[]{:S(2)}, u32[]{:S(2)}) collective-permute-start(bf16[512,1024]{1,0:T(8,128)(2,1)S(1)} %convert_element_type.317), channel_id=1, source_target_pairs={{0,8},{4,12},{8,16},{12,20},{16,24},{20,28},{24,0},{28,4},{1,9},{5... | collective-permute-start | bytes 3145736 | tf_op jit(solution)/shard_map/ppermute | solution.py:58
  325.6 69.0 %collective-permute-start.17 = (bf16[512,1024]{1,0:T(8,128)(2,1)S(1)}, bf16[512,1024]{1,0:T(8,128)(2,1)S(1)}, u32[]{:S(2)}, u32[]{:S(2)}) collective-permute-start(bf16[512,1024]{1,0:T(8,128)(2,1)S(1)} %collective-permute-done.16), channel_id=1, source_target_pairs={{0,4},{4,0},{8,12},{12,8},{16,20},{20,16},{24,28},{28,24},{1,5},{5... | collective-permute-start | bytes 3145736 | tf_op jit(solution)/shard_map/ppermute | solution.py:53
  346.3 124.6 %collective-permute-start.10 = (bf16[1024,1024]{1,0:T(8,128)(2,1)}, bf16[1024,1024]{1,0:T(8,128)(2,1)}, u32[]{:S(2)}, u32[]{:S(2)}) collective-permute-start(bf16[1024,1024]{1,0:T(8,128)(2,1)} %get-tuple-element.76), channel_id=1, source_target_pairs={{0,1},{1,0},{2,3},{3,2},{4,5},{5,4},{6,7},{7,6},{8,9},{9,8},{10,11... | collective-permute-start | bytes 6291464 | tf_op jit(solution)/shard_map/ppermute | solution.py:53
  366.3 104.6 %collective-permute-start.12 = (bf16[1024,1024]{1,0:T(8,128)(2,1)}, bf16[1024,1024]{1,0:T(8,128)(2,1)}, u32[]{:S(2)}, u32[]{:S(2)}) collective-permute-start(bf16[1024,1024]{1,0:T(8,128)(2,1)} %collective-permute-done.11), channel_id=1, source_target_pairs={{0,1},{1,0},{2,3},{3,2},{4,5},{5,4},{6,7},{7,6},{8,9},{9,8},{10,11... | collective-permute-start | bytes 6291464 | tf_op jit(solution)/shard_map/ppermute | solution.py:53
  376.9 72.6 %collective-permute-start.23 = (bf16[128,1000]{0,1:T(8,128)(2,1)}, bf16[128,1000]{0,1:T(8,128)(2,1)}, u32[]{:S(2)}, u32[]{:S(2)}) collective-permute-start(bf16[128,1000]{0,1:T(8,128)(2,1)} %collective-permute-done.21), channel_id=1, source_target_pairs={{0,8},{4,12},{8,16},{12,20},{16,24},{20,28},{24,0},{28,4},{1,9},{5... | collective-permute-start | bytes 768008 | tf_op jit(solution)/shard_map/ppermute | solution.py:58
  394.6 69.9 %collective-permute-start.19 = (bf16[512,1024]{1,0:T(8,128)(2,1)}, bf16[512,1024]{1,0:T(8,128)(2,1)}, u32[]{:S(2)}, u32[]{:S(2)}) collective-permute-start(bf16[512,1024]{1,0:T(8,128)(2,1)} %collective-permute-done.18), channel_id=1, source_target_pairs={{0,4},{4,0},{8,12},{12,8},{16,20},{20,16},{24,28},{28,24},{1,5},{5... | collective-permute-start | bytes 3145736 | tf_op jit(solution)/shard_map/ppermute | solution.py:53
  567.1 92.9 %collective-permute-start.35 = (f32[1024,1024]{1,0:T(8,128)}, f32[1024,1024]{1,0:T(8,128)}, u32[]{:S(2)}, u32[]{:S(2)}) collective-permute-start(f32[1024,1024]{1,0:T(8,128)} %fusion.10), channel_id=1, source_target_pairs={{0,2},{1,3},{2,0},{3,1},{4,6},{5,7},{6,4},{7,5},{8,10},{9,11},{10,... | collective-permute-start | bytes 12582920 | tf_op jit(solution)/shard_map/ppermute | solution.py:53
  788.2 66.1 %collective-permute-start.41 = (bf16[1152,1024]{1,0:T(8,128)(2,1)}, bf16[1152,1024]{1,0:T(8,128)(2,1)}, u32[]{:S(2)}, u32[]{:S(2)}) collective-permute-start(bf16[1152,1024]{1,0:T(8,128)(2,1)} %get-tuple-element.60), channel_id=1, source_target_pairs={{0,4},{4,0},{8,12},{12,8},{16,20},{20,16},{24,28},{28,24},{1,5},{5... | collective-permute-start | bytes 7077896 | tf_op jit(solution)/shard_map/ppermute | solution.py:53
  789.4 64.9 %collective-permute-start.43 = (bf16[1152,1024]{1,0:T(8,128)(2,1)}, bf16[1152,1024]{1,0:T(8,128)(2,1)}, u32[]{:S(2)}, u32[]{:S(2)}) collective-permute-start(bf16[1152,1024]{1,0:T(8,128)(2,1)} %get-tuple-element.59), channel_id=1, source_target_pairs={{0,8},{4,12},{8,16},{12,20},{16,24},{20,28},{24,0},{28,4},{1,9},{5... | collective-permute-start | bytes 7077896 | tf_op jit(solution)/shard_map/ppermute | solution.py:58
  853.2 114.5 %collective-permute-start.40 = (bf16[1152,1024]{1,0:T(8,128)(2,1)}, bf16[1152,1024]{1,0:T(8,128)(2,1)}, u32[]{:S(2)}, u32[]{:S(2)}) collective-permute-start(bf16[1152,1024]{1,0:T(8,128)(2,1)} %get-tuple-element.61), channel_id=1, source_target_pairs={{0,4},{4,0},{8,12},{12,8},{16,20},{20,16},{24,28},{28,24},{1,5},{5... | collective-permute-start | bytes 7077896 | tf_op jit(solution)/shard_map/ppermute | solution.py:53
  861.6 107.0 %collective-permute-start.44 = (bf16[1152,1024]{1,0:T(8,128)(2,1)}, bf16[1152,1024]{1,0:T(8,128)(2,1)}, u32[]{:S(2)}, u32[]{:S(2)}) collective-permute-start(bf16[1152,1024]{1,0:T(8,128)(2,1)} %add_convert_fusion.1), channel_id=1, source_target_pairs={{0,8},{4,12},{8,16},{12,20},{16,24},{20,28},{24,0},{28,4},{1,9},{5... | collective-permute-start | bytes 7077896 | tf_op jit(solution)/shard_map/ppermute | solution.py:58
  886.2 76.3 %collective-permute-start.51 = (bf16[512,1024]{1,0:T(8,128)(2,1)}, bf16[512,1024]{1,0:T(8,128)(2,1)}, u32[]{:S(2)}, u32[]{:S(2)}) collective-permute-start(bf16[512,1024]{1,0:T(8,128)(2,1)} %get-tuple-element.64), channel_id=1, source_target_pairs={{0,4},{4,0},{8,12},{12,8},{16,20},{20,16},{24,28},{28,24},{1,5},{5... | collective-permute-start | bytes 3145736 | tf_op jit(solution)/shard_map/ppermute | solution.py:53
  887.3 76.4 %collective-permute-start.53 = (bf16[512,1024]{1,0:T(8,128)(2,1)}, bf16[512,1024]{1,0:T(8,128)(2,1)}, u32[]{:S(2)}, u32[]{:S(2)}) collective-permute-start(bf16[512,1024]{1,0:T(8,128)(2,1)} %get-tuple-element.63), channel_id=1, source_target_pairs={{0,8},{4,12},{8,16},{12,20},{16,24},{20,28},{24,0},{28,4},{1,9},{5... | collective-permute-start | bytes 3145736 | tf_op jit(solution)/shard_map/ppermute | solution.py:58
  994.2 89.3 %collective-permute-start.39 = (bf16[1152,1024]{1,0:T(8,128)(2,1)}, bf16[1152,1024]{1,0:T(8,128)(2,1)}, u32[]{:S(2)}, u32[]{:S(2)}) collective-permute-start(bf16[1152,1024]{1,0:T(8,128)(2,1)} %get-tuple-element.58), channel_id=1, source_target_pairs={{0,4},{4,0},{8,12},{12,8},{16,20},{20,16},{24,28},{28,24},{1,5},{5... | collective-permute-start | bytes 7077896 | tf_op jit(solution)/shard_map/ppermute | solution.py:53
  995.1 88.4 %collective-permute-start.45 = (bf16[1152,1024]{1,0:T(8,128)(2,1)}, bf16[1152,1024]{1,0:T(8,128)(2,1)}, u32[]{:S(2)}, u32[]{:S(2)}) collective-permute-start(bf16[1152,1024]{1,0:T(8,128)(2,1)} %add_convert_fusion), channel_id=1, source_target_pairs={{0,8},{4,12},{8,16},{12,20},{16,24},{20,28},{24,0},{28,4},{1,9},{5... | collective-permute-start | bytes 7077896 | tf_op jit(solution)/shard_map/ppermute | solution.py:58
  999.4 76.1 %collective-permute-start.49 = (bf16[512,1024]{1,0:T(8,128)(2,1)}, bf16[512,1024]{1,0:T(8,128)(2,1)}, u32[]{:S(2)}, u32[]{:S(2)}) collective-permute-start(bf16[512,1024]{1,0:T(8,128)(2,1)} %get-tuple-element.62), channel_id=1, source_target_pairs={{0,4},{4,0},{8,12},{12,8},{16,20},{20,16},{24,28},{28,24},{1,5},{5... | collective-permute-start | bytes 3145736 | tf_op jit(solution)/shard_map/ppermute | solution.py:53
  1000.5 75.0 %collective-permute-start.55 = (bf16[512,1024]{1,0:T(8,128)(2,1)}, bf16[512,1024]{1,0:T(8,128)(2,1)}, u32[]{:S(2)}, u32[]{:S(2)}) collective-permute-start(bf16[512,1024]{1,0:T(8,128)(2,1)} %add_convert_fusion.3), channel_id=1, source_target_pairs={{0,8},{4,12},{8,16},{12,20},{16,24},{20,28},{24,0},{28,4},{1,9},{5... | collective-permute-start | bytes 3145736 | tf_op jit(solution)/shard_map/ppermute | solution.py:58
  1002.1 61.4 %collective-permute-start.63 = (f32[3048]{0:T(1024)S(1)}, f32[3048]{0:T(1024)S(1)}, u32[]{:S(2)}, u32[]{:S(2)}) collective-permute-start(f32[3048]{0:T(1024)S(1)} %pad_maximum_fusion.3), channel_id=1, source_target_pairs={{0,4},{4,0},{8,12},{12,8},{16,20},{20,16},{24,28},{28,24},{1,5},{5... | collective-permute-start | bytes 36584 | tf_op jit(solution)/shard_map/ppermute | solution.py:53
  (85 other events, 2099.7 us)

commit v2 on v0

v2 whole, which is shorter than its diff:
```python
import jax
import jax.numpy as jnp
from jax import lax
from jax.sharding import PartitionSpec as P

STEP = 3


beta_one = 0.5
beta_two = 0.5
learn_rate = 0.01
bias_rate = 0.05
decay_rate = 0.1
adam_eps = 1e-08
clip_norm = 0.05
tiny_eps = 1e-12


def matmul(left, right):
    return jnp.dot(left, right, preferred_element_type=jnp.float32)


def contract_rows(left, right):
    return lax.dot_general(
        left, right, (((0,), (0,)), ((), ())), preferred_element_type=jnp.float32
    )


def against_rows(left, right):
    return lax.dot_general(
        left, right, (((1,), (1,)), ((), ())), preferred_element_type=jnp.float32
    )


def layer_forward(pre_sum, bias_row):
    pre_act = pre_sum + bias_row
    return (pre_act, jax.nn.silu(pre_act).astype(jnp.bfloat16))


def layer_delta(pre_act, upstream):
    sigmoid_val = jax.nn.sigmoid(pre_act)
    slope = sigmoid_val * (1.0 + pre_act * (1.0 - sigmoid_val))
    return (upstream * slope).astype(jnp.bfloat16)


def grad_limits(grad_block, columns):
    squares = jnp.sum(grad_block * grad_block)
    limit = 2.5 * jnp.sqrt(squares / (grad_block.shape[0] * columns))
    return (limit, jnp.minimum(jnp.max(jnp.abs(grad_block)), limit))


def swap(value, axis, bit):
    size = lax.axis_size(axis)
    return lax.ppermute(value, axis, [(i, i ^ bit) for i in range(size)])


def turn(value):
    size = lax.axis_size("dp")
    return lax.ppermute(value, "dp", [(i, (i + 2) % size) for i in range(size)])


def spread_bits(axis):
    bit = 1
    while bit < lax.axis_size(axis):
        yield bit
        bit *= 2


def fold(value, combine, axes):
    for axis in axes:
        for bit in spread_bits(axis):
            value = combine(value, swap(value, axis, bit))
    return value


def settle(*values):
    return lax.optimization_barrier(values)


def owner(step, flip):
    size = lax.axis_size("dp")
    here = lax.axis_index("dp")
    return ((here + size - 2 * step) % size) ^ flip


def place(index, blocks):
    if blocks is None:
        return index
    mine = lax.axis_index("mp")
    return ((index // blocks) ^ mine) * blocks + index % blocks


def put(whole, piece, index, row=0):
    return lax.dynamic_update_slice(whole, piece[None], (index, row, 0))


def take(whole, index, row, rows):
    return lax.dynamic_slice(whole, (index, row, 0), (1, rows, whole.shape[2]))[0]


def xor_blocks(value, bits):
    blocks = {0: value}
    for bit in bits:
        blocks |= {step ^ bit: swap(item, "mp", bit) for step, item in blocks.items()}
    return blocks


def near_rows(rows, rings):
    return max(16, (rows // (2 * rings + 2) + 8) // 16 * 16)


def reorder(whole, group):
    if group is None:
        return whole
    mine = lax.axis_index("mp")
    ways = whole.shape[0] // group
    grouped = whole.reshape(ways, group, *whole.shape[1:])
    return jnp.concatenate(
        [lax.dynamic_index_in_dim(grouped, mine ^ step, 0, keepdims=False) for step in range(ways)]
    )


def overlaps(sizes, row, count):
    start = 0
    for spot, size in enumerate(sizes):
        low, high = max(row, start), min(row + count, start + size)
        if low < high:
            yield spot, low - start, high - low, low - row
        start += size


def soft_ternary(grad_block, limit, peak_val, noise_val):
    clipped = jnp.clip(grad_block, -limit, limit)
    ratio = clipped / (peak_val + tiny_eps)
    value = jnp.clip(4.0 * ratio, -1.0, 1.0) * jnp.clip(
        2.0 * (jnp.abs(ratio) - noise_val.astype(jnp.float32)) + 0.5, 0.0, 1.0
    )
    return value.astype(jnp.bfloat16)


def adam_step(weight, moment, second, grad_val, decay, rate):
    moment_new = beta_one * moment + (1.0 - beta_one) * grad_val
    second_new = beta_two * second + (1.0 - beta_two) * grad_val * grad_val
    first_fix = 1.0 - beta_one**STEP
    second_fix = 1.0 - beta_two**STEP
    weight_new = weight - rate * (
        moment_new / first_fix / (jnp.sqrt(second_new / second_fix) + adam_eps) + decay * weight
    )
    return (weight_new, moment_new, second_new)


LONG_RING = 8


def spans_of(rows, count):
    marks = [rows * i // count // 16 * 16 for i in range(count)] + [rows]
    return list(zip(marks[:-1], marks[1:]))


def same(carried):
    return carried


def gather(shards, groups, near, beside, carried):
    rings = lax.axis_size("dp") // 2
    if rings > LONG_RING:
        wholes = [lax.all_gather(shard, "dp", axis=0) for shard in shards]
        for work in beside:
            carried = work(carried)
        return [reorder(whole, group) for whole, group in zip(wholes, groups)], carried
    beside = beside + [same] * (2 * rings - len(beside))
    sizes = [shard.shape[0] for shard in shards]
    shard = jnp.concatenate(shards) if len(shards) > 1 else shards[0]
    cut = shard.shape[0] - near
    far, pair = shard[:cut], shard[cut:]

    def store(wholes, piece, step, flip, row):
        wholes = list(wholes)
        for spot, inner, count, outer in overlaps(sizes, row, piece.shape[0]):
            index = place(owner(step, flip), groups[spot])
            wholes[spot] = put(wholes[spot], piece[outer : outer + count], index, inner)
        return wholes

    wholes = [jnp.zeros((2 * rings, *item.shape), item.dtype) for item in shards]
    for step in range(rings - 1):
        other = swap(far, "dp", 1)
        if step == 0 and near:
            pair = [pair, swap(pair, "dp", 1)]
        moved = turn(far)
        carried = beside[step](carried)
        if step == 0:
            other, pair, moved, carried, shard = settle(other, pair, moved, carried, shard)
            wholes = store(wholes, shard, 0, 0, 0)
            if near:
                wholes = store(wholes, pair[1], 0, 1, cut)
        else:
            other, pair, moved, carried, wholes = settle(other, pair, moved, carried, wholes)
        wholes = store(wholes, other, step, 1, 0)
        wholes = store(wholes, moved, step + 1, 0, 0)
        far = moved
    pair = jnp.concatenate(pair) if near else None
    for hop, (low, high) in enumerate(spans_of(cut, rings - 1 if near else 1), 1):
        other = swap(far[low:high], "dp", 1)
        pair = turn(pair) if near else None
        carried = beside[rings - 2 + hop](carried)
        other, pair, far, carried, wholes = settle(other, pair, far, carried, wholes)
        wholes = store(wholes, other, rings - 1, 1, low)
        for flip in (0, 1) if near else ():
            wholes = store(wholes, pair[flip * near : (flip + 1) * near], hop, flip, cut)
    return wholes, carried


def scatter(grads, limits, tops, noises, groups, nears, ahead, beside, carried):
    rings = lax.axis_size("dp") // 2
    if rings > LONG_RING:
        for work in beside:
            carried = work(carried)
        results = []
        for grad, limit, top, noise, group in zip(grads, limits, tops, noises, groups):
            tern = soft_ternary(reorder(grad, group), limit, top, noise)
            total = lax.psum_scatter(tern.astype(jnp.float32), "dp", scatter_dimension=0)
            results.append(top * total)
        return results, carried
    beside = beside + [same] * (2 * rings - len(beside))
    spots = range(len(grads))
    cuts = [grad.shape[1] - near for grad, near in zip(grads, nears)]
    hops = rings - 1 if any(nears) else 1
    cutting = [
        spans_of(cut, hops) if near else [(0, cut)] + [None] * (hops - 1)
        for cut, near in zip(cuts, nears)
    ]

    ready = [
        soft_ternary(grad, limit, top, noise) if group is None else None
        for grad, limit, top, noise, group in zip(grads, limits, tops, noises, groups)
    ]

    def tern(spot, step, flip, row, count):
        index = owner(step, flip)
        if ready[spot] is not None:
            return take(ready[spot], index, row, count)
        return soft_ternary(
            take(grads[spot], place(index, groups[spot]), row, count),
            limits[spot],
            tops[spot],
            take(noises[spot], index, row, count),
        )

    def terns(step, flip, spans):
        return [
            None if span is None else tern(spot, step, flip, span[0], span[1] - span[0])
            for spot, span in zip(spots, spans)
        ]

    def far_terns(step, flip):
        return terns(step, flip, [(0, cut) for cut in cuts])

    def near_terns(step):
        return [
            jnp.concatenate([tern(spot, step, flip, cuts[spot], nears[spot]) for flip in (0, 1)])
            if nears[spot]
            else None
            for spot in spots
        ]

    def each(work, *lists):
        return [None if items[0] is None else work(*items) for items in zip(*lists)]

    def wide(value):
        return value.astype(jnp.float32)

    def narrow(value):
        return value.astype(jnp.bfloat16)

    def across(value):
        return swap(value, "dp", 1)

    order = list(range(1, rings)) + [0]
    pairs = near_terns(order[0])
    sending = [terns(order[0], 1, [cut[0] for cut in cutting])]
    pairs, sending, limits, carried, ready = settle(pairs, sending, limits, carried, ready)
    aways, owns = {}, {}
    got = [[] for spot in spots]
    for hop in range(1, hops + 1):
        others = each(across, sending[hop - 1])
        arrived = each(lambda item: turn(narrow(item)), pairs)
        more = near_terns(order[hop])
        if hop < hops:
            sending.append(terns(order[0], 1, [cut[hop] for cut in cutting]))
        if hop == 1:
            owns[0] = far_terns(order[0], 0)
        if hop == hops:
            aways[1] = far_terns(order[1], 1)
        carried = beside[hop - 1](carried)
        others, arrived, more, sending, aways, owns, limits, carried = settle(
            others, arrived, more, sending, aways, owns, limits, carried
        )
        pairs = each(lambda item, add: wide(item) + wide(add), arrived, more)
        for spot in spots:
            if others[spot] is not None:
                got[spot].append(others[spot])
    sums = [wide(owns[0][spot]) + wide(jnp.concatenate(got[spot])) for spot in spots]
    for spin in range(1, rings):
        others = each(across, aways[spin])
        moved = each(lambda item: turn(narrow(item)), sums)
        lasts = None
        if spin == rings - 1:
            lasts = [
                item if item is None else across(narrow(item[near:]))
                for item, near in zip(pairs, nears)
            ]
        for later in range(spin, rings if ahead else spin + 1):
            if later not in owns:
                owns[later] = far_terns(order[later], 0)
        for later in range(spin + 1, rings if ahead else min(spin + 2, rings)):
            if later not in aways:
                aways[later] = far_terns(order[later], 1)
        carried = beside[hops - 1 + spin](carried)
        others, moved, lasts, pairs, aways, owns, limits, carried = settle(
            others, moved, lasts, pairs, aways, owns, limits, carried
        )
        sums = each(
            lambda own, item, more: wide(own) + wide(item) + wide(more), owns[spin], others, moved
        )
    results = []
    for spot, near in zip(spots, nears):
        total = sums[spot]
        if near:
            total = jnp.concatenate([total, pairs[spot][:near] + wide(lasts[spot])])
        results.append(tops[spot] * total)
    return results, carried


def shards(
    features,
    labels,
    noise_six,
    noise_seven,
    noise_eight,
    w_six,
    w_seven,
    w_eight,
    m_six,
    m_seven,
    m_eight,
    v_six,
    v_seven,
    v_eight,
    biases,
    bias_out,
    m_biases,
    v_biases,
    m_bias_out,
    v_bias_out,
):
    mine = lax.axis_index("mp")
    replicas = lax.axis_size("dp")
    ways = lax.axis_size("mp")
    rings = replicas // 2
    batch_rows = features.shape[0]
    tokens = batch_rows * replicas
    half = batch_rows // 2
    width = biases.shape[1]
    outs = bias_out.shape[0]
    padded = outs + -outs % 128
    rows_six, rows_seven, rows_eight = w_six.shape[0], w_seven.shape[0], w_eight.shape[0]
    group_six, group_seven = features.shape[1] // rows_six, width // rows_seven
    near_six = near_rows(rows_six, rings)
    near_seven = near_rows(rows_seven + rows_eight, rings)
    bits = list(reversed(list(spread_bits("mp"))))
    far_bits, near_bit = bits[:-1], bits[-1]

    def widen(value):
        return jnp.pad(value, ((0, 0), (0, padded - outs)))

    def halves(value):
        return [value[:half], value[half:]]

    def over_far(own):
        done = xor_blocks(own, far_bits)
        del done[0]
        return done

    def over_near(blocks):
        return {step ^ near_bit: swap(item, "mp", near_bit) for step, item in blocks.items()}

    def join(halves_of_blocks):
        return jnp.concatenate(
            [
                jnp.concatenate([blocks[step] for step in range(ways)], axis=1)
                for blocks in halves_of_blocks
            ]
        )

    far_features = over_far(features)
    (kept_six,), (inputs, noise_wide) = gather(
        [w_six.astype(jnp.bfloat16)],
        [group_six],
        near_six,
        [
            same,
            lambda carried: swap(features, "mp", near_bit),
            lambda carried: (carried, far_features, widen(noise_eight)),
            lambda carried: carried + (over_near(carried[1]),),
            lambda carried: (
                join([{0: features, near_bit: carried[0]} | carried[1] | carried[3]]),
                carried[2],
            ),
        ],
        None,
    )

    def fc_six(carried):
        inputs, kept = carried
        pre_six, out_six = layer_forward(matmul(inputs, kept.reshape(-1, width)), biases[0])
        return (inputs, pre_six, [{0: item} for item in halves(out_six)])

    def far_half(step):
        def work(carried):
            inputs, pre_six, blocks = carried
            got = [dict(item) for item in blocks]
            got[step] |= over_far(blocks[step][0])
            for item in (0, 1):
                source = {} if item == step else {0: blocks[item][0]}
                if item < step:
                    source = {key: value for key, value in blocks[item].items() if key ^ near_bit not in blocks[item]}
                elif item > step:
                    source = {}
                got[item] |= over_near(source)
            return (inputs, pre_six, got)

        return work

    def near_half(carried):
        inputs, pre_six, blocks = carried
        got = [dict(item) for item in blocks]
        got[1] |= over_near(dict(blocks[1]))
        return (inputs, pre_six, got)

    kept_six, inputs, cast_eight, cast_seven = settle(
        kept_six, inputs, widen(w_eight.astype(jnp.bfloat16)), w_seven.astype(jnp.bfloat16)
    )
    (kept_eight, kept_seven), (inputs, pre_six, hidden_blocks) = gather(
        [cast_eight, cast_seven],
        [None, group_seven],
        near_seven,
        [fc_six, far_half(0), far_half(1), near_half],
        (inputs, kept_six),
    )
    kept_seven, kept_eight = kept_seven.reshape(-1, width), kept_eight.reshape(-1, padded)

    bias_wide = jnp.pad(bias_out, (0, padded - outs), constant_values=-1e30)
    share = half // ways

    def half_forward(number):
        pre, out = layer_forward(matmul(join([hidden_blocks[number]]), kept_seven), biases[1])
        shares = out.reshape(ways, share, width)
        parts = {
            step: matmul(lax.dynamic_index_in_dim(shares, mine ^ step, 0, keepdims=False), kept_eight)
            for step in range(ways)
        }
        for bit in reversed(bits):
            for step in range(0, ways, 2 * bit):
                parts[step] = parts[step] + swap(parts[step + bit], "mp", bit)
        logits = parts[0] + bias_wide
        labels_part = lax.dynamic_slice_in_dim(labels, number * half + mine * share, share, 0)
        top_logit = jnp.max(logits, axis=1, keepdims=True)
        shifted = jnp.exp(logits - top_logit)
        row_total = jnp.sum(shifted, axis=1, keepdims=True)
        log_total = top_logit[:, 0] + jnp.log(row_total[:, 0])
        classes = lax.broadcasted_iota(jnp.int32, logits.shape, 1)
        onehot = (classes == labels_part[:, None]).astype(jnp.float32)
        loss_part = jnp.sum(log_total - jnp.sum(onehot * logits, axis=1)) / tokens
        dz_part = ((shifted / row_total - onehot) / tokens).astype(jnp.bfloat16)
        dlogits = jnp.zeros((ways, share, padded), jnp.bfloat16)
        for step, item in xor_blocks(dz_part, bits).items():
            dlogits = put(dlogits, item, mine ^ step)
        return pre, out, dlogits.reshape(half, padded), loss_part

    both = [half_forward(number) for number in (0, 1)]
    pre_seven, out_seven, dlogits = (
        jnp.concatenate([item[spot] for item in both]) for spot in range(3)
    )
    loss_part = both[0][3] + both[1][3]
    hidden = join(hidden_blocks)

    delta_seven = layer_delta(pre_seven, against_rows(dlogits, kept_eight))

    def upstream(delta, step):
        return against_rows(delta, kept_seven[step * width : (step + 1) * width])

    top_bit = bits[0]
    cuts = [0, batch_rows // 64 * 22, batch_rows // 64 * 43, batch_rows]

    def near_sums(first, delta):
        ups = {step: upstream(delta, step) for step in range(first, first + top_bit)}
        for bit in reversed(bits[1:]):
            for step in range(first, first + top_bit, 2 * bit):
                ups[step] = ups[step] + swap(ups[step + bit], "mp", bit)
        return ups[first]

    crossing = near_sums(top_bit, delta_seven)
    grad_eight = contract_rows(out_seven, dlogits)
    limit_eight, peak_eight = grad_limits(grad_eight, outs)
    crossing, grad_eight, limit_eight, peak_eight, delta_seven, dlogits = settle(
        crossing, grad_eight, limit_eight, peak_eight, delta_seven, dlogits
    )
    crossing = [crossing[low:high] for low, high in zip(cuts[:-1], cuts[1:])]
    grad_seven = contract_rows(hidden, delta_seven)
    limit_seven, peak_seven = grad_limits(grad_seven, width)
    tops = fold(jnp.stack([peak_eight, peak_seven]), jnp.maximum, ("dp",))
    crossing, grad_seven, limit_seven, tops, delta_seven = settle(
        crossing, grad_seven, limit_seven, tops, delta_seven
    )
    top_eight, top_seven = tops[0], tops[1]

    def cross(step):
        def work(carried):
            delta, crossing, crossed, own_up = carried
            if step == 0:
                own_up = near_sums(0, delta)
            return (delta, crossing, crossed + [swap(crossing[step], "mp", top_bit)], own_up)

        return work

    def grad_fc_six(carried):
        _, _, crossed, own_up = carried
        delta_six = layer_delta(pre_six, own_up + jnp.concatenate(crossed))
        grad_six = contract_rows(inputs, delta_six)
        limit_six, peak_six = grad_limits(grad_six, width)
        return (delta_six, grad_six, limit_six, peak_six)

    def sum_or_max(one, two):
        return jnp.concatenate([one[:-1] + two[:-1], jnp.maximum(one[-1:], two[-1:])])

    def small_sums(carried):
        delta_six, grad_six, limit_six, peak_six = carried
        columns = [
            jnp.sum(item.astype(jnp.float32), axis=0) for item in (delta_six, delta_seven, dlogits)
        ]
        small = fold(jnp.concatenate(columns + [peak_six[None]]), sum_or_max, ("dp",))
        return (grad_six, limit_six, small)

    beside = [
        cross(0),
        cross(1),
        cross(2),
        grad_fc_six,
    ]
    (reduced_eight, reduced_seven), carried = scatter(
        [grad_eight.reshape(replicas, rows_eight, padded), grad_seven.reshape(replicas, rows_seven, width)],
        [limit_eight, limit_seven],
        [top_eight, top_seven],
        [noise_wide.reshape(replicas, rows_eight, padded), noise_seven.reshape(replicas, rows_seven, width)],
        [None, group_seven],
        [0, 0],
        False,
        beside,
        (delta_seven, crossing, [], None),
    )
    grad_six, limit_six, small = small_sums(carried)
    top_six = small[-1]
    (reduced_six,), (reduced_seven, reduced_eight) = scatter(
        [grad_six.reshape(replicas, rows_six, width)],
        [limit_six],
        [top_six],
        [noise_six.reshape(replicas, rows_six, width)],
        [group_six],
        [near_six],
        False,
        [same] * rings + [lambda carried: (carried[0], carried[1].T)],
        (reduced_seven, reduced_eight[:, :outs]),
    )
    grad_pair = small[: 2 * width].reshape(2, width)
    grad_out = small[2 * width : 2 * width + outs]
    squares = (
        jnp.sum(reduced_six * reduced_six)
        + jnp.sum(reduced_seven * reduced_seven)
        + jnp.sum(reduced_eight * reduced_eight)
        + jnp.sum(grad_pair * grad_pair) / replicas
        + jnp.sum(grad_out * grad_out) / (replicas * ways)
    )
    totals = fold(jnp.stack([squares, loss_part]), jnp.add, ("dp", "mp"))
    total_squares, loss = totals[0], totals[1]
    grad_norm = jnp.sqrt(total_squares)
    factor = clip_norm / jnp.maximum(grad_norm, clip_norm)
    new_six, new_m_six, new_v_six = adam_step(
        w_six, m_six, v_six, factor * reduced_six, decay_rate, learn_rate
    )
    new_seven, new_m_seven, new_v_seven = adam_step(
        w_seven, m_seven, v_seven, factor * reduced_seven, decay_rate, learn_rate
    )
    new_eight, new_m_eight, new_v_eight = (
        item.T
        for item in adam_step(
            w_eight.T, m_eight.T, v_eight.T, factor * reduced_eight, decay_rate, learn_rate
        )
    )
    new_biases, new_m_biases, new_v_biases = adam_step(
        biases, m_biases, v_biases, factor * grad_pair, 0.0, bias_rate
    )
    new_bias_out, new_m_bias_out, new_v_bias_out = adam_step(
        bias_out, m_bias_out, v_bias_out, factor * grad_out, 0.0, bias_rate
    )
    return (
        loss,
        grad_norm,
        new_six,
        new_seven,
        new_eight,
        new_m_six,
        new_m_seven,
        new_m_eight,
        new_v_six,
        new_v_seven,
        new_v_eight,
        new_six.astype(jnp.bfloat16),
        new_seven.astype(jnp.bfloat16),
        new_eight.astype(jnp.bfloat16),
        new_biases,
        new_bias_out,
        new_m_biases,
        new_v_biases,
        new_m_bias_out,
        new_v_bias_out,
    )


def solution(mesh):
    return jax.shard_map(
        shards,
        mesh=mesh,
        in_specs=(
            P("dp", "mp"),
            P("dp"),
            P("dp", "mp"),
            P("dp", "mp"),
            P(("dp", "mp"), None),
            P("dp", "mp"),
            P("dp", "mp"),
            P(("mp", "dp"), None),
            P("dp", "mp"),
            P("dp", "mp"),
            P(("mp", "dp"), None),
            P("dp", "mp"),
            P("dp", "mp"),
            P(("mp", "dp"), None),
            P(None, "mp"),
            P(),
            P(None, "mp"),
            P(None, "mp"),
            P(),
            P(),
        ),
        out_specs=(
            P(),
            P(),
            P("dp", "mp"),
            P("dp", "mp"),
            P(("mp", "dp"), None),
            P("dp", "mp"),
            P("dp", "mp"),
            P(("mp", "dp"), None),
            P("dp", "mp"),
            P("dp", "mp"),
            P(("mp", "dp"), None),
            P("dp", "mp"),
            P("dp", "mp"),
            P(("mp", "dp"), None),
            P(None, "mp"),
            P(),
            P(None, "mp"),
            P(None, "mp"),
            P(),
            P(),
        ),
        check_vma=False,
    )
```

time: 2150 us -> 900 us (0.42)
  waiting for transfers between devices: 1690 us -> 379 us
  blocking collectives: 96.5 us -> 0 us
  starting transfers between devices: 1.03 us -> 85.5 us
  local copies, waits for them, and re-layouts: 64.5 us -> 108 us
  other arithmetic: 137 us -> 177 us
    reduce_scatter x4 -> x0, waiting for transfers between devices: 928 us -> none  [the longest x1 604 us: shards(): lax.psum_scatter(tern_six.astype(jnp.float32), 'dp', scatter_dimension=0,...]
    all_gather x5 -> x0, waiting for transfers between devices: 678 us -> none  [the longest x1 365 us: shards(): lax.all_gather(cast_six, 'dp', axis=0, tiled=True)]
    ppermute x0 -> x90, waiting for transfers between devices: none -> 379 us  [the longest x66 318 us: swap(): return lax.ppermute(value, axis, [(i, i ^ bit) for i in range(size)])]
    ppermute x0 -> x90, starting transfers between devices: none -> 85.5 us  [the longest x66 64.9 us: swap(): return lax.ppermute(value, axis, [(i, i ^ bit) for i in range(size)])]
    psum x1 -> x0, waiting for transfers between devices: 82 us -> none  [shards(): logits = lax.psum(matmul(out_seven, kept_eight), 'mp') + bias_out]
    psum x2 -> x0, blocking collectives: 74.5 us -> none  [the longest x1 39.6 us: shards(): total_squares = lax.psum(squares, ('dp', 'mp'))]
    convert_element_type x6 -> x33, other arithmetic: 61.2 us -> 114 us  [the longest x18 74.5 us: soft_ternary(): return value.astype(jnp.bfloat16)]
    unnamed x62 -> x129, local copies, waits for them, and re-layouts: 64.5 us -> 13.9 us
  transfers between devices with their start and end apart: 10 -> 90, of which waited for: 9 -> 49; matrix products, arithmetic and copies ran while one was open for 9% -> 33% of each run, Pallas kernels for 0% -> 0%
where the time goes in v2:
time: 900 us; the launch traced here: 889 us
  waiting for transfers between devices  379 us (42%)
  other arithmetic  177 us (20%)
  matrix products  124 us (14%)
  local copies, waits for them, and re-layouts  108 us (12%)
  starting transfers between devices  85.5 us (10%)
  between operations  15.9 us (2%)
    ppermute x66, waiting for transfers between devices, swap(): return lax.ppermute(value, axis, [(i, i ^ bit) for i in range(size)])  318 us
    convert_element_type x18, other arithmetic, soft_ternary(): return value.astype(jnp.bfloat16)  74.5 us
    ppermute x66, starting transfers between devices, swap(): return lax.ppermute(value, axis, [(i, i ^ bit) for i in range(size)])  64.9 us
    ppermute x24, waiting for transfers between devices, turn(): return lax.ppermute(value, 'dp', [(i, (i + 2) % size) for i in range(size)])  61.2 us
    dot_general x3, matrix products, contract_rows(): lax.dot_general(left, right, (((0,), (0,)), ((), ())), preferred_element_...  51.9 us
    dynamic_update_slice x48, local copies, waits for them, and re-layouts, put(): return lax.dynamic_update_slice(whole, piece[None], (index, row, 0))  47.4 us
    dot_general x11, matrix products, matmul(): return jnp.dot(left, right, preferred_element_type=jnp.float32)  46.9 us
    convert_element_type x11, other arithmetic, narrow(): return value.astype(jnp.bfloat16)  31.1 us
  transfers between devices with their start and end apart: 90, of which 49 were waited for; matrix products, arithmetic and copies ran while one was open for 33% of the time, Pallas kernels for 0%

profile of v2, /device:TPU:0, one launch (start us, length us, event | category | flops | bytes accessed | tf_op | source)
XLA Modules:
  0.0 889.4 jit_solution(5756433594818410404)
XLA Ops:
  11.6 48.4 %collective-permute-done.1 = bf16[112,1024]{1,0:T(8,128)(2,1)S(1)} collective-permute-done((bf16[112,1024]{1,0:T(8,128)(2,1)S(1)}, bf16[112,1024]{1,0:T(8,128)(2,1)S(1)}, u32[]{:S(2)}, u32[]{:S(2)}) %collective-permute-start.1) | collective-permute-done | bytes 229408 | tf_op jit(solution)/shard_map/ppermute | solution.py:54
  78.7 29.9 %collective-permute-done.3 = bf16[1040,1024]{1,0:T(8,128)(2,1)S(1)} collective-permute-done((bf16[1040,1024]{1,0:T(8,128)(2,1)}, bf16[1040,1024]{1,0:T(8,128)(2,1)S(1)}, u32[]{:S(2)}, u32[]{:S(2)}) %collective-permute-start.3) | collective-permute-done | bytes 2129952 | tf_op jit(solution)/shard_map/ppermute | solution.py:54
  126.5 32.6 %collective-permute-done.6 = bf16[1040,1024]{1,0:T(8,128)(2,1)} collective-permute-done((bf16[1040,1024]{1,0:T(8,128)(2,1)}, bf16[1040,1024]{1,0:T(8,128)(2,1)}, u32[]{:S(2)}, u32[]{:S(2)}) %collective-permute-start.6) | collective-permute-done | bytes 2129952 | tf_op jit(solution)/shard_map/ppermute | solution.py:54
  172.6 9.8 %collective-permute-done.10 = bf16[224,1024]{1,0:T(8,128)(2,1)S(1)} collective-permute-done((bf16[224,1024]{1,0:T(8,128)(2,1)S(1)}, bf16[224,1024]{1,0:T(8,128)(2,1)S(1)}, u32[]{:S(2)}, u32[]{:S(2)}) %collective-permute-start.10) | collective-permute-done | bytes 458784 | tf_op jit(solution)/shard_map/ppermute | solution.py:59
  184.7 16.2 %pad_maximum_fusion = bf16[1024,9216]{1,0:T(8,128)(2,1)} fusion(bf16[1024,2304]{1,0:T(8,128)(2,1)} %collective-permute-done.11, bf16[1024,2304]{1,0:T(8,128)(2,1)} %collective-permute-done.8, bf16[1024,2304]{1,0:T(8,128)(2,1)} %collective-permute-done.5, bf16[1024,2304]{1,0:T(8,128)(2,1)} %param.20), kind=kLoop, calls=%fused_computation.2 | loop fusion | flops 75497472 | bytes 37748736 | tf_op jit(solution)/shard_map/concatenate | solution.py:390
  207.0 10.5 %collective-permute-done.15 = bf16[224,1024]{1,0:T(8,128)(2,1)S(1)} collective-permute-done((bf16[224,1024]{1,0:T(8,128)(2,1)S(1)}, bf16[224,1024]{1,0:T(8,128)(2,1)S(1)}, u32[]{:S(2)}, u32[]{:S(2)}) %collective-permute-start.15) | collective-permute-done | bytes 458784 | tf_op jit(solution)/shard_map/ppermute | solution.py:59
  225.6 27.2 %fusion.10 = (bf16[1024,1024]{1,0:T(8,128)(2,1)S(1)}, f32[1024,1024]{1,0:T(8,128)}) fusion(f32[1024]{0:T(1024)S(1)} %bitcast.349, bf16[1024,9216]{1,0:T(8,128)(2,1)} %pad_maximum_fusion, bf16[9216,1024]{1,0:T(8,128)(2,1)} %bitcast.17), kind=kOutput, calls=%fused_computation.42 | convolution fusion | flops 19333644288 | bytes 44044288 | tf_op jit(solution)/shard_map/dot_general | solution.py:20
  266.7 11.8 %collective-permute-done.21 = bf16[512,1024]{1,0:T(8,128)(2,1)S(1)} collective-permute-done((bf16[512,1024]{1,0:T(8,128)(2,1)S(1)}, bf16[512,1024]{1,0:T(8,128)(2,1)S(1)}, u32[]{:S(2)}, u32[]{:S(2)}) %collective-permute-start.21) | collective-permute-done | bytes 1048608 | tf_op jit(solution)/shard_map/ppermute | solution.py:54
  293.2 16.7 %collective-permute-done.26 = bf16[512,1024]{1,0:T(8,128)(2,1)} collective-permute-done((bf16[512,1024]{1,0:T(8,128)(2,1)}, bf16[512,1024]{1,0:T(8,128)(2,1)}, u32[]{:S(2)}, u32[]{:S(2)}) %collective-permute-start.26) | collective-permute-done | bytes 1048608 | tf_op jit(solution)/shard_map/ppermute | solution.py:54
  348.8 8.7 multiply_convert_fusion.18
  370.8 11.7 %collective-permute-done.43 = f32[128,1024]{1,0:T(8,128)S(1)} collective-permute-done((f32[128,1024]{1,0:T(8,128)S(1)}, f32[128,1024]{1,0:T(8,128)S(1)}, u32[]{:S(2)}, u32[]{:S(2)}) %collective-permute-start.43) | collective-permute-done | bytes 524320 | tf_op jit(solution)/shard_map/ppermute | solution.py:54
  386.0 7.7 collective-permute-done.37
  433.7 14.5 %abs_reduce_fusion.1 = (f32[]{:T(128)}, f32[]{:T(128)}, f32[4096,1024]{1,0:T(8,128)}) fusion(bf16[1024,1024]{1,0:T(8,128)(2,1)S(1)} %copy-done.20, bf16[512,4096]{1,0:T(8,128)(2,1)S(1)} %copy-done.40, bf16[512,4096]{1,0:T(8,128)(2,1)S(1)} %copy-done.38), kind=kOutput, calls=%fused_computation.3 | convolution fusion | flops 8623489024 | bytes 27262984 | tf_op jit(solution)/shard_map/dot_general | solution.py:24
  490.5 7.2 convolution_add_fusion
  497.7 11.2 %collective-permute-done.52 = bf16[512,1024]{1,0:T(8,128)(2,1)} collective-permute-done((bf16[512,1024]{1,0:T(8,128)(2,1)}, bf16[512,1024]{1,0:T(8,128)(2,1)}, u32[]{:S(2)}, u32[]{:S(2)}) %collective-permute-start.52) | collective-permute-done | bytes 1048608 | tf_op jit(solution)/shard_map/ppermute | solution.py:54
  530.3 14.4 %collective-permute-done.55 = bf16[128,1024]{0,1:T(8,128)(2,1)} collective-permute-done((bf16[128,1024]{0,1:T(8,128)(2,1)}, bf16[128,1024]{0,1:T(8,128)(2,1)}, u32[]{:S(2)}, u32[]{:S(2)}) %collective-permute-start.55) | collective-permute-done | bytes 262176 | tf_op jit(solution)/shard_map/ppermute | solution.py:54
  568.0 10.3 %collective-permute-done.60 = bf16[128,1024]{0,1:T(8,128)(2,1)S(1)} collective-permute-done((bf16[128,1024]{0,1:T(8,128)(2,1)}, bf16[128,1024]{0,1:T(8,128)(2,1)S(1)}, u32[]{:S(2)}, u32[]{:S(2)}) %collective-permute-start.60) | collective-permute-done | bytes 262176 | tf_op jit(solution)/shard_map/ppermute | solution.py:54
  594.8 32.4 %abs_reduce_fusion = (f32[]{:T(128)}, f32[]{:T(128)}, f32[9216,1024]{1,0:T(8,128)}) fusion(bf16[1024,9216]{1,0:T(8,128)(2,1)} %pad_maximum_fusion, bf16[1024,1024]{1,0:T(8,128)(2,1)S(1)} %fusion.9), kind=kOutput, calls=%fused_computation | convolution fusion | flops 19365101568 | bytes 58720264 | tf_op jit(solution)/shard_map/dot_general | solution.py:24
  708.5 7.7 fusion.14
  716.3 30.8 %collective-permute-done.78 = bf16[1040,1024]{1,0:T(8,128)(2,1)} collective-permute-done((bf16[1040,1024]{1,0:T(8,128)(2,1)}, bf16[1040,1024]{1,0:T(8,128)(2,1)}, u32[]{:S(2)}, u32[]{:S(2)}) %collective-permute-start.78) | collective-permute-done | bytes 2129952 | tf_op jit(solution)/shard_map/ppermute | solution.py:54
  755.1 7.4 fusion.16
  762.5 30.9 %collective-permute-done.80 = bf16[1040,1024]{1,0:T(8,128)(2,1)} collective-permute-done((bf16[1040,1024]{1,0:T(8,128)(2,1)}, bf16[1040,1024]{1,0:T(8,128)(2,1)}, u32[]{:S(2)}, u32[]{:S(2)}) %collective-permute-start.80) | collective-permute-done | bytes 2129952 | tf_op jit(solution)/shard_map/ppermute | solution.py:54
  814.1 24.0 %collective-permute-done.84 = bf16[112,1024]{1,0:T(8,128)(2,1)S(1)} collective-permute-done((bf16[112,1024]{1,0:T(8,128)(2,1)}, bf16[112,1024]{1,0:T(8,128)(2,1)S(1)}, u32[]{:S(2)}, u32[]{:S(2)}) %collective-permute-start.84) | collective-permute-done | bytes 229408 | tf_op jit(solution)/shard_map/ppermute | solution.py:54
  867.6 12.8 %fusion.93 = (bf16[1152,1024]{1,0:T(8,128)(2,1)}, f32[1152,1024]{1,0:T(8,128)}, f32[1152,1024]{1,0:T(8,128)}, f32[1152,1024]{1,0:T(8,128)}) fusion(f32[1152,1024]{1,0:T(8,128)} %param.25, f32[112,1024]{1,0:T(8,128)S(1)} %convert_add_fusion.2, f32[1040,1024]{1,0:T(8,128)} %copy-done, f32[]{:T(128)} %bitcast.95, f32[]{:T(128)S(6)} %div.436, ...), kind=kLoop, calls=%fused_computation.277 | loop fusion | flops 21233664 | bytes 35389448 | tf_op jit(solution)/shard_map/convert_element_type | solution.py:617
  (478 shorter events, 438.7 us)
Async XLA Ops:
  0.7 111.2 %collective-permute-start.5 = (bf16[1024,2304]{1,0:T(8,128)(2,1)}, bf16[1024,2304]{1,0:T(8,128)(2,1)}, u32[]{:S(2)}, u32[]{:S(2)}) collective-permute-start(bf16[1024,2304]{1,0:T(8,128)(2,1)} %param.20), channel_id=1, source_target_pairs={{0,1},{1,0},{2,3},{3,2},{4,5},{5,4},{6,7},{7,6},{8,9},{9,8},{10,11... | collective-permute-start | bytes 14155784 | tf_op jit(solution)/shard_map/ppermute | solution.py:54
  5.4 54.6 %collective-permute-start = (bf16[1040,1024]{1,0:T(8,128)(2,1)}, bf16[1040,1024]{1,0:T(8,128)(2,1)}, u32[]{:S(2)}, u32[]{:S(2)}) collective-permute-start(bf16[1040,1024]{1,0:T(8,128)(2,1)} %slice.279), channel_id=1, source_target_pairs={{0,4},{4,0},{8,12},{12,8},{16,20},{20,16},{24,28},{28,24},{1,5},{5... | collective-permute-start | bytes 6389768 | tf_op jit(solution)/shard_map/ppermute | solution.py:54
  7.9 52.1 %collective-permute-start.2 = (bf16[1040,1024]{1,0:T(8,128)(2,1)}, bf16[1040,1024]{1,0:T(8,128)(2,1)}, u32[]{:S(2)}, u32[]{:S(2)}) collective-permute-start(bf16[1040,1024]{1,0:T(8,128)(2,1)} %slice.279), channel_id=1, source_target_pairs={{0,8},{4,12},{8,16},{12,20},{16,24},{20,28},{24,0},{28,4},{1,9},{5... | collective-permute-start | bytes 6389768 | tf_op jit(solution)/shard_map/ppermute | solution.py:59
  9.5 117.0 %collective-permute-start.8 = (bf16[1024,2304]{1,0:T(8,128)(2,1)}, bf16[1024,2304]{1,0:T(8,128)(2,1)}, u32[]{:S(2)}, u32[]{:S(2)}) collective-permute-start(bf16[1024,2304]{1,0:T(8,128)(2,1)} %param.20), channel_id=1, source_target_pairs={{0,2},{1,3},{2,0},{3,1},{4,6},{5,7},{6,4},{7,5},{8,10},{9,11},{10,... | collective-permute-start | bytes 14155784 | tf_op jit(solution)/shard_map/ppermute | solution.py:54
  11.0 49.0 %collective-permute-start.1 = (bf16[112,1024]{1,0:T(8,128)(2,1)S(1)}, bf16[112,1024]{1,0:T(8,128)(2,1)S(1)}, u32[]{:S(2)}, u32[]{:S(2)}) collective-permute-start(bf16[112,1024]{1,0:T(8,128)(2,1)S(1)} %slice.280), channel_id=1, source_target_pairs={{0,4},{4,0},{8,12},{12,8},{16,20},{20,16},{24,28},{28,24},{1,5},{5... | collective-permute-start | bytes 688136 | tf_op jit(solution)/shard_map/ppermute | solution.py:54
  60.0 48.5 %collective-permute-start.3 = (bf16[1040,1024]{1,0:T(8,128)(2,1)}, bf16[1040,1024]{1,0:T(8,128)(2,1)S(1)}, u32[]{:S(2)}, u32[]{:S(2)}) collective-permute-start(bf16[1040,1024]{1,0:T(8,128)(2,1)} %collective-permute-done.2), channel_id=1, source_target_pairs={{0,4},{4,0},{8,12},{12,8},{16,20},{20,16},{24,28},{28,24},{1,5},{5... | collective-permute-start | bytes 6389768 | tf_op jit(solution)/shard_map/ppermute | solution.py:54
  61.9 50.0 %collective-permute-start.4 = (bf16[1040,1024]{1,0:T(8,128)(2,1)}, bf16[1040,1024]{1,0:T(8,128)(2,1)}, u32[]{:S(2)}, u32[]{:S(2)}) collective-permute-start(bf16[1040,1024]{1,0:T(8,128)(2,1)} %collective-permute-done.2), channel_id=1, source_target_pairs={{0,8},{4,12},{8,16},{12,20},{16,24},{20,28},{24,0},{28,4},{1,9},{5... | collective-permute-start | bytes 6389768 | tf_op jit(solution)/shard_map/ppermute | solution.py:59
  111.8 47.3 %collective-permute-start.6 = (bf16[1040,1024]{1,0:T(8,128)(2,1)}, bf16[1040,1024]{1,0:T(8,128)(2,1)}, u32[]{:S(2)}, u32[]{:S(2)}) collective-permute-start(bf16[1040,1024]{1,0:T(8,128)(2,1)} %collective-permute-done.4), channel_id=1, source_target_pairs={{0,4},{4,0},{8,12},{12,8},{16,20},{20,16},{24,28},{28,24},{1,5},{5... | collective-permute-start | bytes 6389768 | tf_op jit(solution)/shard_map/ppermute | solution.py:54
  112.3 48.9 %collective-permute-start.7 = (bf16[1040,1024]{1,0:T(8,128)(2,1)}, bf16[1040,1024]{1,0:T(8,128)(2,1)S(1)}, u32[]{:S(2)}, u32[]{:S(2)}) collective-permute-start(bf16[1040,1024]{1,0:T(8,128)(2,1)} %collective-permute-done.4), channel_id=1, source_target_pairs={{0,8},{4,12},{8,16},{12,20},{16,24},{20,28},{24,0},{28,4},{1,9},{5... | collective-permute-start | bytes 6389768 | tf_op jit(solution)/shard_map/ppermute | solution.py:59
  479.5 33.8 %collective-permute-start.53 = (f32[352,1024]{1,0:T(8,128)}, f32[352,1024]{1,0:T(8,128)}, u32[]{:S(2)}, u32[]{:S(2)}) collective-permute-start(f32[352,1024]{1,0:T(8,128)} %slice.257), channel_id=1, source_target_pairs={{0,2},{1,3},{2,0},{3,1},{4,6},{5,7},{6,4},{7,5},{8,10},{9,11},{10,... | collective-permute-start | bytes 4325384 | tf_op jit(solution)/shard_map/ppermute | solution.py:54
  513.2 35.6 %collective-permute-start.59 = (f32[336,1024]{1,0:T(8,128)}, f32[336,1024]{1,0:T(8,128)S(1)}, u32[]{:S(2)}, u32[]{:S(2)}) collective-permute-start(f32[336,1024]{1,0:T(8,128)} %get-tuple-element.405), channel_id=1, source_target_pairs={{0,2},{1,3},{2,0},{3,1},{4,6},{5,7},{6,4},{7,5},{8,10},{9,11},{10,... | collective-permute-start | bytes 4128776 | tf_op jit(solution)/shard_map/ppermute | solution.py:54
  514.9 33.9 %collective-permute-start.56 = (bf16[512,1024]{1,0:T(8,128)(2,1)}, bf16[512,1024]{1,0:T(8,128)(2,1)}, u32[]{:S(2)}, u32[]{:S(2)}) collective-permute-start(bf16[512,1024]{1,0:T(8,128)(2,1)} %get-tuple-element.399), channel_id=1, source_target_pairs={{0,4},{4,0},{8,12},{12,8},{16,20},{20,16},{24,28},{28,24},{1,5},{5... | collective-permute-start | bytes 3145736 | tf_op jit(solution)/shard_map/ppermute | solution.py:54
  549.8 34.3 %collective-permute-start.61 = (bf16[512,1024]{1,0:T(8,128)(2,1)}, bf16[512,1024]{1,0:T(8,128)(2,1)}, u32[]{:S(2)}, u32[]{:S(2)}) collective-permute-start(bf16[512,1024]{1,0:T(8,128)(2,1)} %get-tuple-element.410), channel_id=1, source_target_pairs={{0,4},{4,0},{8,12},{12,8},{16,20},{20,16},{24,28},{28,24},{1,5},{5... | collective-permute-start | bytes 3145736 | tf_op jit(solution)/shard_map/ppermute | solution.py:54
  550.7 33.4 %collective-permute-start.64 = (f32[336,1024]{1,0:T(8,128)}, f32[336,1024]{1,0:T(8,128)S(1)}, u32[]{:S(2)}, u32[]{:S(2)}) collective-permute-start(f32[336,1024]{1,0:T(8,128)} %get-tuple-element.418), channel_id=1, source_target_pairs={{0,2},{1,3},{2,0},{3,1},{4,6},{5,7},{6,4},{7,5},{8,10},{9,11},{10,... | collective-permute-start | bytes 4128776 | tf_op jit(solution)/shard_map/ppermute | solution.py:54
  584.1 47.4 %collective-permute-start.65 = (bf16[128,1024]{0,1:T(8,128)(2,1)}, bf16[128,1024]{0,1:T(8,128)(2,1)}, u32[]{:S(2)}, u32[]{:S(2)}) collective-permute-start(bf16[128,1024]{0,1:T(8,128)(2,1)} %bitcast.88), channel_id=1, source_target_pairs={{0,4},{4,0},{8,12},{12,8},{16,20},{20,16},{24,28},{28,24},{1,5},{5... | collective-permute-start | bytes 786440 | tf_op jit(solution)/shard_map/ppermute | solution.py:54
  585.2 46.3 %collective-permute-start.66 = (bf16[512,1024]{1,0:T(8,128)(2,1)}, bf16[512,1024]{1,0:T(8,128)(2,1)}, u32[]{:S(2)}, u32[]{:S(2)}) collective-permute-start(bf16[512,1024]{1,0:T(8,128)(2,1)} %get-tuple-element.423), channel_id=1, source_target_pairs={{0,4},{4,0},{8,12},{12,8},{16,20},{20,16},{24,28},{28,24},{1,5},{5... | collective-permute-start | bytes 3145736 | tf_op jit(solution)/shard_map/ppermute | solution.py:54
  587.9 43.6 %collective-permute-start.67 = (bf16[128,1024]{0,1:T(8,128)(2,1)}, bf16[128,1024]{0,1:T(8,128)(2,1)}, u32[]{:S(2)}, u32[]{:S(2)}) collective-permute-start(bf16[128,1024]{0,1:T(8,128)(2,1)} %add_convert_fusion.8), channel_id=1, source_target_pairs={{0,8},{4,12},{8,16},{12,20},{16,24},{20,28},{24,0},{28,4},{1,9},{5... | collective-permute-start | bytes 786440 | tf_op jit(solution)/shard_map/ppermute | solution.py:59
  591.1 40.5 %collective-permute-start.68 = (bf16[512,1024]{1,0:T(8,128)(2,1)}, bf16[512,1024]{1,0:T(8,128)(2,1)}, u32[]{:S(2)}, u32[]{:S(2)}) collective-permute-start(bf16[512,1024]{1,0:T(8,128)(2,1)} %add_convert_fusion.3), channel_id=1, source_target_pairs={{0,8},{4,12},{8,16},{12,20},{16,24},{20,28},{24,0},{28,4},{1,9},{5... | collective-permute-start | bytes 3145736 | tf_op jit(solution)/shard_map/ppermute | solution.py:59
  700.5 46.5 %collective-permute-start.78 = (bf16[1040,1024]{1,0:T(8,128)(2,1)}, bf16[1040,1024]{1,0:T(8,128)(2,1)}, u32[]{:S(2)}, u32[]{:S(2)}) collective-permute-start(bf16[1040,1024]{1,0:T(8,128)(2,1)} %fusion.12), channel_id=1, source_target_pairs={{0,4},{4,0},{8,12},{12,8},{16,20},{20,16},{24,28},{28,24},{1,5},{5... | collective-permute-start | bytes 6389768 | tf_op jit(solution)/shard_map/ppermute | solution.py:54
  705.4 41.6 %collective-permute-start.79 = (bf16[1040,1024]{1,0:T(8,128)(2,1)}, bf16[1040,1024]{1,0:T(8,128)(2,1)}, u32[]{:S(2)}, u32[]{:S(2)}) collective-permute-start(bf16[1040,1024]{1,0:T(8,128)(2,1)} %add_convert_fusion.2), channel_id=1, source_target_pairs={{0,8},{4,12},{8,16},{12,20},{16,24},{20,28},{24,0},{28,4},{1,9},{5... | collective-permute-start | bytes 6389768 | tf_op jit(solution)/shard_map/ppermute | solution.py:59
  747.0 46.4 %collective-permute-start.80 = (bf16[1040,1024]{1,0:T(8,128)(2,1)}, bf16[1040,1024]{1,0:T(8,128)(2,1)}, u32[]{:S(2)}, u32[]{:S(2)}) collective-permute-start(bf16[1040,1024]{1,0:T(8,128)(2,1)} %get-tuple-element.477), channel_id=1, source_target_pairs={{0,4},{4,0},{8,12},{12,8},{16,20},{20,16},{24,28},{28,24},{1,5},{5... | collective-permute-start | bytes 6389768 | tf_op jit(solution)/shard_map/ppermute | solution.py:54
  753.3 40.1 %collective-permute-start.81 = (bf16[1040,1024]{1,0:T(8,128)(2,1)}, bf16[1040,1024]{1,0:T(8,128)(2,1)}, u32[]{:S(2)}, u32[]{:S(2)}) collective-permute-start(bf16[1040,1024]{1,0:T(8,128)(2,1)} %add_convert_fusion.1), channel_id=1, source_target_pairs={{0,8},{4,12},{8,16},{12,20},{16,24},{20,28},{24,0},{28,4},{1,9},{5... | collective-permute-start | bytes 6389768 | tf_op jit(solution)/shard_map/ppermute | solution.py:59
  793.5 44.7 %collective-permute-start.82 = (bf16[1040,1024]{1,0:T(8,128)(2,1)}, bf16[1040,1024]{1,0:T(8,128)(2,1)}, u32[]{:S(2)}, u32[]{:S(2)}) collective-permute-start(bf16[1040,1024]{1,0:T(8,128)(2,1)} %get-tuple-element.485), channel_id=1, source_target_pairs={{0,4},{4,0},{8,12},{12,8},{16,20},{20,16},{24,28},{28,24},{1,5},{5... | collective-permute-start | bytes 6389768 | tf_op jit(solution)/shard_map/ppermute | solution.py:54
  799.8 38.3 %collective-permute-start.83 = (bf16[1040,1024]{1,0:T(8,128)(2,1)}, bf16[1040,1024]{1,0:T(8,128)(2,1)}, u32[]{:S(2)}, u32[]{:S(2)}) collective-permute-start(bf16[1040,1024]{1,0:T(8,128)(2,1)} %add_convert_fusion), channel_id=1, source_target_pairs={{0,8},{4,12},{8,16},{12,20},{16,24},{20,28},{24,0},{28,4},{1,9},{5... | collective-permute-start | bytes 6389768 | tf_op jit(solution)/shard_map/ppermute | solution.py:59
  (127 other events, 1738.4 us)

commit v3 on v2

--- a/solution.py
+++ b/solution.py
@@ -161,53 +161,88 @@
     return carried
 
 
-def gather(shards, groups, near, beside, carried):
+def gather_whole(shard, group):
+    return reorder(lax.all_gather(shard, "dp", axis=0), group)
+
+
+def gather_queue(first, second, groups, near, hooks, carried):
     rings = lax.axis_size("dp") // 2
-    if rings > LONG_RING:
-        wholes = [lax.all_gather(shard, "dp", axis=0) for shard in shards]
-        for work in beside:
-            carried = work(carried)
-        return [reorder(whole, group) for whole, group in zip(wholes, groups)], carried
-    beside = beside + [same] * (2 * rings - len(beside))
-    sizes = [shard.shape[0] for shard in shards]
-    shard = jnp.concatenate(shards) if len(shards) > 1 else shards[0]
-    cut = shard.shape[0] - near
-    far, pair = shard[:cut], shard[cut:]
+    rows = first.shape[0]
+    middle = rows // 32 * 16
+    sizes = [shard.shape[0] for shard in second]
+    joined = jnp.concatenate(second)
+    cut = joined.shape[0] - near
+    ready = {
+        ("a", 0): first[:middle],
+        ("b", 0): first[middle:],
+        ("f", 0): joined[:cut],
+        ("n",): joined[cut:],
+    }
+    z_tasks = [(name, hop) for hop in range(rings - 1) for name in "ab"]
+    z_tasks += [(name, hop) for hop in range(rings - 1) for name in "fp"]
+    y_tasks = [(name, hop) for hop in range(rings) for name in "ab"]
+    y_tasks += [("f", hop) for hop in range(rings)]
 
     def store(wholes, piece, step, flip, row):
         wholes = list(wholes)
         for spot, inner, count, outer in overlaps(sizes, row, piece.shape[0]):
-            index = place(owner(step, flip), groups[spot])
-            wholes[spot] = put(wholes[spot], piece[outer : outer + count], index, inner)
+            index = place(owner(step, flip), groups[1][spot])
+            wholes[1 + spot] = put(wholes[1 + spot], piece[outer : outer + count], index, inner)
         return wholes
 
-    wholes = [jnp.zeros((2 * rings, *item.shape), item.dtype) for item in shards]
-    for step in range(rings - 1):
-        other = swap(far, "dp", 1)
-        if step == 0 and near:
-            pair = [pair, swap(pair, "dp", 1)]
-        moved = turn(far)
-        carried = beside[step](carried)
-        if step == 0:
-            other, pair, moved, carried, shard = settle(other, pair, moved, carried, shard)
-            wholes = store(wholes, shard, 0, 0, 0)
-            if near:
-                wholes = store(wholes, pair[1], 0, 1, cut)
-        else:
-            other, pair, moved, carried, wholes = settle(other, pair, moved, carried, wholes)
-        wholes = store(wholes, other, step, 1, 0)
-        wholes = store(wholes, moved, step + 1, 0, 0)
-        far = moved
-    pair = jnp.concatenate(pair) if near else None
-    for hop, (low, high) in enumerate(spans_of(cut, rings - 1 if near else 1), 1):
-        other = swap(far[low:high], "dp", 1)
-        pair = turn(pair) if near else None
-        carried = beside[rings - 2 + hop](carried)
-        other, pair, far, carried, wholes = settle(other, pair, far, carried, wholes)
-        wholes = store(wholes, other, rings - 1, 1, low)
-        for flip in (0, 1) if near else ():
-            wholes = store(wholes, pair[flip * near : (flip + 1) * near], hop, flip, cut)
-    return wholes, carried
+    def store_first(wholes, piece, step, flip, row):
+        index = place(owner(step, flip), groups[0])
+        return [put(wholes[0], piece, index, row)] + list(wholes[1:])
+
+    wholes = None
+    flight, pending, last = {}, None, {}
+    step = 0
+    while z_tasks or y_tasks or flight:
+        started = {}
+        if z_tasks and z_tasks[0] in ready:
+            name, hop = z_tasks.pop(0)
+            started["z", name, hop + 1] = turn(ready[name, hop])
+        if y_tasks and y_tasks[0] in ready:
+            name, hop = y_tasks.pop(0)
+            started["y", name, hop] = swap(ready[name, hop], "dp", 1)
+            if (name, hop) == ("b", rings - 2):
+                started["y", "n", 0] = swap(ready["n",], "dp", 1)
+        if step == 1:
+            wholes = [jnp.zeros((2 * rings, *item.shape), item.dtype) for item in (first, *second)]
+            wholes = store_first(wholes, ready["a", 0], 0, 0, 0)
+            wholes = store_first(wholes, ready["b", 0], 0, 0, middle)
+        if step == 2:
+            wholes = store(wholes, ready["f", 0], 0, 0, 0)
+            wholes = store(wholes, ready["n",], 0, 0, cut)
+        later = None
+        if step in hooks:
+            carried, later = hooks[step](carried, wholes, last)
+        flight, ready, wholes, carried, pending, last = settle(
+            flight, ready, wholes, carried, pending, last
+        )
+        if pending is not None:
+            carried = carried | pending
+        pending = later
+        for (axis, name, hop), piece in flight.items():
+            if name in "ab":
+                row = 0 if name == "a" else middle
+                if axis == "y" and hop == rings - 1:
+                    last[name] = piece
+                else:
+                    wholes = store_first(wholes, piece, hop, int(axis == "y"), row)
+            elif name == "f":
+                wholes = store(wholes, piece, hop, int(axis == "y"), 0)
+            elif name == "n":
+                wholes = store(wholes, piece, 0, 1, cut)
+                ready["p", 0] = jnp.concatenate([ready["n",], piece])
+            else:
+                for flip in (0, 1):
+                    wholes = store(wholes, piece[flip * near : (flip + 1) * near], hop, flip, cut)
+            if axis == "z":
+                ready[name, hop] = piece
+        flight = started
+        step += 1
+    return wholes, carried | (pending or {})
 
 
 def scatter(grads, limits, tops, noises, groups, nears, ahead, beside, carried):
@@ -366,7 +401,6 @@
     rows_six, rows_seven, rows_eight = w_six.shape[0], w_seven.shape[0], w_eight.shape[0]
     group_six, group_seven = features.shape[1] // rows_six, width // rows_seven
     near_six = near_rows(rows_six, rings)
-    near_seven = near_rows(rows_seven + rows_eight, rings)
     bits = list(reversed(list(spread_bits("mp"))))
     far_bits, near_bit = bits[:-1], bits[-1]
 
@@ -393,60 +427,92 @@
         )
 
     far_features = over_far(features)
-    (kept_six,), (inputs, noise_wide) = gather(
-        [w_six.astype(jnp.bfloat16)],
-        [group_six],
-        near_six,
-        [
-            same,
-            lambda carried: swap(features, "mp", near_bit),
-            lambda carried: (carried, far_features, widen(noise_eight)),
-            lambda carried: carried + (over_near(carried[1]),),
-            lambda carried: (
-                join([{0: features, near_bit: carried[0]} | carried[1] | carried[3]]),
-                carried[2],
-            ),
-        ],
-        None,
-    )
-
-    def fc_six(carried):
-        inputs, kept = carried
-        pre_six, out_six = layer_forward(matmul(inputs, kept.reshape(-1, width)), biases[0])
-        return (inputs, pre_six, [{0: item} for item in halves(out_six)])
-
-    def far_half(step):
-        def work(carried):
-            inputs, pre_six, blocks = carried
-            got = [dict(item) for item in blocks]
-            got[step] |= over_far(blocks[step][0])
-            for item in (0, 1):
-                source = {} if item == step else {0: blocks[item][0]}
-                if item < step:
-                    source = {key: value for key, value in blocks[item].items() if key ^ near_bit not in blocks[item]}
-                elif item > step:
-                    source = {}
-                got[item] |= over_near(source)
-            return (inputs, pre_six, got)
-
-        return work
-
-    def near_half(carried):
-        inputs, pre_six, blocks = carried
-        got = [dict(item) for item in blocks]
-        got[1] |= over_near(dict(blocks[1]))
-        return (inputs, pre_six, got)
-
-    kept_six, inputs, cast_eight, cast_seven = settle(
-        kept_six, inputs, widen(w_eight.astype(jnp.bfloat16)), w_seven.astype(jnp.bfloat16)
-    )
-    (kept_eight, kept_seven), (inputs, pre_six, hidden_blocks) = gather(
-        [cast_eight, cast_seven],
-        [None, group_seven],
-        near_seven,
-        [fc_six, far_half(0), far_half(1), near_half],
-        (inputs, kept_six),
-    )
+    shards_cast = [
+        w_six.astype(jnp.bfloat16),
+        widen(w_eight.astype(jnp.bfloat16)),
+        w_seven.astype(jnp.bfloat16),
+    ]
+    if rings > LONG_RING:
+        inputs = join([{0: features} | far_features | over_near({0: features} | far_features)])
+        noise_wide = widen(noise_eight)
+        kept_six = gather_whole(shards_cast[0], group_six).reshape(-1, width)
+        kept_eight = gather_whole(shards_cast[1], None)
+        kept_seven = gather_whole(shards_cast[2], group_seven)
+        pre_six, out_six = layer_forward(matmul(inputs, kept_six), biases[0])
+        hidden_blocks = []
+        for item in halves(out_six):
+            blocks = {0: item} | over_far(item)
+            hidden_blocks.append(blocks | over_near(blocks))
+    else:
+        count = 2 * rings
+
+        def own_near(carried, wholes, last):
+            return {"near": swap(features, "mp", near_bit), "noise": widen(noise_eight)}, None
+
+        def far_there(carried, wholes, last):
+            return carried | {"far": far_features}, None
+
+        def far_near(carried, wholes, last):
+            return carried | {"both": over_near(carried["far"])}, None
+
+        def join_inputs(carried, wholes, last):
+            blocks = {0: features, near_bit: carried["near"]} | carried["far"] | carried["both"]
+            return {"inputs": join([blocks]), "noise": carried["noise"]}, None
+
+        def fc_six_most(carried, wholes, last):
+            early = matmul(carried["inputs"], wholes[0].reshape(-1, width))
+            return carried, {"early": early}
+
+        def fc_six_rest(carried, wholes, last):
+            start = place(owner(rings - 1, 1), group_six) * rows_six
+            columns = lax.dynamic_slice_in_dim(carried["inputs"], start, rows_six, 1)
+            rest = matmul(columns, jnp.concatenate([last["a"], last["b"]]))
+            pre_six, out_six = layer_forward(carried["early"] + rest, biases[0])
+            one, two = halves(out_six)
+            crossing["one"], crossing["two"] = over_far(one), over_far(two)
+            return (
+                {"inputs": carried["inputs"], "noise": carried["noise"], "pre": pre_six, "out": (one, two)},
+                None,
+            )
+
+        crossing = {}
+
+        def hidden_own(carried, wholes, last):
+            own = [over_near({0: item}) for item in carried["out"]]
+            return carried | {"own": own}, None
+
+        def hidden_one(carried, wholes, last):
+            return carried | {"one": crossing["one"]}, None
+
+        def hidden_one_near(carried, wholes, last):
+            return carried | {"one_near": over_near(carried["one"])}, None
+
+        hooks = {
+            1: own_near,
+            count - 4: far_there,
+            count - 3: far_near,
+            count - 2: join_inputs,
+            count - 1: fc_six_most,
+            count + 1: fc_six_rest,
+            count + 2: hidden_own,
+            count + 3: hidden_one,
+            count + 4: hidden_one_near,
+        }
+        near = (rows_six + rows_seven + rows_eight) // (2 * rings - 2) // 16 * 16
+        (_, kept_eight, kept_seven), carried = gather_queue(
+            shards_cast[0],
+            shards_cast[1:],
+            [group_six, [None, group_seven]],
+            min(near, rows_seven // 32 * 16),
+            hooks,
+            {},
+        )
+        inputs, noise_wide, pre_six = carried["inputs"], carried["noise"], carried["pre"]
+        one, two = carried["out"]
+        hidden_blocks = [
+            {0: one} | carried["own"][0] | carried["one"] | carried["one_near"],
+            {0: two} | carried["own"][1] | crossing["two"] | over_near(crossing["two"]),
+        ]
     kept_seven, kept_eight = kept_seven.reshape(-1, width), kept_eight.reshape(-1, padded)
 
     bias_wide = jnp.pad(bias_out, (0, padded - outs), constant_values=-1e30)

time: 900 us -> 882 us (0.980)
  waiting for transfers between devices: 379 us -> 358 us
    ppermute x66 -> x65, waiting for transfers between devices: 318 us -> 304 us  [swap(): return lax.ppermute(value, axis, [(i, i ^ bit) for i in range(size)])]
    ppermute x66 -> x65, starting transfers between devices: 64.9 us -> 52.3 us  [swap(): return lax.ppermute(value, axis, [(i, i ^ bit) for i in range(size)])]
    dynamic_update_slice x48 -> x44, local copies, waits for them, and re-layouts: 47.4 us -> 56 us  [put(): return lax.dynamic_update_slice(whole, piece[None], (index, row, 0))]
    dot_general x11 -> x12, matrix products: 46.9 us -> 50.2 us  [matmul(): return jnp.dot(left, right, preferred_element_type=jnp.float32)]
  transfers between devices with their start and end apart: 90 -> 89, of which waited for: 49 -> 48; matrix products, arithmetic and copies ran while one was open for 33% -> 37% of each run, Pallas kernels for 0% -> 0%
where the time goes in v3:
time: 882 us; the launch traced here: 866 us
  waiting for transfers between devices  358 us (41%)
  other arithmetic  171 us (19%)
  matrix products  127 us (14%)
  local copies, waits for them, and re-layouts  114 us (13%)
  starting transfers between devices  80.5 us (9%)
  between operations  15.9 us (2%)
    ppermute x65, waiting for transfers between devices, swap(): return lax.ppermute(value, axis, [(i, i ^ bit) for i in range(size)])  304 us
    convert_element_type x18, other arithmetic, soft_ternary(): return value.astype(jnp.bfloat16)  72.5 us
    dynamic_update_slice x44, local copies, waits for them, and re-layouts, put(): return lax.dynamic_update_slice(whole, piece[None], (index, row, 0))  56 us
    ppermute x24, waiting for transfers between devices, turn(): return lax.ppermute(value, 'dp', [(i, (i + 2) % size) for i in range(size)])  53.6 us
    ppermute x65, starting transfers between devices, swap(): return lax.ppermute(value, axis, [(i, i ^ bit) for i in range(size)])  52.3 us
    dot_general x3, matrix products, contract_rows(): lax.dot_general(left, right, (((0,), (0,)), ((), ())), preferred_element_...  51.6 us
    dot_general x12, matrix products, matmul(): return jnp.dot(left, right, preferred_element_type=jnp.float32)  50.2 us
    convert_element_type x11, other arithmetic, narrow(): return value.astype(jnp.bfloat16)  30.2 us
  transfers between devices with their start and end apart: 89, of which 48 were waited for; matrix products, arithmetic and copies ran while one was open for 37% of the time, Pallas kernels for 0%

profile of v3, /device:TPU:0, one launch (start us, length us, event | category | flops | bytes accessed | tf_op | source)
XLA Modules:
  0.0 865.9 jit_solution(3106642301282991042)
XLA Ops:
  28.2 8.6 collective-permute-done
  74.0 13.4 %collective-permute-done.3 = bf16[576,1024]{1,0:T(8,128)(2,1)} collective-permute-done((bf16[576,1024]{1,0:T(8,128)(2,1)}, bf16[576,1024]{1,0:T(8,128)(2,1)}, u32[]{:S(2)}, u32[]{:S(2)}) %collective-permute-start.3) | collective-permute-done | bytes 1179680 | tf_op jit(solution)/shard_map/ppermute | solution.py:54
  97.7 8.8 %collective-permute-done.11 = bf16[1024,2304]{1,0:T(8,128)(2,1)} collective-permute-done((bf16[1024,2304]{1,0:T(8,128)(2,1)}, bf16[1024,2304]{1,0:T(8,128)(2,1)}, u32[]{:S(2)}, u32[]{:S(2)}) %collective-permute-start.11) | collective-permute-done | bytes 4718624 | tf_op jit(solution)/shard_map/ppermute | solution.py:54
  124.0 20.9 %collective-permute-done.7 = bf16[576,1024]{1,0:T(8,128)(2,1)} collective-permute-done((bf16[576,1024]{1,0:T(8,128)(2,1)}, bf16[576,1024]{1,0:T(8,128)(2,1)}, u32[]{:S(2)}, u32[]{:S(2)}) %collective-permute-start.7) | collective-permute-done | bytes 1179680 | tf_op jit(solution)/shard_map/ppermute | solution.py:54
  148.7 9.7 %pad_maximum_fusion = bf16[1024,9216]{1,0:T(8,128)(2,1)S(1)} fusion(bf16[1024,2304]{1,0:T(8,128)(2,1)} %collective-permute-done.12, bf16[1024,2304]{1,0:T(8,128)(2,1)} %collective-permute-done.11, bf16[1024,2304]{1,0:T(8,128)(2,1)} %collective-permute-done.2, bf16[1024,2304]{1,0:T(8,128)(2,1)} %param.20), kind=kLoop, calls=%fused_computation.2 | loop fusion | flops 75497472 | bytes 37748736 | tf_op jit(solution)/shard_map/concatenate | solution.py:424
  165.6 15.6 %collective-permute-done.16 = bf16[256,1024]{1,0:T(8,128)(2,1)S(1)} collective-permute-done((bf16[256,1024]{1,0:T(8,128)(2,1)S(1)}, bf16[256,1024]{1,0:T(8,128)(2,1)S(1)}, u32[]{:S(2)}, u32[]{:S(2)}) %collective-permute-start.16) | collective-permute-done | bytes 524320 | tf_op jit(solution)/shard_map/ppermute | solution.py:54
  186.8 23.0 %fusion.109 = f32[1024,1024]{1,0:T(8,128)S(1)} fusion(bf16[1024,9216]{1,0:T(8,128)(2,1)S(1)} %pad_maximum_fusion, bf16[9216,1024]{1,0:T(8,128)(2,1)} %bitcast.20), kind=kOutput, calls=%fused_computation.285 | convolution fusion | flops 19327352832 | bytes 41943040 | tf_op jit(solution)/shard_map/dot_general | solution.py:20
  213.3 18.6 %collective-permute-done.20 = bf16[576,1024]{1,0:T(8,128)(2,1)} collective-permute-done((bf16[576,1024]{1,0:T(8,128)(2,1)S(1)}, bf16[576,1024]{1,0:T(8,128)(2,1)}, u32[]{:S(2)}, u32[]{:S(2)}) %collective-permute-start.20) | collective-permute-done | bytes 1179680 | tf_op jit(solution)/shard_map/ppermute | solution.py:54
  258.2 12.0 %collective-permute-done.24 = bf16[384,1024]{1,0:T(8,128)(2,1)S(1)} collective-permute-done((bf16[384,1024]{1,0:T(8,128)(2,1)}, bf16[384,1024]{1,0:T(8,128)(2,1)S(1)}, u32[]{:S(2)}, u32[]{:S(2)}) %collective-permute-start.24) | collective-permute-done | bytes 786464 | tf_op jit(solution)/shard_map/ppermute | solution.py:54
  279.7 9.7 %collective-permute-done.22 = bf16[384,1024]{1,0:T(8,128)(2,1)S(1)} collective-permute-done((bf16[384,1024]{1,0:T(8,128)(2,1)}, bf16[384,1024]{1,0:T(8,128)(2,1)S(1)}, u32[]{:S(2)}, u32[]{:S(2)}) %collective-permute-start.22) | collective-permute-done | bytes 786464 | tf_op jit(solution)/shard_map/ppermute | solution.py:54
  301.8 13.4 %collective-permute-done.30 = bf16[512,1024]{1,0:T(8,128)(2,1)S(1)} collective-permute-done((bf16[512,1024]{1,0:T(8,128)(2,1)}, bf16[512,1024]{1,0:T(8,128)(2,1)S(1)}, u32[]{:S(2)}, u32[]{:S(2)}) %collective-permute-start.30) | collective-permute-done | bytes 1048608 | tf_op jit(solution)/shard_map/ppermute | solution.py:59
  324.7 8.6 multiply_convert_fusion.19
  333.4 8.7 %multiply_convert_fusion.18 = (bf16[512,1024]{1,0:T(8,128)(2,1)S(1)}, f32[512,1024]{1,0:T(8,128)S(1)}) fusion(f32[1024]{0:T(1024)S(1)} %bitcast.341, bf16[512,4096]{1,0:T(8,128)(2,1)S(1)} %constant_dynamic-update-slice_fusion.6, bf16[4096,1024]{1,0:T(8,128)(2,1)} %bitcast.39), kind=kOutput, calls=%fused_computation.73 | convolution fusion | flops 4298113024 | bytes 15732736 | tf_op jit(solution)/shard_map/dot_general | solution.py:20
  348.2 11.7 %collective-permute-done.42 = f32[128,1024]{1,0:T(8,128)S(1)} collective-permute-done((f32[128,1024]{1,0:T(8,128)S(1)}, f32[128,1024]{1,0:T(8,128)S(1)}, u32[]{:S(2)}, u32[]{:S(2)}) %collective-permute-start.42) | collective-permute-done | bytes 524320 | tf_op jit(solution)/shard_map/ppermute | solution.py:54
  362.3 8.9 %collective-permute-done.34 = f32[128,1024]{1,0:T(8,128)S(1)} collective-permute-done((f32[128,1024]{1,0:T(8,128)S(1)}, f32[128,1024]{1,0:T(8,128)S(1)}, u32[]{:S(2)}, u32[]{:S(2)}) %collective-permute-start.34) | collective-permute-done | bytes 524320 | tf_op jit(solution)/shard_map/ppermute | solution.py:54
  411.0 14.3 %abs_reduce_fusion.1 = (f32[]{:T(128)}, f32[]{:T(128)}, f32[4096,1024]{1,0:T(8,128)}) fusion(bf16[1024,1024]{1,0:T(8,128)(2,1)S(1)} %copy-done.20, bf16[512,4096]{1,0:T(8,128)(2,1)S(1)} %copy-done.34, bf16[512,4096]{1,0:T(8,128)(2,1)S(1)} %copy-done.36), kind=kOutput, calls=%fused_computation.3 | convolution fusion | flops 8623489024 | bytes 27262984 | tf_op jit(solution)/shard_map/dot_general | solution.py:24
  473.3 12.9 %collective-permute-done.51 = bf16[512,1024]{1,0:T(8,128)(2,1)} collective-permute-done((bf16[512,1024]{1,0:T(8,128)(2,1)}, bf16[512,1024]{1,0:T(8,128)(2,1)}, u32[]{:S(2)}, u32[]{:S(2)}) %collective-permute-start.51) | collective-permute-done | bytes 1048608 | tf_op jit(solution)/shard_map/ppermute | solution.py:54
  539.5 14.8 %collective-permute-done.59 = bf16[128,1024]{0,1:T(8,128)(2,1)S(1)} collective-permute-done((bf16[128,1024]{0,1:T(8,128)(2,1)}, bf16[128,1024]{0,1:T(8,128)(2,1)S(1)}, u32[]{:S(2)}, u32[]{:S(2)}) %collective-permute-start.59) | collective-permute-done | bytes 262176 | tf_op jit(solution)/shard_map/ppermute | solution.py:54
  571.9 32.2 %abs_reduce_fusion = (f32[]{:T(128)}, f32[]{:T(128)}, f32[9216,1024]{1,0:T(8,128)}) fusion(bf16[1024,9216]{1,0:T(8,128)(2,1)} %copy-done.1, bf16[1024,1024]{1,0:T(8,128)(2,1)S(1)} %fusion.6), kind=kOutput, calls=%fused_computation | convolution fusion | flops 19365101568 | bytes 58720264 | tf_op jit(solution)/shard_map/dot_general | solution.py:24
  685.2 7.7 fusion.15
  692.9 30.7 %collective-permute-done.77 = bf16[1040,1024]{1,0:T(8,128)(2,1)} collective-permute-done((bf16[1040,1024]{1,0:T(8,128)(2,1)}, bf16[1040,1024]{1,0:T(8,128)(2,1)}, u32[]{:S(2)}, u32[]{:S(2)}) %collective-permute-start.77) | collective-permute-done | bytes 2129952 | tf_op jit(solution)/shard_map/ppermute | solution.py:54
  738.8 31.2 %collective-permute-done.79 = bf16[1040,1024]{1,0:T(8,128)(2,1)} collective-permute-done((bf16[1040,1024]{1,0:T(8,128)(2,1)}, bf16[1040,1024]{1,0:T(8,128)(2,1)}, u32[]{:S(2)}, u32[]{:S(2)}) %collective-permute-start.79) | collective-permute-done | bytes 2129952 | tf_op jit(solution)/shard_map/ppermute | solution.py:54
  790.3 24.2 %collective-permute-done.83 = bf16[112,1024]{1,0:T(8,128)(2,1)S(1)} collective-permute-done((bf16[112,1024]{1,0:T(8,128)(2,1)}, bf16[112,1024]{1,0:T(8,128)(2,1)S(1)}, u32[]{:S(2)}, u32[]{:S(2)}) %collective-permute-start.83) | collective-permute-done | bytes 229408 | tf_op jit(solution)/shard_map/ppermute | solution.py:54
  844.1 12.8 %fusion.97 = (bf16[1152,1024]{1,0:T(8,128)(2,1)}, f32[1152,1024]{1,0:T(8,128)}, f32[1152,1024]{1,0:T(8,128)}, f32[1152,1024]{1,0:T(8,128)}) fusion(f32[1152,1024]{1,0:T(8,128)} %param.25, f32[112,1024]{1,0:T(8,128)S(1)} %convert_add_fusion.2, f32[1040,1024]{1,0:T(8,128)} %copy-done, f32[]{:T(128)} %bitcast.91, f32[]{:T(128)S(6)} %div.433, ...), kind=kLoop, calls=%fused_computation.274 | loop fusion | flops 21233664 | bytes 35389448 | tf_op jit(solution)/shard_map/convert_element_type | solution.py:683
  (457 shorter events, 477.6 us)
Async XLA Ops:
  0.7 38.5 %collective-permute-start.2 = (bf16[1024,2304]{1,0:T(8,128)(2,1)}, bf16[1024,2304]{1,0:T(8,128)(2,1)}, u32[]{:S(2)}, u32[]{:S(2)}) collective-permute-start(bf16[1024,2304]{1,0:T(8,128)(2,1)} %param.20), channel_id=1, source_target_pairs={{0,1},{1,0},{2,3},{3,2},{4,5},{5,4},{6,7},{7,6},{8,9},{9,8},{10,11... | collective-permute-start | bytes 14155784 | tf_op jit(solution)/shard_map/ppermute | solution.py:54
  1.2 105.3 %collective-permute-start.11 = (bf16[1024,2304]{1,0:T(8,128)(2,1)}, bf16[1024,2304]{1,0:T(8,128)(2,1)}, u32[]{:S(2)}, u32[]{:S(2)}) collective-permute-start(bf16[1024,2304]{1,0:T(8,128)(2,1)} %param.20), channel_id=1, source_target_pairs={{0,2},{1,3},{2,0},{3,1},{4,6},{5,7},{6,4},{7,5},{8,10},{9,11},{10,... | collective-permute-start | bytes 14155784 | tf_op jit(solution)/shard_map/ppermute | solution.py:54
  13.0 49.1 %collective-permute-start.5 = (bf16[576,1024]{1,0:T(8,128)(2,1)S(1)}, bf16[576,1024]{1,0:T(8,128)(2,1)}, u32[]{:S(2)}, u32[]{:S(2)}) collective-permute-start(bf16[576,1024]{1,0:T(8,128)(2,1)S(1)} %get-tuple-element.275), channel_id=1, source_target_pairs={{0,4},{4,0},{8,12},{12,8},{16,20},{20,16},{24,28},{28,24},{1,5},{5... | collective-permute-start | bytes 3538952 | tf_op jit(solution)/shard_map/ppermute | solution.py:54
  39.2 48.2 %collective-permute-start.3 = (bf16[576,1024]{1,0:T(8,128)(2,1)}, bf16[576,1024]{1,0:T(8,128)(2,1)}, u32[]{:S(2)}, u32[]{:S(2)}) collective-permute-start(bf16[576,1024]{1,0:T(8,128)(2,1)} %collective-permute-done.1), channel_id=1, source_target_pairs={{0,4},{4,0},{8,12},{12,8},{16,20},{20,16},{24,28},{28,24},{1,5},{5... | collective-permute-start | bytes 3538952 | tf_op jit(solution)/shard_map/ppermute | solution.py:54
  39.9 53.0 %collective-permute-start.4 = (bf16[576,1024]{1,0:T(8,128)(2,1)}, bf16[576,1024]{1,0:T(8,128)(2,1)}, u32[]{:S(2)}, u32[]{:S(2)}) collective-permute-start(bf16[576,1024]{1,0:T(8,128)(2,1)} %collective-permute-done.1), channel_id=1, source_target_pairs={{0,8},{4,12},{8,16},{12,20},{16,24},{20,28},{24,0},{28,4},{1,9},{5... | collective-permute-start | bytes 3538952 | tf_op jit(solution)/shard_map/ppermute | solution.py:59
  67.6 44.3 %collective-permute-start.9 = (bf16[576,1024]{1,0:T(8,128)(2,1)}, bf16[576,1024]{1,0:T(8,128)(2,1)}, u32[]{:S(2)}, u32[]{:S(2)}) collective-permute-start(bf16[576,1024]{1,0:T(8,128)(2,1)} %collective-permute-done.6), channel_id=1, source_target_pairs={{0,4},{4,0},{8,12},{12,8},{16,20},{20,16},{24,28},{28,24},{1,5},{5... | collective-permute-start | bytes 3538952 | tf_op jit(solution)/shard_map/ppermute | solution.py:54
  69.2 46.6 %collective-permute-start.10 = (bf16[576,1024]{1,0:T(8,128)(2,1)}, bf16[576,1024]{1,0:T(8,128)(2,1)}, u32[]{:S(2)}, u32[]{:S(2)}) collective-permute-start(bf16[576,1024]{1,0:T(8,128)(2,1)} %collective-permute-done.6), channel_id=1, source_target_pairs={{0,8},{4,12},{8,16},{12,20},{16,24},{20,28},{24,0},{28,4},{1,9},{5... | collective-permute-start | bytes 3538952 | tf_op jit(solution)/shard_map/ppermute | solution.py:59
  117.3 64.0 %collective-permute-start.15 = (bf16[576,1024]{1,0:T(8,128)(2,1)}, bf16[576,1024]{1,0:T(8,128)(2,1)S(1)}, u32[]{:S(2)}, u32[]{:S(2)}) collective-permute-start(bf16[576,1024]{1,0:T(8,128)(2,1)} %collective-permute-done.10), channel_id=1, source_target_pairs={{0,4},{4,0},{8,12},{12,8},{16,20},{20,16},{24,28},{28,24},{1,5},{5... | collective-permute-start | bytes 3538952 | tf_op jit(solution)/shard_map/ppermute | solution.py:54
  117.9 63.4 %collective-permute-start.17 = (bf16[576,1024]{1,0:T(8,128)(2,1)}, bf16[576,1024]{1,0:T(8,128)(2,1)S(1)}, u32[]{:S(2)}, u32[]{:S(2)}) collective-permute-start(bf16[576,1024]{1,0:T(8,128)(2,1)} %collective-permute-done.10), channel_id=1, source_target_pairs={{0,8},{4,12},{8,16},{12,20},{16,24},{20,28},{24,0},{28,4},{1,9},{5... | collective-permute-start | bytes 3538952 | tf_op jit(solution)/shard_map/ppermute | solution.py:59
  148.2 62.5 %collective-permute-start.13 = (bf16[576,1024]{1,0:T(8,128)(2,1)}, bf16[576,1024]{1,0:T(8,128)(2,1)}, u32[]{:S(2)}, u32[]{:S(2)}) collective-permute-start(bf16[576,1024]{1,0:T(8,128)(2,1)} %collective-permute-done.8), channel_id=1, source_target_pairs={{0,4},{4,0},{8,12},{12,8},{16,20},{20,16},{24,28},{28,24},{1,5},{5... | collective-permute-start | bytes 3538952 | tf_op jit(solution)/shard_map/ppermute | solution.py:54
  148.7 62.0 %collective-permute-start.14 = (bf16[384,1024]{1,0:T(8,128)(2,1)}, bf16[384,1024]{1,0:T(8,128)(2,1)S(1)}, u32[]{:S(2)}, u32[]{:S(2)}) collective-permute-start(bf16[384,1024]{1,0:T(8,128)(2,1)} %fusion.37), channel_id=1, source_target_pairs={{0,8},{4,12},{8,16},{12,20},{16,24},{20,28},{24,0},{28,4},{1,9},{5... | collective-permute-start | bytes 2359304 | tf_op jit(solution)/shard_map/ppermute | solution.py:59
  182.1 49.8 %collective-permute-start.20 = (bf16[576,1024]{1,0:T(8,128)(2,1)S(1)}, bf16[576,1024]{1,0:T(8,128)(2,1)}, u32[]{:S(2)}, u32[]{:S(2)}) collective-permute-start(bf16[576,1024]{1,0:T(8,128)(2,1)S(1)} %collective-permute-done.17), channel_id=1, source_target_pairs={{0,4},{4,0},{8,12},{12,8},{16,20},{20,16},{24,28},{28,24},{1,5},{5... | collective-permute-start | bytes 3538952 | tf_op jit(solution)/shard_map/ppermute | solution.py:54
  231.9 38.8 %collective-permute-start.25 = (bf16[512,1024]{1,0:T(8,128)(2,1)}, bf16[512,1024]{1,0:T(8,128)(2,1)}, u32[]{:S(2)}, u32[]{:S(2)}) collective-permute-start(bf16[512,1024]{1,0:T(8,128)(2,1)} %collective-permute-done.21), channel_id=1, source_target_pairs={{0,8},{4,12},{8,16},{12,20},{16,24},{20,28},{24,0},{28,4},{1,9},{5... | collective-permute-start | bytes 3145736 | tf_op jit(solution)/shard_map/ppermute | solution.py:59
  273.6 41.6 %collective-permute-start.30 = (bf16[512,1024]{1,0:T(8,128)(2,1)}, bf16[512,1024]{1,0:T(8,128)(2,1)S(1)}, u32[]{:S(2)}, u32[]{:S(2)}) collective-permute-start(bf16[512,1024]{1,0:T(8,128)(2,1)} %collective-permute-done.25), channel_id=1, source_target_pairs={{0,8},{4,12},{8,16},{12,20},{16,24},{20,28},{24,0},{28,4},{1,9},{5... | collective-permute-start | bytes 3145736 | tf_op jit(solution)/shard_map/ppermute | solution.py:59
  561.9 46.3 %collective-permute-start.64 = (bf16[128,1024]{0,1:T(8,128)(2,1)S(1)}, bf16[128,1024]{0,1:T(8,128)(2,1)}, u32[]{:S(2)}, u32[]{:S(2)}) collective-permute-start(bf16[128,1024]{0,1:T(8,128)(2,1)S(1)} %bitcast.337), channel_id=1, source_target_pairs={{0,4},{4,0},{8,12},{12,8},{16,20},{20,16},{24,28},{28,24},{1,5},{5... | collective-permute-start | bytes 786440 | tf_op jit(solution)/shard_map/ppermute | solution.py:54
  562.5 45.8 %collective-permute-start.65 = (bf16[512,1024]{1,0:T(8,128)(2,1)S(1)}, bf16[512,1024]{1,0:T(8,128)(2,1)}, u32[]{:S(2)}, u32[]{:S(2)}) collective-permute-start(bf16[512,1024]{1,0:T(8,128)(2,1)S(1)} %get-tuple-element.451), channel_id=1, source_target_pairs={{0,4},{4,0},{8,12},{12,8},{16,20},{20,16},{24,28},{28,24},{1,5},{5... | collective-permute-start | bytes 3145736 | tf_op jit(solution)/shard_map/ppermute | solution.py:54
  564.8 43.4 %collective-permute-start.66 = (bf16[128,1024]{0,1:T(8,128)(2,1)}, bf16[128,1024]{0,1:T(8,128)(2,1)}, u32[]{:S(2)}, u32[]{:S(2)}) collective-permute-start(bf16[128,1024]{0,1:T(8,128)(2,1)} %add_convert_fusion.8), channel_id=1, source_target_pairs={{0,8},{4,12},{8,16},{12,20},{16,24},{20,28},{24,0},{28,4},{1,9},{5... | collective-permute-start | bytes 786440 | tf_op jit(solution)/shard_map/ppermute | solution.py:59
  568.0 40.3 %collective-permute-start.67 = (bf16[512,1024]{1,0:T(8,128)(2,1)}, bf16[512,1024]{1,0:T(8,128)(2,1)}, u32[]{:S(2)}, u32[]{:S(2)}) collective-permute-start(bf16[512,1024]{1,0:T(8,128)(2,1)} %add_convert_fusion.3), channel_id=1, source_target_pairs={{0,8},{4,12},{8,16},{12,20},{16,24},{20,28},{24,0},{28,4},{1,9},{5... | collective-permute-start | bytes 3145736 | tf_op jit(solution)/shard_map/ppermute | solution.py:59
  677.1 46.5 %collective-permute-start.77 = (bf16[1040,1024]{1,0:T(8,128)(2,1)}, bf16[1040,1024]{1,0:T(8,128)(2,1)}, u32[]{:S(2)}, u32[]{:S(2)}) collective-permute-start(bf16[1040,1024]{1,0:T(8,128)(2,1)} %fusion.13), channel_id=1, source_target_pairs={{0,4},{4,0},{8,12},{12,8},{16,20},{20,16},{24,28},{28,24},{1,5},{5... | collective-permute-start | bytes 6389768 | tf_op jit(solution)/shard_map/ppermute | solution.py:54
  681.0 42.6 %collective-permute-start.78 = (bf16[1040,1024]{1,0:T(8,128)(2,1)}, bf16[1040,1024]{1,0:T(8,128)(2,1)}, u32[]{:S(2)}, u32[]{:S(2)}) collective-permute-start(bf16[1040,1024]{1,0:T(8,128)(2,1)} %add_convert_fusion.2), channel_id=1, source_target_pairs={{0,8},{4,12},{8,16},{12,20},{16,24},{20,28},{24,0},{28,4},{1,9},{5... | collective-permute-start | bytes 6389768 | tf_op jit(solution)/shard_map/ppermute | solution.py:59
  723.6 46.4 %collective-permute-start.79 = (bf16[1040,1024]{1,0:T(8,128)(2,1)}, bf16[1040,1024]{1,0:T(8,128)(2,1)}, u32[]{:S(2)}, u32[]{:S(2)}) collective-permute-start(bf16[1040,1024]{1,0:T(8,128)(2,1)} %get-tuple-element.505), channel_id=1, source_target_pairs={{0,4},{4,0},{8,12},{12,8},{16,20},{20,16},{24,28},{28,24},{1,5},{5... | collective-permute-start | bytes 6389768 | tf_op jit(solution)/shard_map/ppermute | solution.py:54
  728.9 41.1 %collective-permute-start.80 = (bf16[1040,1024]{1,0:T(8,128)(2,1)}, bf16[1040,1024]{1,0:T(8,128)(2,1)}, u32[]{:S(2)}, u32[]{:S(2)}) collective-permute-start(bf16[1040,1024]{1,0:T(8,128)(2,1)} %add_convert_fusion.1), channel_id=1, source_target_pairs={{0,8},{4,12},{8,16},{12,20},{16,24},{20,28},{24,0},{28,4},{1,9},{5... | collective-permute-start | bytes 6389768 | tf_op jit(solution)/shard_map/ppermute | solution.py:59
  770.0 44.5 %collective-permute-start.81 = (bf16[1040,1024]{1,0:T(8,128)(2,1)}, bf16[1040,1024]{1,0:T(8,128)(2,1)}, u32[]{:S(2)}, u32[]{:S(2)}) collective-permute-start(bf16[1040,1024]{1,0:T(8,128)(2,1)} %get-tuple-element.513), channel_id=1, source_target_pairs={{0,4},{4,0},{8,12},{12,8},{16,20},{20,16},{24,28},{28,24},{1,5},{5... | collective-permute-start | bytes 6389768 | tf_op jit(solution)/shard_map/ppermute | solution.py:54
  775.4 39.1 %collective-permute-start.82 = (bf16[1040,1024]{1,0:T(8,128)(2,1)}, bf16[1040,1024]{1,0:T(8,128)(2,1)}, u32[]{:S(2)}, u32[]{:S(2)}) collective-permute-start(bf16[1040,1024]{1,0:T(8,128)(2,1)} %add_convert_fusion), channel_id=1, source_target_pairs={{0,8},{4,12},{8,16},{12,20},{16,24},{20,28},{24,0},{28,4},{1,9},{5... | collective-permute-start | bytes 6389768 | tf_op jit(solution)/shard_map/ppermute | solution.py:59
  (122 other events, 2021.2 us)

commit v4 on v3

--- a/solution.py
+++ b/solution.py
@@ -232,17 +232,21 @@
                     wholes = store_first(wholes, piece, hop, int(axis == "y"), row)
             elif name == "f":
                 wholes = store(wholes, piece, hop, int(axis == "y"), 0)
+                if axis == "y" and hop == rings - 1:
+                    last[name] = piece
             elif name == "n":
                 wholes = store(wholes, piece, 0, 1, cut)
                 ready["p", 0] = jnp.concatenate([ready["n",], piece])
             else:
+                if hop == rings - 1:
+                    last[name] = piece
                 for flip in (0, 1):
                     wholes = store(wholes, piece[flip * near : (flip + 1) * near], hop, flip, cut)
             if axis == "z":
                 ready[name, hop] = piece
         flight = started
         step += 1
-    return wholes, carried | (pending or {})
+    return wholes, last, carried | (pending or {})
 
 
 def scatter(grads, limits, tops, noises, groups, nears, ahead, beside, carried):
@@ -443,6 +447,11 @@
         for item in halves(out_six):
             blocks = {0: item} | over_far(item)
             hidden_blocks.append(blocks | over_near(blocks))
+        hiddens = [join([blocks]) for blocks in hidden_blocks]
+
+        def sum_seven(number):
+            return matmul(hiddens[number], kept_seven.reshape(-1, width))
+
     else:
         count = 2 * rings
 
@@ -485,7 +494,17 @@
             return carried | {"one": crossing["one"]}, None
 
         def hidden_one_near(carried, wholes, last):
-            return carried | {"one_near": over_near(carried["one"])}, None
+            blocks = {0: carried["out"][0]} | carried["own"][0] | carried["one"]
+            hidden = join([blocks | over_near(carried["one"])])
+            early = matmul(hidden, wholes[2].reshape(-1, width))
+            return carried, {"hidden_one": hidden, "early_one": early}
+
+        def fc_seven_most(carried, wholes, last):
+            far = crossing["two"]
+            two = join([{0: carried["out"][1]} | carried["own"][1] | far | over_near(far)])
+            early = matmul(two, wholes[2].reshape(-1, width))
+            names = ("inputs", "noise", "pre")
+            return {name: carried[name] for name in names} | {"hidden_two": two, "early_two": early}, None
 
         hooks = {
             1: own_near,
@@ -497,9 +516,10 @@
             count + 2: hidden_own,
             count + 3: hidden_one,
             count + 4: hidden_one_near,
+            count + 5: fc_seven_most,
         }
         near = (rows_six + rows_seven + rows_eight) // (2 * rings - 2) // 16 * 16
-        (_, kept_eight, kept_seven), carried = gather_queue(
+        (_, kept_eight, kept_seven), last, carried = gather_queue(
             shards_cast[0],
             shards_cast[1:],
             [group_six, [None, group_seven]],
@@ -508,18 +528,32 @@
             {},
         )
         inputs, noise_wide, pre_six = carried["inputs"], carried["noise"], carried["pre"]
-        one, two = carried["out"]
-        hidden_blocks = [
-            {0: one} | carried["own"][0] | carried["one"] | carried["one_near"],
-            {0: two} | carried["own"][1] | crossing["two"] | over_near(crossing["two"]),
-        ]
+        hiddens = [carried["hidden_one"], carried["hidden_two"]]
+        start = place(owner(rings - 1, 1), group_seven) * rows_seven
+        other_start = place(owner(rings - 1, 0), group_seven) * rows_seven
+        rest = last["f"][rows_eight:]
+        count, most = last["p"].shape[0] // 2, rest.shape[0]
+
+        def columns(number, low, size):
+            return lax.dynamic_slice_in_dim(hiddens[number], low, size, 1)
+
+        def sum_seven(number):
+            if number == 1:
+                return carried["early_two"] + matmul(columns(1, start, most), rest)
+            whole_block = jnp.concatenate([rest, last["p"][count:]])
+            return (
+                carried["early_one"]
+                + matmul(columns(0, start, rows_seven), whole_block)
+                + matmul(columns(0, other_start + most, count), last["p"][:count])
+            )
+
     kept_seven, kept_eight = kept_seven.reshape(-1, width), kept_eight.reshape(-1, padded)
 
     bias_wide = jnp.pad(bias_out, (0, padded - outs), constant_values=-1e30)
     share = half // ways
 
     def half_forward(number):
-        pre, out = layer_forward(matmul(join([hidden_blocks[number]]), kept_seven), biases[1])
+        pre, out = layer_forward(sum_seven(number), biases[1])
         shares = out.reshape(ways, share, width)
         parts = {
             step: matmul(lax.dynamic_index_in_dim(shares, mine ^ step, 0, keepdims=False), kept_eight)
@@ -548,7 +582,7 @@
         jnp.concatenate([item[spot] for item in both]) for spot in range(3)
     )
     loss_part = both[0][3] + both[1][3]
-    hidden = join(hidden_blocks)
+    hidden = jnp.concatenate(hiddens)
 
     delta_seven = layer_delta(pre_seven, against_rows(dlogits, kept_eight))
 

time: 882 us -> 870 us (0.986)
  waiting for transfers between devices: 358 us -> 349 us
    ppermute x24, waiting for transfers between devices: 53.6 us -> 39.2 us  [turn(): return lax.ppermute(value, 'dp', [(i, (i + 2) % size) for i in range(size)])]
    dot_general x12 -> x15, matrix products: 50.2 us -> 51.7 us  [matmul(): return jnp.dot(left, right, preferred_element_type=jnp.float32)]
  transfers between devices with their start and end apart: 89 -> 89, of which waited for: 48 -> 46; matrix products, arithmetic and copies ran while one was open for 37% -> 38% of each run, Pallas kernels for 0% -> 0%
where the time goes in v4:
time: 870 us; the launch traced here: 855 us
  waiting for transfers between devices  349 us (40%)
  other arithmetic  174 us (20%)
  matrix products  129 us (15%)
  local copies, waits for them, and re-layouts  113 us (13%)
  starting transfers between devices  73.1 us (8%)
  between operations  16 us (2%)
    ppermute x65, waiting for transfers between devices, swap(): return lax.ppermute(value, axis, [(i, i ^ bit) for i in range(size)])  310 us
    convert_element_type x18, other arithmetic, soft_ternary(): return value.astype(jnp.bfloat16)  74.4 us
    dynamic_update_slice x44, local copies, waits for them, and re-layouts, put(): return lax.dynamic_update_slice(whole, piece[None], (index, row, 0))  55.8 us
    dot_general x3, matrix products, contract_rows(): lax.dot_general(left, right, (((0,), (0,)), ((), ())), preferred_element_...  51.8 us
    dot_general x15, matrix products, matmul(): return jnp.dot(left, right, preferred_element_type=jnp.float32)  51.7 us
    ppermute x65, starting transfers between devices, swap(): return lax.ppermute(value, axis, [(i, i ^ bit) for i in range(size)])  50.2 us
    ppermute x24, waiting for transfers between devices, turn(): return lax.ppermute(value, 'dp', [(i, (i + 2) % size) for i in range(size)])  39.2 us
    convert_element_type x11, other arithmetic, narrow(): return value.astype(jnp.bfloat16)  31.2 us
  transfers between devices with their start and end apart: 89, of which 46 were waited for; matrix products, arithmetic and copies ran while one was open for 38% of the time, Pallas kernels for 0%

profile of v4, /device:TPU:0, one launch (start us, length us, event | category | flops | bytes accessed | tf_op | source)
XLA Modules:
  0.0 854.6 jit_solution(865831428989056438)
XLA Ops:
  28.2 8.6 %collective-permute-done = bf16[576,1024]{1,0:T(8,128)(2,1)} collective-permute-done((bf16[576,1024]{1,0:T(8,128)(2,1)}, bf16[576,1024]{1,0:T(8,128)(2,1)}, u32[]{:S(2)}, u32[]{:S(2)}) %collective-permute-start) | collective-permute-done | bytes 1179680 | tf_op jit(solution)/shard_map/ppermute | solution.py:54
  52.6 9.5 %collective-permute-done.5 = bf16[576,1024]{1,0:T(8,128)(2,1)} collective-permute-done((bf16[576,1024]{1,0:T(8,128)(2,1)S(1)}, bf16[576,1024]{1,0:T(8,128)(2,1)}, u32[]{:S(2)}, u32[]{:S(2)}) %collective-permute-start.5) | collective-permute-done | bytes 1179680 | tf_op jit(solution)/shard_map/ppermute | solution.py:54
  73.9 13.5 %collective-permute-done.3 = bf16[576,1024]{1,0:T(8,128)(2,1)} collective-permute-done((bf16[576,1024]{1,0:T(8,128)(2,1)}, bf16[576,1024]{1,0:T(8,128)(2,1)}, u32[]{:S(2)}, u32[]{:S(2)}) %collective-permute-start.3) | collective-permute-done | bytes 1179680 | tf_op jit(solution)/shard_map/ppermute | solution.py:54
  97.7 8.8 %collective-permute-done.11 = bf16[1024,2304]{1,0:T(8,128)(2,1)} collective-permute-done((bf16[1024,2304]{1,0:T(8,128)(2,1)}, bf16[1024,2304]{1,0:T(8,128)(2,1)}, u32[]{:S(2)}, u32[]{:S(2)}) %collective-permute-start.11) | collective-permute-done | bytes 4718624 | tf_op jit(solution)/shard_map/ppermute | solution.py:54
  122.6 22.1 %collective-permute-done.7 = bf16[576,1024]{1,0:T(8,128)(2,1)} collective-permute-done((bf16[576,1024]{1,0:T(8,128)(2,1)}, bf16[576,1024]{1,0:T(8,128)(2,1)}, u32[]{:S(2)}, u32[]{:S(2)}) %collective-permute-start.7) | collective-permute-done | bytes 1179680 | tf_op jit(solution)/shard_map/ppermute | solution.py:54
  148.6 9.8 %pad_maximum_fusion = bf16[1024,9216]{1,0:T(8,128)(2,1)S(1)} fusion(bf16[1024,2304]{1,0:T(8,128)(2,1)} %collective-permute-done.12, bf16[1024,2304]{1,0:T(8,128)(2,1)} %collective-permute-done.11, bf16[1024,2304]{1,0:T(8,128)(2,1)} %collective-permute-done.2, bf16[1024,2304]{1,0:T(8,128)(2,1)} %param.20), kind=kLoop, calls=%fused_computation.2 | loop fusion | flops 75497472 | bytes 37748736 | tf_op jit(solution)/shard_map/concatenate | solution.py:428
  165.5 15.6 %collective-permute-done.16 = bf16[256,1024]{1,0:T(8,128)(2,1)S(1)} collective-permute-done((bf16[256,1024]{1,0:T(8,128)(2,1)S(1)}, bf16[256,1024]{1,0:T(8,128)(2,1)S(1)}, u32[]{:S(2)}, u32[]{:S(2)}) %collective-permute-start.16) | collective-permute-done | bytes 524320 | tf_op jit(solution)/shard_map/ppermute | solution.py:54
  185.2 23.0 %fusion.126 = f32[1024,1024]{1,0:T(8,128)S(1)} fusion(bf16[1024,9216]{1,0:T(8,128)(2,1)S(1)} %pad_maximum_fusion, bf16[9216,1024]{1,0:T(8,128)(2,1)} %bitcast.20), kind=kOutput, calls=%fused_computation.300 | convolution fusion | flops 19327352832 | bytes 41943040 | tf_op jit(solution)/shard_map/dot_general | solution.py:20
  213.7 18.1 %collective-permute-done.20 = bf16[576,1024]{1,0:T(8,128)(2,1)} collective-permute-done((bf16[576,1024]{1,0:T(8,128)(2,1)S(1)}, bf16[576,1024]{1,0:T(8,128)(2,1)}, u32[]{:S(2)}, u32[]{:S(2)}) %collective-permute-start.20) | collective-permute-done | bytes 1179680 | tf_op jit(solution)/shard_map/ppermute | solution.py:54
  282.3 10.8 %collective-permute-done.28 = bf16[512,1024]{1,0:T(8,128)(2,1)S(1)} collective-permute-done((bf16[512,1024]{1,0:T(8,128)(2,1)}, bf16[512,1024]{1,0:T(8,128)(2,1)S(1)}, u32[]{:S(2)}, u32[]{:S(2)}) %collective-permute-start.28) | collective-permute-done | bytes 1048608 | tf_op jit(solution)/shard_map/ppermute | solution.py:54
  300.2 8.4 fusion.128
  317.0 8.4 fusion.127
  335.4 11.4 %collective-permute-done.42 = f32[128,1024]{1,0:T(8,128)S(1)} collective-permute-done((f32[128,1024]{1,0:T(8,128)S(1)}, f32[128,1024]{1,0:T(8,128)S(1)}, u32[]{:S(2)}, u32[]{:S(2)}) %collective-permute-start.42) | collective-permute-done | bytes 524320 | tf_op jit(solution)/shard_map/ppermute | solution.py:54
  349.2 8.8 %collective-permute-done.36 = f32[128,1024]{1,0:T(8,128)S(1)} collective-permute-done((f32[128,1024]{1,0:T(8,128)S(1)}, f32[128,1024]{1,0:T(8,128)S(1)}, u32[]{:S(2)}, u32[]{:S(2)}) %collective-permute-start.36) | collective-permute-done | bytes 524320 | tf_op jit(solution)/shard_map/ppermute | solution.py:54
  398.7 14.2 %abs_reduce_fusion.1 = (f32[]{:T(128)}, f32[]{:T(128)}, f32[4096,1024]{1,0:T(8,128)}) fusion(bf16[1024,1024]{1,0:T(8,128)(2,1)S(1)} %copy-done.22, bf16[512,4096]{1,0:T(8,128)(2,1)S(1)} %copy-done.41, bf16[512,4096]{1,0:T(8,128)(2,1)S(1)} %copy-done.37), kind=kOutput, calls=%fused_computation.3 | convolution fusion | flops 8623489024 | bytes 27262984 | tf_op jit(solution)/shard_map/dot_general | solution.py:24
  461.5 12.3 %collective-permute-done.51 = bf16[512,1024]{1,0:T(8,128)(2,1)} collective-permute-done((bf16[512,1024]{1,0:T(8,128)(2,1)}, bf16[512,1024]{1,0:T(8,128)(2,1)}, u32[]{:S(2)}, u32[]{:S(2)}) %collective-permute-start.51) | collective-permute-done | bytes 1048608 | tf_op jit(solution)/shard_map/ppermute | solution.py:54
  494.0 14.4 %collective-permute-done.54 = bf16[128,1024]{0,1:T(8,128)(2,1)} collective-permute-done((bf16[128,1024]{0,1:T(8,128)(2,1)}, bf16[128,1024]{0,1:T(8,128)(2,1)}, u32[]{:S(2)}, u32[]{:S(2)}) %collective-permute-start.54) | collective-permute-done | bytes 262176 | tf_op jit(solution)/shard_map/ppermute | solution.py:54
  531.2 10.3 %collective-permute-done.59 = bf16[128,1024]{0,1:T(8,128)(2,1)} collective-permute-done((bf16[128,1024]{0,1:T(8,128)(2,1)}, bf16[128,1024]{0,1:T(8,128)(2,1)}, u32[]{:S(2)}, u32[]{:S(2)}) %collective-permute-start.59) | collective-permute-done | bytes 262176 | tf_op jit(solution)/shard_map/ppermute | solution.py:54
  559.7 32.4 %abs_reduce_fusion = (f32[]{:T(128)}, f32[]{:T(128)}, f32[9216,1024]{1,0:T(8,128)}) fusion(bf16[1024,9216]{1,0:T(8,128)(2,1)} %copy-done.1, bf16[1024,1024]{1,0:T(8,128)(2,1)S(1)} %fusion.6), kind=kOutput, calls=%fused_computation | convolution fusion | flops 19365101568 | bytes 58720264 | tf_op jit(solution)/shard_map/dot_general | solution.py:24
  673.2 7.7 fusion.15
  681.0 31.3 %collective-permute-done.77 = bf16[1040,1024]{1,0:T(8,128)(2,1)} collective-permute-done((bf16[1040,1024]{1,0:T(8,128)(2,1)}, bf16[1040,1024]{1,0:T(8,128)(2,1)}, u32[]{:S(2)}, u32[]{:S(2)}) %collective-permute-start.77) | collective-permute-done | bytes 2129952 | tf_op jit(solution)/shard_map/ppermute | solution.py:54
  727.3 31.4 %collective-permute-done.79 = bf16[1040,1024]{1,0:T(8,128)(2,1)} collective-permute-done((bf16[1040,1024]{1,0:T(8,128)(2,1)}, bf16[1040,1024]{1,0:T(8,128)(2,1)}, u32[]{:S(2)}, u32[]{:S(2)}) %collective-permute-start.79) | collective-permute-done | bytes 2129952 | tf_op jit(solution)/shard_map/ppermute | solution.py:54
  778.6 24.4 %collective-permute-done.83 = bf16[112,1024]{1,0:T(8,128)(2,1)S(1)} collective-permute-done((bf16[112,1024]{1,0:T(8,128)(2,1)}, bf16[112,1024]{1,0:T(8,128)(2,1)S(1)}, u32[]{:S(2)}, u32[]{:S(2)}) %collective-permute-start.83) | collective-permute-done | bytes 229408 | tf_op jit(solution)/shard_map/ppermute | solution.py:54
  832.8 12.8 %fusion.114 = (bf16[1152,1024]{1,0:T(8,128)(2,1)}, f32[1152,1024]{1,0:T(8,128)}, f32[1152,1024]{1,0:T(8,128)}, f32[1152,1024]{1,0:T(8,128)}) fusion(f32[1152,1024]{1,0:T(8,128)} %param.25, f32[112,1024]{1,0:T(8,128)S(1)} %convert_add_fusion.2, f32[1040,1024]{1,0:T(8,128)} %copy-done, f32[]{:T(128)} %bitcast.92, f32[]{:T(128)S(6)} %div.435, ...), kind=kLoop, calls=%fused_computation.289 | loop fusion | flops 21233664 | bytes 35389448 | tf_op jit(solution)/shard_map/convert_element_type | solution.py:717
  (471 shorter events, 470.6 us)
Async XLA Ops:
  1.2 105.3 %collective-permute-start.11 = (bf16[1024,2304]{1,0:T(8,128)(2,1)}, bf16[1024,2304]{1,0:T(8,128)(2,1)}, u32[]{:S(2)}, u32[]{:S(2)}) collective-permute-start(bf16[1024,2304]{1,0:T(8,128)(2,1)} %param.20), channel_id=1, source_target_pairs={{0,2},{1,3},{2,0},{3,1},{4,6},{5,7},{6,4},{7,5},{8,10},{9,11},{10,... | collective-permute-start | bytes 14155784 | tf_op jit(solution)/shard_map/ppermute | solution.py:54
  13.0 49.1 %collective-permute-start.5 = (bf16[576,1024]{1,0:T(8,128)(2,1)S(1)}, bf16[576,1024]{1,0:T(8,128)(2,1)}, u32[]{:S(2)}, u32[]{:S(2)}) collective-permute-start(bf16[576,1024]{1,0:T(8,128)(2,1)S(1)} %get-tuple-element.270), channel_id=1, source_target_pairs={{0,4},{4,0},{8,12},{12,8},{16,20},{20,16},{24,28},{28,24},{1,5},{5... | collective-permute-start | bytes 3538952 | tf_op jit(solution)/shard_map/ppermute | solution.py:54
  39.2 48.2 %collective-permute-start.3 = (bf16[576,1024]{1,0:T(8,128)(2,1)}, bf16[576,1024]{1,0:T(8,128)(2,1)}, u32[]{:S(2)}, u32[]{:S(2)}) collective-permute-start(bf16[576,1024]{1,0:T(8,128)(2,1)} %collective-permute-done.1), channel_id=1, source_target_pairs={{0,4},{4,0},{8,12},{12,8},{16,20},{20,16},{24,28},{28,24},{1,5},{5... | collective-permute-start | bytes 3538952 | tf_op jit(solution)/shard_map/ppermute | solution.py:54
  39.9 53.0 %collective-permute-start.4 = (bf16[576,1024]{1,0:T(8,128)(2,1)}, bf16[576,1024]{1,0:T(8,128)(2,1)}, u32[]{:S(2)}, u32[]{:S(2)}) collective-permute-start(bf16[576,1024]{1,0:T(8,128)(2,1)} %collective-permute-done.1), channel_id=1, source_target_pairs={{0,8},{4,12},{8,16},{12,20},{16,24},{20,28},{24,0},{28,4},{1,9},{5... | collective-permute-start | bytes 3538952 | tf_op jit(solution)/shard_map/ppermute | solution.py:59
  67.6 44.3 %collective-permute-start.9 = (bf16[576,1024]{1,0:T(8,128)(2,1)}, bf16[576,1024]{1,0:T(8,128)(2,1)}, u32[]{:S(2)}, u32[]{:S(2)}) collective-permute-start(bf16[576,1024]{1,0:T(8,128)(2,1)} %collective-permute-done.6), channel_id=1, source_target_pairs={{0,4},{4,0},{8,12},{12,8},{16,20},{20,16},{24,28},{28,24},{1,5},{5... | collective-permute-start | bytes 3538952 | tf_op jit(solution)/shard_map/ppermute | solution.py:54
  69.1 46.5 %collective-permute-start.10 = (bf16[576,1024]{1,0:T(8,128)(2,1)}, bf16[576,1024]{1,0:T(8,128)(2,1)S(1)}, u32[]{:S(2)}, u32[]{:S(2)}) collective-permute-start(bf16[576,1024]{1,0:T(8,128)(2,1)} %collective-permute-done.6), channel_id=1, source_target_pairs={{0,8},{4,12},{8,16},{12,20},{16,24},{20,28},{24,0},{28,4},{1,9},{5... | collective-permute-start | bytes 3538952 | tf_op jit(solution)/shard_map/ppermute | solution.py:59
  117.2 63.9 %collective-permute-start.15 = (bf16[576,1024]{1,0:T(8,128)(2,1)S(1)}, bf16[576,1024]{1,0:T(8,128)(2,1)S(1)}, u32[]{:S(2)}, u32[]{:S(2)}) collective-permute-start(bf16[576,1024]{1,0:T(8,128)(2,1)S(1)} %collective-permute-done.10), channel_id=1, source_target_pairs={{0,4},{4,0},{8,12},{12,8},{16,20},{20,16},{24,28},{28,24},{1,5},{5... | collective-permute-start | bytes 3538952 | tf_op jit(solution)/shard_map/ppermute | solution.py:54
  117.8 63.4 %collective-permute-start.17 = (bf16[576,1024]{1,0:T(8,128)(2,1)S(1)}, bf16[576,1024]{1,0:T(8,128)(2,1)S(1)}, u32[]{:S(2)}, u32[]{:S(2)}) collective-permute-start(bf16[576,1024]{1,0:T(8,128)(2,1)S(1)} %collective-permute-done.10), channel_id=1, source_target_pairs={{0,8},{4,12},{8,16},{12,20},{16,24},{20,28},{24,0},{28,4},{1,9},{5... | collective-permute-start | bytes 3538952 | tf_op jit(solution)/shard_map/ppermute | solution.py:59
  148.1 61.0 %collective-permute-start.13 = (bf16[576,1024]{1,0:T(8,128)(2,1)}, bf16[576,1024]{1,0:T(8,128)(2,1)}, u32[]{:S(2)}, u32[]{:S(2)}) collective-permute-start(bf16[576,1024]{1,0:T(8,128)(2,1)} %collective-permute-done.8), channel_id=1, source_target_pairs={{0,4},{4,0},{8,12},{12,8},{16,20},{20,16},{24,28},{28,24},{1,5},{5... | collective-permute-start | bytes 3538952 | tf_op jit(solution)/shard_map/ppermute | solution.py:54
  148.6 60.5 %collective-permute-start.14 = (bf16[384,1024]{1,0:T(8,128)(2,1)S(1)}, bf16[384,1024]{1,0:T(8,128)(2,1)}, u32[]{:S(2)}, u32[]{:S(2)}) collective-permute-start(bf16[384,1024]{1,0:T(8,128)(2,1)S(1)} %copy-done.15), channel_id=1, source_target_pairs={{0,8},{4,12},{8,16},{12,20},{16,24},{20,28},{24,0},{28,4},{1,9},{5... | collective-permute-start | bytes 2359304 | tf_op jit(solution)/shard_map/ppermute | solution.py:59
  181.2 50.6 %collective-permute-start.20 = (bf16[576,1024]{1,0:T(8,128)(2,1)S(1)}, bf16[576,1024]{1,0:T(8,128)(2,1)}, u32[]{:S(2)}, u32[]{:S(2)}) collective-permute-start(bf16[576,1024]{1,0:T(8,128)(2,1)S(1)} %collective-permute-done.17), channel_id=1, source_target_pairs={{0,4},{4,0},{8,12},{12,8},{16,20},{20,16},{24,28},{28,24},{1,5},{5... | collective-permute-start | bytes 3538952 | tf_op jit(solution)/shard_map/ppermute | solution.py:54
  209.1 41.7 %collective-permute-start.18 = (bf16[384,1024]{1,0:T(8,128)(2,1)S(1)}, bf16[384,1024]{1,0:T(8,128)(2,1)}, u32[]{:S(2)}, u32[]{:S(2)}) collective-permute-start(bf16[384,1024]{1,0:T(8,128)(2,1)S(1)} %copy-done.15), channel_id=1, source_target_pairs={{0,4},{4,0},{8,12},{12,8},{16,20},{20,16},{24,28},{28,24},{1,5},{5... | collective-permute-start | bytes 2359304 | tf_op jit(solution)/shard_map/ppermute | solution.py:54
  209.5 41.3 %collective-permute-start.19 = (bf16[384,1024]{1,0:T(8,128)(2,1)}, bf16[384,1024]{1,0:T(8,128)(2,1)S(1)}, u32[]{:S(2)}, u32[]{:S(2)}) collective-permute-start(bf16[384,1024]{1,0:T(8,128)(2,1)} %collective-permute-done.14), channel_id=1, source_target_pairs={{0,8},{4,12},{8,16},{12,20},{16,24},{20,28},{24,0},{28,4},{1,9},{5... | collective-permute-start | bytes 2359304 | tf_op jit(solution)/shard_map/ppermute | solution.py:59
  274.0 43.0 %collective-permute-start.32 = (bf16[512,1024]{1,0:T(8,128)(2,1)}, bf16[512,1024]{1,0:T(8,128)(2,1)S(1)}, u32[]{:S(2)}, u32[]{:S(2)}) collective-permute-start(bf16[512,1024]{1,0:T(8,128)(2,1)} %collective-permute-done.31), channel_id=1, source_target_pairs={{0,1},{1,0},{2,3},{3,2},{4,5},{5,4},{6,7},{7,6},{8,9},{9,8},{10,11... | collective-permute-start | bytes 3145736 | tf_op jit(solution)/shard_map/ppermute | solution.py:54
  274.0 38.6 %collective-permute-start.30 = (bf16[512,1024]{1,0:T(8,128)(2,1)}, bf16[512,1024]{1,0:T(8,128)(2,1)S(1)}, u32[]{:S(2)}, u32[]{:S(2)}) collective-permute-start(bf16[512,1024]{1,0:T(8,128)(2,1)} %collective-permute-done.25), channel_id=1, source_target_pairs={{0,8},{4,12},{8,16},{12,20},{16,24},{20,28},{24,0},{28,4},{1,9},{5... | collective-permute-start | bytes 3145736 | tf_op jit(solution)/shard_map/ppermute | solution.py:59
  548.8 47.7 %collective-permute-start.64 = (bf16[128,1024]{0,1:T(8,128)(2,1)}, bf16[128,1024]{0,1:T(8,128)(2,1)}, u32[]{:S(2)}, u32[]{:S(2)}) collective-permute-start(bf16[128,1024]{0,1:T(8,128)(2,1)} %bitcast.85), channel_id=1, source_target_pairs={{0,4},{4,0},{8,12},{12,8},{16,20},{20,16},{24,28},{28,24},{1,5},{5... | collective-permute-start | bytes 786440 | tf_op jit(solution)/shard_map/ppermute | solution.py:54
  549.4 47.1 %collective-permute-start.65 = (bf16[512,1024]{1,0:T(8,128)(2,1)}, bf16[512,1024]{1,0:T(8,128)(2,1)}, u32[]{:S(2)}, u32[]{:S(2)}) collective-permute-start(bf16[512,1024]{1,0:T(8,128)(2,1)} %get-tuple-element.441), channel_id=1, source_target_pairs={{0,4},{4,0},{8,12},{12,8},{16,20},{20,16},{24,28},{28,24},{1,5},{5... | collective-permute-start | bytes 3145736 | tf_op jit(solution)/shard_map/ppermute | solution.py:54
  552.6 43.9 %collective-permute-start.66 = (bf16[128,1024]{0,1:T(8,128)(2,1)}, bf16[128,1024]{0,1:T(8,128)(2,1)}, u32[]{:S(2)}, u32[]{:S(2)}) collective-permute-start(bf16[128,1024]{0,1:T(8,128)(2,1)} %add_convert_fusion.8), channel_id=1, source_target_pairs={{0,8},{4,12},{8,16},{12,20},{16,24},{20,28},{24,0},{28,4},{1,9},{5... | collective-permute-start | bytes 786440 | tf_op jit(solution)/shard_map/ppermute | solution.py:59
  555.9 40.6 %collective-permute-start.67 = (bf16[512,1024]{1,0:T(8,128)(2,1)}, bf16[512,1024]{1,0:T(8,128)(2,1)}, u32[]{:S(2)}, u32[]{:S(2)}) collective-permute-start(bf16[512,1024]{1,0:T(8,128)(2,1)} %add_convert_fusion.3), channel_id=1, source_target_pairs={{0,8},{4,12},{8,16},{12,20},{16,24},{20,28},{24,0},{28,4},{1,9},{5... | collective-permute-start | bytes 3145736 | tf_op jit(solution)/shard_map/ppermute | solution.py:59
  665.7 46.5 %collective-permute-start.77 = (bf16[1040,1024]{1,0:T(8,128)(2,1)}, bf16[1040,1024]{1,0:T(8,128)(2,1)}, u32[]{:S(2)}, u32[]{:S(2)}) collective-permute-start(bf16[1040,1024]{1,0:T(8,128)(2,1)} %fusion.13), channel_id=1, source_target_pairs={{0,4},{4,0},{8,12},{12,8},{16,20},{20,16},{24,28},{28,24},{1,5},{5... | collective-permute-start | bytes 6389768 | tf_op jit(solution)/shard_map/ppermute | solution.py:54
  670.0 42.2 %collective-permute-start.78 = (bf16[1040,1024]{1,0:T(8,128)(2,1)}, bf16[1040,1024]{1,0:T(8,128)(2,1)}, u32[]{:S(2)}, u32[]{:S(2)}) collective-permute-start(bf16[1040,1024]{1,0:T(8,128)(2,1)} %add_convert_fusion.2), channel_id=1, source_target_pairs={{0,8},{4,12},{8,16},{12,20},{16,24},{20,28},{24,0},{28,4},{1,9},{5... | collective-permute-start | bytes 6389768 | tf_op jit(solution)/shard_map/ppermute | solution.py:59
  712.2 46.4 %collective-permute-start.79 = (bf16[1040,1024]{1,0:T(8,128)(2,1)}, bf16[1040,1024]{1,0:T(8,128)(2,1)}, u32[]{:S(2)}, u32[]{:S(2)}) collective-permute-start(bf16[1040,1024]{1,0:T(8,128)(2,1)} %get-tuple-element.495), channel_id=1, source_target_pairs={{0,4},{4,0},{8,12},{12,8},{16,20},{20,16},{24,28},{28,24},{1,5},{5... | collective-permute-start | bytes 6389768 | tf_op jit(solution)/shard_map/ppermute | solution.py:54
  717.9 40.7 %collective-permute-start.80 = (bf16[1040,1024]{1,0:T(8,128)(2,1)}, bf16[1040,1024]{1,0:T(8,128)(2,1)}, u32[]{:S(2)}, u32[]{:S(2)}) collective-permute-start(bf16[1040,1024]{1,0:T(8,128)(2,1)} %add_convert_fusion.1), channel_id=1, source_target_pairs={{0,8},{4,12},{8,16},{12,20},{16,24},{20,28},{24,0},{28,4},{1,9},{5... | collective-permute-start | bytes 6389768 | tf_op jit(solution)/shard_map/ppermute | solution.py:59
  758.7 44.3 %collective-permute-start.81 = (bf16[1040,1024]{1,0:T(8,128)(2,1)}, bf16[1040,1024]{1,0:T(8,128)(2,1)}, u32[]{:S(2)}, u32[]{:S(2)}) collective-permute-start(bf16[1040,1024]{1,0:T(8,128)(2,1)} %get-tuple-element.503), channel_id=1, source_target_pairs={{0,4},{4,0},{8,12},{12,8},{16,20},{20,16},{24,28},{28,24},{1,5},{5... | collective-permute-start | bytes 6389768 | tf_op jit(solution)/shard_map/ppermute | solution.py:54
  (126 other events, 1950.1 us)

commit v5 on v4

--- a/solution.py
+++ b/solution.py
@@ -317,7 +317,7 @@
     order = list(range(1, rings)) + [0]
     pairs = near_terns(order[0])
     sending = [terns(order[0], 1, [cut[0] for cut in cutting])]
-    pairs, sending, limits, carried, ready = settle(pairs, sending, limits, carried, ready)
+    limits, carried = settle(limits, carried)
     aways, owns = {}, {}
     got = [[] for spot in spots]
     for hop in range(1, hops + 1):
@@ -502,9 +502,8 @@
         def fc_seven_most(carried, wholes, last):
             far = crossing["two"]
             two = join([{0: carried["out"][1]} | carried["own"][1] | far | over_near(far)])
-            early = matmul(two, wholes[2].reshape(-1, width))
             names = ("inputs", "noise", "pre")
-            return {name: carried[name] for name in names} | {"hidden_two": two, "early_two": early}, None
+            return {name: carried[name] for name in names} | {"hidden_two": two}, None
 
         hooks = {
             1: own_near,
@@ -539,7 +538,7 @@
 
         def sum_seven(number):
             if number == 1:
-                return carried["early_two"] + matmul(columns(1, start, most), rest)
+                return matmul(hiddens[1], kept_seven)
             whole_block = jnp.concatenate([rest, last["p"][count:]])
             return (
                 carried["early_one"]
@@ -552,8 +551,10 @@
     bias_wide = jnp.pad(bias_out, (0, padded - outs), constant_values=-1e30)
     share = half // ways
 
-    def half_forward(number):
+    def half_forward(number, earlier):
         pre, out = layer_forward(sum_seven(number), biases[1])
+        if earlier is not None:
+            pre, out, earlier = settle(pre, out, earlier)
         shares = out.reshape(ways, share, width)
         parts = {
             step: matmul(lax.dynamic_index_in_dim(shares, mine ^ step, 0, keepdims=False), kept_eight)
@@ -575,12 +576,16 @@
         dlogits = jnp.zeros((ways, share, padded), jnp.bfloat16)
         for step, item in xor_blocks(dz_part, bits).items():
             dlogits = put(dlogits, item, mine ^ step)
-        return pre, out, dlogits.reshape(half, padded), loss_part
-
-    both = [half_forward(number) for number in (0, 1)]
-    pre_seven, out_seven, dlogits = (
-        jnp.concatenate([item[spot] for item in both]) for spot in range(3)
-    )
+        return pre, out, dlogits.reshape(half, padded), loss_part, logits
+
+    both = [half_forward(0, None)]
+    both.append(half_forward(1, both[0][4]))
+    dlogits = jnp.concatenate([item[2] for item in both])
+    pre_seven, out_seven, _ = settle(
+        [item[0] for item in both], [item[1] for item in both], both[0][4][:8, :128]
+    )
+    pre_seven, out_seven = jnp.concatenate(pre_seven), jnp.concatenate(out_seven)
+    pre_seven, out_seven, dlogits = settle(pre_seven, out_seven, dlogits)
     loss_part = both[0][3] + both[1][3]
     hidden = jnp.concatenate(hiddens)
 

time: 870 us -> 856 us (0.984)
  waiting for transfers between devices: 349 us -> 363 us
  other arithmetic: 174 us -> 162 us
    ppermute x65, waiting for transfers between devices: 310 us -> 319 us  [swap(): return lax.ppermute(value, axis, [(i, i ^ bit) for i in range(size)])]
    convert_element_type x18 -> x16, other arithmetic: 74.4 us -> 65.9 us  [soft_ternary(): return value.astype(jnp.bfloat16)]
    dot_general x15 -> x14, matrix products: 51.7 us -> 50.1 us  [matmul(): return jnp.dot(left, right, preferred_element_type=jnp.float32)]
  transfers between devices with their start and end apart: 89 -> 89, of which waited for: 46 -> 47; matrix products, arithmetic and copies ran while one was open for 38% -> 38% of each run, Pallas kernels for 0% -> 0%
where the time goes in v5:
time: 856 us; the launch traced here: 846 us
  waiting for transfers between devices  363 us (42%)
  other arithmetic  162 us (19%)
  matrix products  128 us (15%)
  local copies, waits for them, and re-layouts  109 us (13%)
  starting transfers between devices  68.4 us (8%)
  between operations  16.1 us (2%)
    ppermute x65, waiting for transfers between devices, swap(): return lax.ppermute(value, axis, [(i, i ^ bit) for i in range(size)])  319 us
    convert_element_type x16, other arithmetic, soft_ternary(): return value.astype(jnp.bfloat16)  65.9 us
    dynamic_update_slice x44, local copies, waits for them, and re-layouts, put(): return lax.dynamic_update_slice(whole, piece[None], (index, row, 0))  55.7 us
    dot_general x3, matrix products, contract_rows(): lax.dot_general(left, right, (((0,), (0,)), ((), ())), preferred_element_...  51.4 us
    dot_general x14, matrix products, matmul(): return jnp.dot(left, right, preferred_element_type=jnp.float32)  50.1 us
    ppermute x65, starting transfers between devices, swap(): return lax.ppermute(value, axis, [(i, i ^ bit) for i in range(size)])  48.4 us
    ppermute x24, waiting for transfers between devices, turn(): return lax.ppermute(value, 'dp', [(i, (i + 2) % size) for i in range(size)])  43.7 us
    convert_element_type x11, other arithmetic, narrow(): return value.astype(jnp.bfloat16)  28.6 us
  transfers between devices with their start and end apart: 89, of which 47 were waited for; matrix products, arithmetic and copies ran while one was open for 38% of the time, Pallas kernels for 0%

profile of v5, /device:TPU:0, one launch (start us, length us, event | category | flops | bytes accessed | tf_op | source)
XLA Modules:
  0.0 845.6 jit_solution(16885051846928424933)
XLA Ops:
  28.2 8.7 %collective-permute-done = bf16[576,1024]{1,0:T(8,128)(2,1)} collective-permute-done((bf16[576,1024]{1,0:T(8,128)(2,1)}, bf16[576,1024]{1,0:T(8,128)(2,1)}, u32[]{:S(2)}, u32[]{:S(2)}) %collective-permute-start) | collective-permute-done | bytes 1179680 | tf_op jit(solution)/shard_map/ppermute | solution.py:54
  52.5 9.6 %collective-permute-done.5 = bf16[576,1024]{1,0:T(8,128)(2,1)} collective-permute-done((bf16[576,1024]{1,0:T(8,128)(2,1)S(1)}, bf16[576,1024]{1,0:T(8,128)(2,1)}, u32[]{:S(2)}, u32[]{:S(2)}) %collective-permute-start.5) | collective-permute-done | bytes 1179680 | tf_op jit(solution)/shard_map/ppermute | solution.py:54
  73.9 13.4 %collective-permute-done.3 = bf16[576,1024]{1,0:T(8,128)(2,1)} collective-permute-done((bf16[576,1024]{1,0:T(8,128)(2,1)}, bf16[576,1024]{1,0:T(8,128)(2,1)}, u32[]{:S(2)}, u32[]{:S(2)}) %collective-permute-start.3) | collective-permute-done | bytes 1179680 | tf_op jit(solution)/shard_map/ppermute | solution.py:54
  97.6 8.8 %collective-permute-done.11 = bf16[1024,2304]{1,0:T(8,128)(2,1)} collective-permute-done((bf16[1024,2304]{1,0:T(8,128)(2,1)}, bf16[1024,2304]{1,0:T(8,128)(2,1)}, u32[]{:S(2)}, u32[]{:S(2)}) %collective-permute-start.11) | collective-permute-done | bytes 4718624 | tf_op jit(solution)/shard_map/ppermute | solution.py:54
  122.6 22.1 %collective-permute-done.7 = bf16[576,1024]{1,0:T(8,128)(2,1)} collective-permute-done((bf16[576,1024]{1,0:T(8,128)(2,1)}, bf16[576,1024]{1,0:T(8,128)(2,1)}, u32[]{:S(2)}, u32[]{:S(2)}) %collective-permute-start.7) | collective-permute-done | bytes 1179680 | tf_op jit(solution)/shard_map/ppermute | solution.py:54
  148.6 9.8 %pad_maximum_fusion = bf16[1024,9216]{1,0:T(8,128)(2,1)S(1)} fusion(bf16[1024,2304]{1,0:T(8,128)(2,1)} %collective-permute-done.12, bf16[1024,2304]{1,0:T(8,128)(2,1)} %collective-permute-done.11, bf16[1024,2304]{1,0:T(8,128)(2,1)} %collective-permute-done.2, bf16[1024,2304]{1,0:T(8,128)(2,1)} %param.20), kind=kLoop, calls=%fused_computation.2 | loop fusion | flops 75497472 | bytes 37748736 | tf_op jit(solution)/shard_map/concatenate | solution.py:428
  165.6 15.6 %collective-permute-done.16 = bf16[256,1024]{1,0:T(8,128)(2,1)S(1)} collective-permute-done((bf16[256,1024]{1,0:T(8,128)(2,1)S(1)}, bf16[256,1024]{1,0:T(8,128)(2,1)S(1)}, u32[]{:S(2)}, u32[]{:S(2)}) %collective-permute-start.16) | collective-permute-done | bytes 524320 | tf_op jit(solution)/shard_map/ppermute | solution.py:54
  185.2 23.1 %fusion.117 = f32[1024,1024]{1,0:T(8,128)S(1)} fusion(bf16[1024,9216]{1,0:T(8,128)(2,1)S(1)} %pad_maximum_fusion, bf16[9216,1024]{1,0:T(8,128)(2,1)} %bitcast.20), kind=kOutput, calls=%fused_computation.289 | convolution fusion | flops 19327352832 | bytes 41943040 | tf_op jit(solution)/shard_map/dot_general | solution.py:20
  213.7 18.2 %collective-permute-done.20 = bf16[576,1024]{1,0:T(8,128)(2,1)} collective-permute-done((bf16[576,1024]{1,0:T(8,128)(2,1)S(1)}, bf16[576,1024]{1,0:T(8,128)(2,1)}, u32[]{:S(2)}, u32[]{:S(2)}) %collective-permute-start.20) | collective-permute-done | bytes 1179680 | tf_op jit(solution)/shard_map/ppermute | solution.py:54
  282.5 10.9 %collective-permute-done.28 = bf16[512,1024]{1,0:T(8,128)(2,1)S(1)} collective-permute-done((bf16[512,1024]{1,0:T(8,128)(2,1)S(1)}, bf16[512,1024]{1,0:T(8,128)(2,1)S(1)}, u32[]{:S(2)}, u32[]{:S(2)}) %collective-permute-start.28) | collective-permute-done | bytes 1048608 | tf_op jit(solution)/shard_map/ppermute | solution.py:54
  299.2 8.4 fusion.118
  348.6 9.5 %collective-permute-done.42 = f32[128,1024]{1,0:T(8,128)S(1)} collective-permute-done((f32[128,1024]{1,0:T(8,128)S(1)}, f32[128,1024]{1,0:T(8,128)S(1)}, u32[]{:S(2)}, u32[]{:S(2)}) %collective-permute-start.42) | collective-permute-done | bytes 524320 | tf_op jit(solution)/shard_map/ppermute | solution.py:54
  394.9 14.1 %abs_reduce_fusion.1 = (f32[]{:T(128)}, f32[]{:T(128)}, f32[4096,1024]{1,0:T(8,128)}) fusion(bf16[1024,1024]{1,0:T(8,128)(2,1)S(1)} %copy-done.22, bf16[512,4096]{1,0:T(8,128)(2,1)S(1)} %copy-done.13, bf16[512,4096]{1,0:T(8,128)(2,1)S(1)} %copy-done.36), kind=kOutput, calls=%fused_computation.3 | convolution fusion | flops 8623489024 | bytes 27262984 | tf_op jit(solution)/shard_map/dot_general | solution.py:24
  447.2 7.2 convolution_add_fusion
  454.4 13.3 %collective-permute-done.50 = bf16[128,1024]{0,1:T(8,128)(2,1)} collective-permute-done((bf16[128,1024]{0,1:T(8,128)(2,1)}, bf16[128,1024]{0,1:T(8,128)(2,1)}, u32[]{:S(2)}, u32[]{:S(2)}) %collective-permute-start.50) | collective-permute-done | bytes 262176 | tf_op jit(solution)/shard_map/ppermute | solution.py:54
  488.8 12.3 %collective-permute-done.54 = bf16[128,1024]{0,1:T(8,128)(2,1)} collective-permute-done((bf16[128,1024]{0,1:T(8,128)(2,1)}, bf16[128,1024]{0,1:T(8,128)(2,1)}, u32[]{:S(2)}, u32[]{:S(2)}) %collective-permute-start.54) | collective-permute-done | bytes 262176 | tf_op jit(solution)/shard_map/ppermute | solution.py:54
  520.3 15.6 %collective-permute-done.59 = bf16[128,1024]{0,1:T(8,128)(2,1)S(1)} collective-permute-done((bf16[128,1024]{0,1:T(8,128)(2,1)}, bf16[128,1024]{0,1:T(8,128)(2,1)S(1)}, u32[]{:S(2)}, u32[]{:S(2)}) %collective-permute-start.59) | collective-permute-done | bytes 262176 | tf_op jit(solution)/shard_map/ppermute | solution.py:54
  552.9 32.2 %abs_reduce_fusion = (f32[]{:T(128)}, f32[]{:T(128)}, f32[9216,1024]{1,0:T(8,128)}) fusion(bf16[1024,9216]{1,0:T(8,128)(2,1)} %copy-done.1, bf16[1024,1024]{1,0:T(8,128)(2,1)S(1)} %fusion.6), kind=kOutput, calls=%fused_computation | convolution fusion | flops 19365101568 | bytes 58720264 | tf_op jit(solution)/shard_map/dot_general | solution.py:24
  664.8 7.7 fusion.15
  672.6 32.4 %collective-permute-done.77 = bf16[1040,1024]{1,0:T(8,128)(2,1)} collective-permute-done((bf16[1040,1024]{1,0:T(8,128)(2,1)}, bf16[1040,1024]{1,0:T(8,128)(2,1)}, u32[]{:S(2)}, u32[]{:S(2)}) %collective-permute-start.77) | collective-permute-done | bytes 2129952 | tf_op jit(solution)/shard_map/ppermute | solution.py:54
  711.4 7.4 fusion.17
  718.8 32.6 %collective-permute-done.79 = bf16[1040,1024]{1,0:T(8,128)(2,1)} collective-permute-done((bf16[1040,1024]{1,0:T(8,128)(2,1)}, bf16[1040,1024]{1,0:T(8,128)(2,1)}, u32[]{:S(2)}, u32[]{:S(2)}) %collective-permute-start.79) | collective-permute-done | bytes 2129952 | tf_op jit(solution)/shard_map/ppermute | solution.py:54
  771.2 23.2 %collective-permute-done.83 = bf16[112,1024]{1,0:T(8,128)(2,1)S(1)} collective-permute-done((bf16[112,1024]{1,0:T(8,128)(2,1)}, bf16[112,1024]{1,0:T(8,128)(2,1)S(1)}, u32[]{:S(2)}, u32[]{:S(2)}) %collective-permute-start.83) | collective-permute-done | bytes 229408 | tf_op jit(solution)/shard_map/ppermute | solution.py:54
  823.6 12.8 %fusion.105 = (bf16[1152,1024]{1,0:T(8,128)(2,1)}, f32[1152,1024]{1,0:T(8,128)}, f32[1152,1024]{1,0:T(8,128)}, f32[1152,1024]{1,0:T(8,128)}) fusion(f32[1152,1024]{1,0:T(8,128)} %param.25, f32[112,1024]{1,0:T(8,128)S(1)} %convert_add_fusion.2, f32[1040,1024]{1,0:T(8,128)} %copy-done, f32[]{:T(128)} %bitcast.92, f32[]{:T(128)S(6)} %div.435, ...), kind=kLoop, calls=%fused_computation.278 | loop fusion | flops 21233664 | bytes 35389448 | tf_op jit(solution)/shard_map/convert_element_type | solution.py:722
  (461 shorter events, 460.7 us)
Async XLA Ops:
  1.2 105.3 %collective-permute-start.11 = (bf16[1024,2304]{1,0:T(8,128)(2,1)}, bf16[1024,2304]{1,0:T(8,128)(2,1)}, u32[]{:S(2)}, u32[]{:S(2)}) collective-permute-start(bf16[1024,2304]{1,0:T(8,128)(2,1)} %param.20), channel_id=1, source_target_pairs={{0,2},{1,3},{2,0},{3,1},{4,6},{5,7},{6,4},{7,5},{8,10},{9,11},{10,... | collective-permute-start | bytes 14155784 | tf_op jit(solution)/shard_map/ppermute | solution.py:54
  13.0 49.1 %collective-permute-start.5 = (bf16[576,1024]{1,0:T(8,128)(2,1)S(1)}, bf16[576,1024]{1,0:T(8,128)(2,1)}, u32[]{:S(2)}, u32[]{:S(2)}) collective-permute-start(bf16[576,1024]{1,0:T(8,128)(2,1)S(1)} %get-tuple-element.273), channel_id=1, source_target_pairs={{0,4},{4,0},{8,12},{12,8},{16,20},{20,16},{24,28},{28,24},{1,5},{5... | collective-permute-start | bytes 3538952 | tf_op jit(solution)/shard_map/ppermute | solution.py:54
  39.2 48.2 %collective-permute-start.3 = (bf16[576,1024]{1,0:T(8,128)(2,1)}, bf16[576,1024]{1,0:T(8,128)(2,1)}, u32[]{:S(2)}, u32[]{:S(2)}) collective-permute-start(bf16[576,1024]{1,0:T(8,128)(2,1)} %collective-permute-done.1), channel_id=1, source_target_pairs={{0,4},{4,0},{8,12},{12,8},{16,20},{20,16},{24,28},{28,24},{1,5},{5... | collective-permute-start | bytes 3538952 | tf_op jit(solution)/shard_map/ppermute | solution.py:54
  39.9 53.0 %collective-permute-start.4 = (bf16[576,1024]{1,0:T(8,128)(2,1)}, bf16[576,1024]{1,0:T(8,128)(2,1)}, u32[]{:S(2)}, u32[]{:S(2)}) collective-permute-start(bf16[576,1024]{1,0:T(8,128)(2,1)} %collective-permute-done.1), channel_id=1, source_target_pairs={{0,8},{4,12},{8,16},{12,20},{16,24},{20,28},{24,0},{28,4},{1,9},{5... | collective-permute-start | bytes 3538952 | tf_op jit(solution)/shard_map/ppermute | solution.py:59
  67.6 44.3 %collective-permute-start.9 = (bf16[576,1024]{1,0:T(8,128)(2,1)}, bf16[576,1024]{1,0:T(8,128)(2,1)}, u32[]{:S(2)}, u32[]{:S(2)}) collective-permute-start(bf16[576,1024]{1,0:T(8,128)(2,1)} %collective-permute-done.6), channel_id=1, source_target_pairs={{0,4},{4,0},{8,12},{12,8},{16,20},{20,16},{24,28},{28,24},{1,5},{5... | collective-permute-start | bytes 3538952 | tf_op jit(solution)/shard_map/ppermute | solution.py:54
  69.1 46.5 %collective-permute-start.10 = (bf16[576,1024]{1,0:T(8,128)(2,1)}, bf16[576,1024]{1,0:T(8,128)(2,1)S(1)}, u32[]{:S(2)}, u32[]{:S(2)}) collective-permute-start(bf16[576,1024]{1,0:T(8,128)(2,1)} %collective-permute-done.6), channel_id=1, source_target_pairs={{0,8},{4,12},{8,16},{12,20},{16,24},{20,28},{24,0},{28,4},{1,9},{5... | collective-permute-start | bytes 3538952 | tf_op jit(solution)/shard_map/ppermute | solution.py:59
  117.2 63.9 %collective-permute-start.15 = (bf16[576,1024]{1,0:T(8,128)(2,1)S(1)}, bf16[576,1024]{1,0:T(8,128)(2,1)S(1)}, u32[]{:S(2)}, u32[]{:S(2)}) collective-permute-start(bf16[576,1024]{1,0:T(8,128)(2,1)S(1)} %collective-permute-done.10), channel_id=1, source_target_pairs={{0,4},{4,0},{8,12},{12,8},{16,20},{20,16},{24,28},{28,24},{1,5},{5... | collective-permute-start | bytes 3538952 | tf_op jit(solution)/shard_map/ppermute | solution.py:54
  117.8 63.4 %collective-permute-start.17 = (bf16[576,1024]{1,0:T(8,128)(2,1)S(1)}, bf16[576,1024]{1,0:T(8,128)(2,1)S(1)}, u32[]{:S(2)}, u32[]{:S(2)}) collective-permute-start(bf16[576,1024]{1,0:T(8,128)(2,1)S(1)} %collective-permute-done.10), channel_id=1, source_target_pairs={{0,8},{4,12},{8,16},{12,20},{16,24},{20,28},{24,0},{28,4},{1,9},{5... | collective-permute-start | bytes 3538952 | tf_op jit(solution)/shard_map/ppermute | solution.py:59
  148.1 61.0 %collective-permute-start.13 = (bf16[576,1024]{1,0:T(8,128)(2,1)}, bf16[576,1024]{1,0:T(8,128)(2,1)}, u32[]{:S(2)}, u32[]{:S(2)}) collective-permute-start(bf16[576,1024]{1,0:T(8,128)(2,1)} %collective-permute-done.8), channel_id=1, source_target_pairs={{0,4},{4,0},{8,12},{12,8},{16,20},{20,16},{24,28},{28,24},{1,5},{5... | collective-permute-start | bytes 3538952 | tf_op jit(solution)/shard_map/ppermute | solution.py:54
  148.6 60.5 %collective-permute-start.14 = (bf16[384,1024]{1,0:T(8,128)(2,1)S(1)}, bf16[384,1024]{1,0:T(8,128)(2,1)}, u32[]{:S(2)}, u32[]{:S(2)}) collective-permute-start(bf16[384,1024]{1,0:T(8,128)(2,1)S(1)} %copy-done.16), channel_id=1, source_target_pairs={{0,8},{4,12},{8,16},{12,20},{16,24},{20,28},{24,0},{28,4},{1,9},{5... | collective-permute-start | bytes 2359304 | tf_op jit(solution)/shard_map/ppermute | solution.py:59
  181.2 50.6 %collective-permute-start.20 = (bf16[576,1024]{1,0:T(8,128)(2,1)S(1)}, bf16[576,1024]{1,0:T(8,128)(2,1)}, u32[]{:S(2)}, u32[]{:S(2)}) collective-permute-start(bf16[576,1024]{1,0:T(8,128)(2,1)S(1)} %collective-permute-done.17), channel_id=1, source_target_pairs={{0,4},{4,0},{8,12},{12,8},{16,20},{20,16},{24,28},{28,24},{1,5},{5... | collective-permute-start | bytes 3538952 | tf_op jit(solution)/shard_map/ppermute | solution.py:54
  209.1 41.7 %collective-permute-start.18 = (bf16[384,1024]{1,0:T(8,128)(2,1)S(1)}, bf16[384,1024]{1,0:T(8,128)(2,1)}, u32[]{:S(2)}, u32[]{:S(2)}) collective-permute-start(bf16[384,1024]{1,0:T(8,128)(2,1)S(1)} %copy-done.16), channel_id=1, source_target_pairs={{0,4},{4,0},{8,12},{12,8},{16,20},{20,16},{24,28},{28,24},{1,5},{5... | collective-permute-start | bytes 2359304 | tf_op jit(solution)/shard_map/ppermute | solution.py:54
  209.6 41.3 %collective-permute-start.19 = (bf16[384,1024]{1,0:T(8,128)(2,1)}, bf16[384,1024]{1,0:T(8,128)(2,1)S(1)}, u32[]{:S(2)}, u32[]{:S(2)}) collective-permute-start(bf16[384,1024]{1,0:T(8,128)(2,1)} %collective-permute-done.14), channel_id=1, source_target_pairs={{0,8},{4,12},{8,16},{12,20},{16,24},{20,28},{24,0},{28,4},{1,9},{5... | collective-permute-start | bytes 2359304 | tf_op jit(solution)/shard_map/ppermute | solution.py:59
  274.2 40.3 %collective-permute-start.32 = (bf16[512,1024]{1,0:T(8,128)(2,1)}, bf16[512,1024]{1,0:T(8,128)(2,1)S(1)}, u32[]{:S(2)}, u32[]{:S(2)}) collective-permute-start(bf16[512,1024]{1,0:T(8,128)(2,1)} %collective-permute-done.31), channel_id=1, source_target_pairs={{0,1},{1,0},{2,3},{3,2},{4,5},{5,4},{6,7},{7,6},{8,9},{9,8},{10,11... | collective-permute-start | bytes 3145736 | tf_op jit(solution)/shard_map/ppermute | solution.py:54
  274.3 38.6 %collective-permute-start.30 = (bf16[512,1024]{1,0:T(8,128)(2,1)}, bf16[512,1024]{1,0:T(8,128)(2,1)S(1)}, u32[]{:S(2)}, u32[]{:S(2)}) collective-permute-start(bf16[512,1024]{1,0:T(8,128)(2,1)} %collective-permute-done.25), channel_id=1, source_target_pairs={{0,8},{4,12},{8,16},{12,20},{16,24},{20,28},{24,0},{28,4},{1,9},{5... | collective-permute-start | bytes 3145736 | tf_op jit(solution)/shard_map/ppermute | solution.py:59
  542.5 46.7 %collective-permute-start.64 = (bf16[128,1024]{0,1:T(8,128)(2,1)S(1)}, bf16[128,1024]{0,1:T(8,128)(2,1)}, u32[]{:S(2)}, u32[]{:S(2)}) collective-permute-start(bf16[128,1024]{0,1:T(8,128)(2,1)S(1)} %bitcast.332), channel_id=1, source_target_pairs={{0,4},{4,0},{8,12},{12,8},{16,20},{20,16},{24,28},{28,24},{1,5},{5... | collective-permute-start | bytes 786440 | tf_op jit(solution)/shard_map/ppermute | solution.py:54
  544.1 45.1 %collective-permute-start.65 = (bf16[512,1024]{1,0:T(8,128)(2,1)S(1)}, bf16[512,1024]{1,0:T(8,128)(2,1)}, u32[]{:S(2)}, u32[]{:S(2)}) collective-permute-start(bf16[512,1024]{1,0:T(8,128)(2,1)S(1)} %get-tuple-element.449), channel_id=1, source_target_pairs={{0,4},{4,0},{8,12},{12,8},{16,20},{20,16},{24,28},{28,24},{1,5},{5... | collective-permute-start | bytes 3145736 | tf_op jit(solution)/shard_map/ppermute | solution.py:54
  545.4 43.8 %collective-permute-start.66 = (bf16[128,1024]{0,1:T(8,128)(2,1)}, bf16[128,1024]{0,1:T(8,128)(2,1)}, u32[]{:S(2)}, u32[]{:S(2)}) collective-permute-start(bf16[128,1024]{0,1:T(8,128)(2,1)} %add_convert_fusion.8), channel_id=1, source_target_pairs={{0,8},{4,12},{8,16},{12,20},{16,24},{20,28},{24,0},{28,4},{1,9},{5... | collective-permute-start | bytes 786440 | tf_op jit(solution)/shard_map/ppermute | solution.py:59
  548.7 40.5 %collective-permute-start.67 = (bf16[512,1024]{1,0:T(8,128)(2,1)}, bf16[512,1024]{1,0:T(8,128)(2,1)}, u32[]{:S(2)}, u32[]{:S(2)}) collective-permute-start(bf16[512,1024]{1,0:T(8,128)(2,1)} %add_convert_fusion.3), channel_id=1, source_target_pairs={{0,8},{4,12},{8,16},{12,20},{16,24},{20,28},{24,0},{28,4},{1,9},{5... | collective-permute-start | bytes 3145736 | tf_op jit(solution)/shard_map/ppermute | solution.py:59
  658.5 46.5 %collective-permute-start.77 = (bf16[1040,1024]{1,0:T(8,128)(2,1)}, bf16[1040,1024]{1,0:T(8,128)(2,1)}, u32[]{:S(2)}, u32[]{:S(2)}) collective-permute-start(bf16[1040,1024]{1,0:T(8,128)(2,1)} %fusion.13), channel_id=1, source_target_pairs={{0,4},{4,0},{8,12},{12,8},{16,20},{20,16},{24,28},{28,24},{1,5},{5... | collective-permute-start | bytes 6389768 | tf_op jit(solution)/shard_map/ppermute | solution.py:54
  662.0 43.0 %collective-permute-start.78 = (bf16[1040,1024]{1,0:T(8,128)(2,1)}, bf16[1040,1024]{1,0:T(8,128)(2,1)}, u32[]{:S(2)}, u32[]{:S(2)}) collective-permute-start(bf16[1040,1024]{1,0:T(8,128)(2,1)} %add_convert_fusion.2), channel_id=1, source_target_pairs={{0,8},{4,12},{8,16},{12,20},{16,24},{20,28},{24,0},{28,4},{1,9},{5... | collective-permute-start | bytes 6389768 | tf_op jit(solution)/shard_map/ppermute | solution.py:59
  705.0 46.4 %collective-permute-start.79 = (bf16[1040,1024]{1,0:T(8,128)(2,1)}, bf16[1040,1024]{1,0:T(8,128)(2,1)}, u32[]{:S(2)}, u32[]{:S(2)}) collective-permute-start(bf16[1040,1024]{1,0:T(8,128)(2,1)} %get-tuple-element.501), channel_id=1, source_target_pairs={{0,4},{4,0},{8,12},{12,8},{16,20},{20,16},{24,28},{28,24},{1,5},{5... | collective-permute-start | bytes 6389768 | tf_op jit(solution)/shard_map/ppermute | solution.py:54
  710.1 41.3 %collective-permute-start.80 = (bf16[1040,1024]{1,0:T(8,128)(2,1)}, bf16[1040,1024]{1,0:T(8,128)(2,1)}, u32[]{:S(2)}, u32[]{:S(2)}) collective-permute-start(bf16[1040,1024]{1,0:T(8,128)(2,1)} %add_convert_fusion.1), channel_id=1, source_target_pairs={{0,8},{4,12},{8,16},{12,20},{16,24},{20,28},{24,0},{28,4},{1,9},{5... | collective-permute-start | bytes 6389768 | tf_op jit(solution)/shard_map/ppermute | solution.py:59
  751.4 42.9 %collective-permute-start.81 = (bf16[1040,1024]{1,0:T(8,128)(2,1)}, bf16[1040,1024]{1,0:T(8,128)(2,1)}, u32[]{:S(2)}, u32[]{:S(2)}) collective-permute-start(bf16[1040,1024]{1,0:T(8,128)(2,1)} %get-tuple-element.509), channel_id=1, source_target_pairs={{0,4},{4,0},{8,12},{12,8},{16,20},{20,16},{24,28},{28,24},{1,5},{5... | collective-permute-start | bytes 6389768 | tf_op jit(solution)/shard_map/ppermute | solution.py:54
  (124 other events, 1979.9 us)

commit v6 on v5

--- a/solution.py
+++ b/solution.py
@@ -595,7 +595,7 @@
         return against_rows(delta, kept_seven[step * width : (step + 1) * width])
 
     top_bit = bits[0]
-    cuts = [0, batch_rows // 64 * 22, batch_rows // 64 * 43, batch_rows]
+    cuts = [0] + [batch_rows // 64 * mark for mark in (8, 27, 46)] + [batch_rows]
 
     def near_sums(first, delta):
         ups = {step: upstream(delta, step) for step in range(first, first + top_bit)}
@@ -611,11 +611,12 @@
         crossing, grad_eight, limit_eight, peak_eight, delta_seven, dlogits
     )
     crossing = [crossing[low:high] for low, high in zip(cuts[:-1], cuts[1:])]
+    crossed = [swap(crossing[0], "mp", top_bit)]
     grad_seven = contract_rows(hidden, delta_seven)
     limit_seven, peak_seven = grad_limits(grad_seven, width)
     tops = fold(jnp.stack([peak_eight, peak_seven]), jnp.maximum, ("dp",))
-    crossing, grad_seven, limit_seven, tops, delta_seven = settle(
-        crossing, grad_seven, limit_seven, tops, delta_seven
+    crossing, crossed, grad_seven, limit_seven, tops, delta_seven = settle(
+        crossing, crossed, grad_seven, limit_seven, tops, delta_seven
     )
     top_eight, top_seven = tops[0], tops[1]
 
@@ -624,7 +625,7 @@
             delta, crossing, crossed, own_up = carried
             if step == 0:
                 own_up = near_sums(0, delta)
-            return (delta, crossing, crossed + [swap(crossing[step], "mp", top_bit)], own_up)
+            return (delta, crossing, crossed + [swap(crossing[step + 1], "mp", top_bit)], own_up)
 
         return work
 
@@ -661,7 +662,7 @@
         [0, 0],
         False,
         beside,
-        (delta_seven, crossing, [], None),
+        (delta_seven, crossing, crossed, None),
     )
     grad_six, limit_six, small = small_sums(carried)
     top_six = small[-1]

time: 856 us -> 850 us (level)
  waiting for transfers between devices: 363 us -> 346 us
  starting transfers between devices: 68.4 us -> 82.1 us
    ppermute x65 -> x66, waiting for transfers between devices: 319 us -> 303 us  [swap(): return lax.ppermute(value, axis, [(i, i ^ bit) for i in range(size)])]
    ppermute x65 -> x66, starting transfers between devices: 48.4 us -> 59.7 us  [swap(): return lax.ppermute(value, axis, [(i, i ^ bit) for i in range(size)])]
  transfers between devices with their start and end apart: 89 -> 90, of which waited for: 47 -> 48; matrix products, arithmetic and copies ran while one was open for 38% -> 40% of each run, Pallas kernels for 0% -> 0%
where the time goes in v6:
time: 850 us; the launch traced here: 840 us
  waiting for transfers between devices  346 us (41%)
  other arithmetic  162 us (19%)
  matrix products  128 us (15%)
  local copies, waits for them, and re-layouts  106 us (12%)
  starting transfers between devices  82.1 us (10%)
  between operations  15.8 us (2%)
    ppermute x66, waiting for transfers between devices, swap(): return lax.ppermute(value, axis, [(i, i ^ bit) for i in range(size)])  303 us
    convert_element_type x16, other arithmetic, soft_ternary(): return value.astype(jnp.bfloat16)  65.9 us
    ppermute x66, starting transfers between devices, swap(): return lax.ppermute(value, axis, [(i, i ^ bit) for i in range(size)])  59.7 us
    dynamic_update_slice x44, local copies, waits for them, and re-layouts, put(): return lax.dynamic_update_slice(whole, piece[None], (index, row, 0))  55.8 us
    dot_general x3, matrix products, contract_rows(): lax.dot_general(left, right, (((0,), (0,)), ((), ())), preferred_element_...  51.5 us
    dot_general x14, matrix products, matmul(): return jnp.dot(left, right, preferred_element_type=jnp.float32)  50.1 us
    ppermute x24, waiting for transfers between devices, turn(): return lax.ppermute(value, 'dp', [(i, (i + 2) % size) for i in range(size)])  43.1 us
    convert_element_type x11, other arithmetic, narrow(): return value.astype(jnp.bfloat16)  28.6 us
  transfers between devices with their start and end apart: 90, of which 48 were waited for; matrix products, arithmetic and copies ran while one was open for 40% of the time, Pallas kernels for 0%

profile of v6, /device:TPU:0, one launch (start us, length us, event | category | flops | bytes accessed | tf_op | source)
XLA Modules:
  0.0 840.3 jit_solution(7337298655880150444)
XLA Ops:
  28.2 8.6 %collective-permute-done = bf16[576,1024]{1,0:T(8,128)(2,1)} collective-permute-done((bf16[576,1024]{1,0:T(8,128)(2,1)}, bf16[576,1024]{1,0:T(8,128)(2,1)}, u32[]{:S(2)}, u32[]{:S(2)}) %collective-permute-start) | collective-permute-done | bytes 1179680 | tf_op jit(solution)/shard_map/ppermute | solution.py:54
  52.6 9.5 %collective-permute-done.5 = bf16[576,1024]{1,0:T(8,128)(2,1)} collective-permute-done((bf16[576,1024]{1,0:T(8,128)(2,1)S(1)}, bf16[576,1024]{1,0:T(8,128)(2,1)}, u32[]{:S(2)}, u32[]{:S(2)}) %collective-permute-start.5) | collective-permute-done | bytes 1179680 | tf_op jit(solution)/shard_map/ppermute | solution.py:54
  73.9 13.5 %collective-permute-done.3 = bf16[576,1024]{1,0:T(8,128)(2,1)} collective-permute-done((bf16[576,1024]{1,0:T(8,128)(2,1)}, bf16[576,1024]{1,0:T(8,128)(2,1)}, u32[]{:S(2)}, u32[]{:S(2)}) %collective-permute-start.3) | collective-permute-done | bytes 1179680 | tf_op jit(solution)/shard_map/ppermute | solution.py:54
  97.7 8.8 %collective-permute-done.11 = bf16[1024,2304]{1,0:T(8,128)(2,1)} collective-permute-done((bf16[1024,2304]{1,0:T(8,128)(2,1)}, bf16[1024,2304]{1,0:T(8,128)(2,1)}, u32[]{:S(2)}, u32[]{:S(2)}) %collective-permute-start.11) | collective-permute-done | bytes 4718624 | tf_op jit(solution)/shard_map/ppermute | solution.py:54
  122.6 22.1 %collective-permute-done.7 = bf16[576,1024]{1,0:T(8,128)(2,1)} collective-permute-done((bf16[576,1024]{1,0:T(8,128)(2,1)}, bf16[576,1024]{1,0:T(8,128)(2,1)}, u32[]{:S(2)}, u32[]{:S(2)}) %collective-permute-start.7) | collective-permute-done | bytes 1179680 | tf_op jit(solution)/shard_map/ppermute | solution.py:54
  148.6 9.8 %pad_maximum_fusion = bf16[1024,9216]{1,0:T(8,128)(2,1)S(1)} fusion(bf16[1024,2304]{1,0:T(8,128)(2,1)} %collective-permute-done.12, bf16[1024,2304]{1,0:T(8,128)(2,1)} %collective-permute-done.11, bf16[1024,2304]{1,0:T(8,128)(2,1)} %collective-permute-done.2, bf16[1024,2304]{1,0:T(8,128)(2,1)} %param.20), kind=kLoop, calls=%fused_computation.2 | loop fusion | flops 75497472 | bytes 37748736 | tf_op jit(solution)/shard_map/concatenate | solution.py:428
  165.5 15.6 %collective-permute-done.16 = bf16[256,1024]{1,0:T(8,128)(2,1)S(1)} collective-permute-done((bf16[256,1024]{1,0:T(8,128)(2,1)S(1)}, bf16[256,1024]{1,0:T(8,128)(2,1)S(1)}, u32[]{:S(2)}, u32[]{:S(2)}) %collective-permute-start.16) | collective-permute-done | bytes 524320 | tf_op jit(solution)/shard_map/ppermute | solution.py:54
  185.2 23.1 %fusion.117 = f32[1024,1024]{1,0:T(8,128)S(1)} fusion(bf16[1024,9216]{1,0:T(8,128)(2,1)S(1)} %pad_maximum_fusion, bf16[9216,1024]{1,0:T(8,128)(2,1)} %bitcast.20), kind=kOutput, calls=%fused_computation.289 | convolution fusion | flops 19327352832 | bytes 41943040 | tf_op jit(solution)/shard_map/dot_general | solution.py:20
  213.7 18.1 %collective-permute-done.20 = bf16[576,1024]{1,0:T(8,128)(2,1)} collective-permute-done((bf16[576,1024]{1,0:T(8,128)(2,1)S(1)}, bf16[576,1024]{1,0:T(8,128)(2,1)}, u32[]{:S(2)}, u32[]{:S(2)}) %collective-permute-start.20) | collective-permute-done | bytes 1179680 | tf_op jit(solution)/shard_map/ppermute | solution.py:54
  282.8 10.8 %collective-permute-done.28 = bf16[512,1024]{1,0:T(8,128)(2,1)S(1)} collective-permute-done((bf16[512,1024]{1,0:T(8,128)(2,1)S(1)}, bf16[512,1024]{1,0:T(8,128)(2,1)S(1)}, u32[]{:S(2)}, u32[]{:S(2)}) %collective-permute-start.28) | collective-permute-done | bytes 1048608 | tf_op jit(solution)/shard_map/ppermute | solution.py:54
  299.5 8.4 fusion.118
  348.5 9.8 %collective-permute-done.42 = f32[128,1024]{1,0:T(8,128)S(1)} collective-permute-done((f32[128,1024]{1,0:T(8,128)S(1)}, f32[128,1024]{1,0:T(8,128)S(1)}, u32[]{:S(2)}, u32[]{:S(2)}) %collective-permute-start.42) | collective-permute-done | bytes 524320 | tf_op jit(solution)/shard_map/ppermute | solution.py:54
  393.7 14.2 %abs_reduce_fusion.1 = (f32[]{:T(128)}, f32[]{:T(128)}, f32[4096,1024]{1,0:T(8,128)}) fusion(bf16[1024,1024]{1,0:T(8,128)(2,1)S(1)} %copy-done.22, bf16[512,4096]{1,0:T(8,128)(2,1)S(1)} %copy-done.13, bf16[512,4096]{1,0:T(8,128)(2,1)S(1)} %copy-done.36), kind=kOutput, calls=%fused_computation.3 | convolution fusion | flops 8623489024 | bytes 27262984 | tf_op jit(solution)/shard_map/dot_general | solution.py:24
  446.9 7.2 convolution_add_fusion
  454.1 12.6 %collective-permute-done.51 = bf16[128,1024]{0,1:T(8,128)(2,1)} collective-permute-done((bf16[128,1024]{0,1:T(8,128)(2,1)}, bf16[128,1024]{0,1:T(8,128)(2,1)}, u32[]{:S(2)}, u32[]{:S(2)}) %collective-permute-start.51) | collective-permute-done | bytes 262176 | tf_op jit(solution)/shard_map/ppermute | solution.py:54
  485.7 11.7 %collective-permute-done.55 = bf16[128,1024]{0,1:T(8,128)(2,1)} collective-permute-done((bf16[128,1024]{0,1:T(8,128)(2,1)}, bf16[128,1024]{0,1:T(8,128)(2,1)}, u32[]{:S(2)}, u32[]{:S(2)}) %collective-permute-start.55) | collective-permute-done | bytes 262176 | tf_op jit(solution)/shard_map/ppermute | solution.py:54
  515.9 16.6 %collective-permute-done.60 = bf16[128,1024]{0,1:T(8,128)(2,1)S(1)} collective-permute-done((bf16[128,1024]{0,1:T(8,128)(2,1)}, bf16[128,1024]{0,1:T(8,128)(2,1)S(1)}, u32[]{:S(2)}, u32[]{:S(2)}) %collective-permute-start.60) | collective-permute-done | bytes 262176 | tf_op jit(solution)/shard_map/ppermute | solution.py:54
  549.4 32.2 %abs_reduce_fusion = (f32[]{:T(128)}, f32[]{:T(128)}, f32[9216,1024]{1,0:T(8,128)}) fusion(bf16[1024,9216]{1,0:T(8,128)(2,1)} %copy-done.1, bf16[1024,1024]{1,0:T(8,128)(2,1)S(1)} %fusion.6), kind=kOutput, calls=%fused_computation | convolution fusion | flops 19365101568 | bytes 58720264 | tf_op jit(solution)/shard_map/dot_general | solution.py:24
  661.0 7.7 fusion.15
  668.7 29.7 %collective-permute-done.78 = bf16[1040,1024]{1,0:T(8,128)(2,1)} collective-permute-done((bf16[1040,1024]{1,0:T(8,128)(2,1)}, bf16[1040,1024]{1,0:T(8,128)(2,1)}, u32[]{:S(2)}, u32[]{:S(2)}) %collective-permute-start.78) | collective-permute-done | bytes 2129952 | tf_op jit(solution)/shard_map/ppermute | solution.py:54
  707.4 7.4 fusion.17
  714.8 30.0 %collective-permute-done.80 = bf16[1040,1024]{1,0:T(8,128)(2,1)} collective-permute-done((bf16[1040,1024]{1,0:T(8,128)(2,1)}, bf16[1040,1024]{1,0:T(8,128)(2,1)}, u32[]{:S(2)}, u32[]{:S(2)}) %collective-permute-start.80) | collective-permute-done | bytes 2129952 | tf_op jit(solution)/shard_map/ppermute | solution.py:54
  765.5 23.8 %collective-permute-done.84 = bf16[112,1024]{1,0:T(8,128)(2,1)S(1)} collective-permute-done((bf16[112,1024]{1,0:T(8,128)(2,1)}, bf16[112,1024]{1,0:T(8,128)(2,1)S(1)}, u32[]{:S(2)}, u32[]{:S(2)}) %collective-permute-start.84) | collective-permute-done | bytes 229408 | tf_op jit(solution)/shard_map/ppermute | solution.py:54
  818.5 12.8 %fusion.105 = (bf16[1152,1024]{1,0:T(8,128)(2,1)}, f32[1152,1024]{1,0:T(8,128)}, f32[1152,1024]{1,0:T(8,128)}, f32[1152,1024]{1,0:T(8,128)}) fusion(f32[1152,1024]{1,0:T(8,128)} %param.25, f32[112,1024]{1,0:T(8,128)S(1)} %convert_add_fusion.2, f32[1040,1024]{1,0:T(8,128)} %copy-done, f32[]{:T(128)} %bitcast.92, f32[]{:T(128)S(6)} %div.435, ...), kind=kLoop, calls=%fused_computation.278 | loop fusion | flops 21233664 | bytes 35389448 | tf_op jit(solution)/shard_map/convert_element_type | solution.py:723
  (468 shorter events, 460.4 us)
Async XLA Ops:
  1.2 105.3 %collective-permute-start.11 = (bf16[1024,2304]{1,0:T(8,128)(2,1)}, bf16[1024,2304]{1,0:T(8,128)(2,1)}, u32[]{:S(2)}, u32[]{:S(2)}) collective-permute-start(bf16[1024,2304]{1,0:T(8,128)(2,1)} %param.20), channel_id=1, source_target_pairs={{0,2},{1,3},{2,0},{3,1},{4,6},{5,7},{6,4},{7,5},{8,10},{9,11},{10,... | collective-permute-start | bytes 14155784 | tf_op jit(solution)/shard_map/ppermute | solution.py:54
  13.0 49.1 %collective-permute-start.5 = (bf16[576,1024]{1,0:T(8,128)(2,1)S(1)}, bf16[576,1024]{1,0:T(8,128)(2,1)}, u32[]{:S(2)}, u32[]{:S(2)}) collective-permute-start(bf16[576,1024]{1,0:T(8,128)(2,1)S(1)} %get-tuple-element.278), channel_id=1, source_target_pairs={{0,4},{4,0},{8,12},{12,8},{16,20},{20,16},{24,28},{28,24},{1,5},{5... | collective-permute-start | bytes 3538952 | tf_op jit(solution)/shard_map/ppermute | solution.py:54
  39.2 48.2 %collective-permute-start.3 = (bf16[576,1024]{1,0:T(8,128)(2,1)}, bf16[576,1024]{1,0:T(8,128)(2,1)}, u32[]{:S(2)}, u32[]{:S(2)}) collective-permute-start(bf16[576,1024]{1,0:T(8,128)(2,1)} %collective-permute-done.1), channel_id=1, source_target_pairs={{0,4},{4,0},{8,12},{12,8},{16,20},{20,16},{24,28},{28,24},{1,5},{5... | collective-permute-start | bytes 3538952 | tf_op jit(solution)/shard_map/ppermute | solution.py:54
  39.9 53.0 %collective-permute-start.4 = (bf16[576,1024]{1,0:T(8,128)(2,1)}, bf16[576,1024]{1,0:T(8,128)(2,1)}, u32[]{:S(2)}, u32[]{:S(2)}) collective-permute-start(bf16[576,1024]{1,0:T(8,128)(2,1)} %collective-permute-done.1), channel_id=1, source_target_pairs={{0,8},{4,12},{8,16},{12,20},{16,24},{20,28},{24,0},{28,4},{1,9},{5... | collective-permute-start | bytes 3538952 | tf_op jit(solution)/shard_map/ppermute | solution.py:59
  67.6 44.3 %collective-permute-start.9 = (bf16[576,1024]{1,0:T(8,128)(2,1)}, bf16[576,1024]{1,0:T(8,128)(2,1)}, u32[]{:S(2)}, u32[]{:S(2)}) collective-permute-start(bf16[576,1024]{1,0:T(8,128)(2,1)} %collective-permute-done.6), channel_id=1, source_target_pairs={{0,4},{4,0},{8,12},{12,8},{16,20},{20,16},{24,28},{28,24},{1,5},{5... | collective-permute-start | bytes 3538952 | tf_op jit(solution)/shard_map/ppermute | solution.py:54
  69.1 46.5 %collective-permute-start.10 = (bf16[576,1024]{1,0:T(8,128)(2,1)}, bf16[576,1024]{1,0:T(8,128)(2,1)S(1)}, u32[]{:S(2)}, u32[]{:S(2)}) collective-permute-start(bf16[576,1024]{1,0:T(8,128)(2,1)} %collective-permute-done.6), channel_id=1, source_target_pairs={{0,8},{4,12},{8,16},{12,20},{16,24},{20,28},{24,0},{28,4},{1,9},{5... | collective-permute-start | bytes 3538952 | tf_op jit(solution)/shard_map/ppermute | solution.py:59
  117.2 63.9 %collective-permute-start.15 = (bf16[576,1024]{1,0:T(8,128)(2,1)S(1)}, bf16[576,1024]{1,0:T(8,128)(2,1)S(1)}, u32[]{:S(2)}, u32[]{:S(2)}) collective-permute-start(bf16[576,1024]{1,0:T(8,128)(2,1)S(1)} %collective-permute-done.10), channel_id=1, source_target_pairs={{0,4},{4,0},{8,12},{12,8},{16,20},{20,16},{24,28},{28,24},{1,5},{5... | collective-permute-start | bytes 3538952 | tf_op jit(solution)/shard_map/ppermute | solution.py:54
  117.8 63.4 %collective-permute-start.17 = (bf16[576,1024]{1,0:T(8,128)(2,1)S(1)}, bf16[576,1024]{1,0:T(8,128)(2,1)S(1)}, u32[]{:S(2)}, u32[]{:S(2)}) collective-permute-start(bf16[576,1024]{1,0:T(8,128)(2,1)S(1)} %collective-permute-done.10), channel_id=1, source_target_pairs={{0,8},{4,12},{8,16},{12,20},{16,24},{20,28},{24,0},{28,4},{1,9},{5... | collective-permute-start | bytes 3538952 | tf_op jit(solution)/shard_map/ppermute | solution.py:59
  148.1 61.0 %collective-permute-start.13 = (bf16[576,1024]{1,0:T(8,128)(2,1)}, bf16[576,1024]{1,0:T(8,128)(2,1)}, u32[]{:S(2)}, u32[]{:S(2)}) collective-permute-start(bf16[576,1024]{1,0:T(8,128)(2,1)} %collective-permute-done.8), channel_id=1, source_target_pairs={{0,4},{4,0},{8,12},{12,8},{16,20},{20,16},{24,28},{28,24},{1,5},{5... | collective-permute-start | bytes 3538952 | tf_op jit(solution)/shard_map/ppermute | solution.py:54
  148.6 60.5 %collective-permute-start.14 = (bf16[384,1024]{1,0:T(8,128)(2,1)S(1)}, bf16[384,1024]{1,0:T(8,128)(2,1)}, u32[]{:S(2)}, u32[]{:S(2)}) collective-permute-start(bf16[384,1024]{1,0:T(8,128)(2,1)S(1)} %copy-done.16), channel_id=1, source_target_pairs={{0,8},{4,12},{8,16},{12,20},{16,24},{20,28},{24,0},{28,4},{1,9},{5... | collective-permute-start | bytes 2359304 | tf_op jit(solution)/shard_map/ppermute | solution.py:59
  181.2 50.6 %collective-permute-start.20 = (bf16[576,1024]{1,0:T(8,128)(2,1)S(1)}, bf16[576,1024]{1,0:T(8,128)(2,1)}, u32[]{:S(2)}, u32[]{:S(2)}) collective-permute-start(bf16[576,1024]{1,0:T(8,128)(2,1)S(1)} %collective-permute-done.17), channel_id=1, source_target_pairs={{0,4},{4,0},{8,12},{12,8},{16,20},{20,16},{24,28},{28,24},{1,5},{5... | collective-permute-start | bytes 3538952 | tf_op jit(solution)/shard_map/ppermute | solution.py:54
  209.1 42.0 %collective-permute-start.18 = (bf16[384,1024]{1,0:T(8,128)(2,1)S(1)}, bf16[384,1024]{1,0:T(8,128)(2,1)}, u32[]{:S(2)}, u32[]{:S(2)}) collective-permute-start(bf16[384,1024]{1,0:T(8,128)(2,1)S(1)} %copy-done.16), channel_id=1, source_target_pairs={{0,4},{4,0},{8,12},{12,8},{16,20},{20,16},{24,28},{28,24},{1,5},{5... | collective-permute-start | bytes 2359304 | tf_op jit(solution)/shard_map/ppermute | solution.py:54
  209.5 41.6 %collective-permute-start.19 = (bf16[384,1024]{1,0:T(8,128)(2,1)}, bf16[384,1024]{1,0:T(8,128)(2,1)S(1)}, u32[]{:S(2)}, u32[]{:S(2)}) collective-permute-start(bf16[384,1024]{1,0:T(8,128)(2,1)} %collective-permute-done.14), channel_id=1, source_target_pairs={{0,8},{4,12},{8,16},{12,20},{16,24},{20,28},{24,0},{28,4},{1,9},{5... | collective-permute-start | bytes 2359304 | tf_op jit(solution)/shard_map/ppermute | solution.py:59
  274.5 40.3 %collective-permute-start.32 = (bf16[512,1024]{1,0:T(8,128)(2,1)}, bf16[512,1024]{1,0:T(8,128)(2,1)S(1)}, u32[]{:S(2)}, u32[]{:S(2)}) collective-permute-start(bf16[512,1024]{1,0:T(8,128)(2,1)} %collective-permute-done.31), channel_id=1, source_target_pairs={{0,1},{1,0},{2,3},{3,2},{4,5},{5,4},{6,7},{7,6},{8,9},{9,8},{10,11... | collective-permute-start | bytes 3145736 | tf_op jit(solution)/shard_map/ppermute | solution.py:54
  274.5 38.6 %collective-permute-start.30 = (bf16[512,1024]{1,0:T(8,128)(2,1)}, bf16[512,1024]{1,0:T(8,128)(2,1)S(1)}, u32[]{:S(2)}, u32[]{:S(2)}) collective-permute-start(bf16[512,1024]{1,0:T(8,128)(2,1)} %collective-permute-done.25), channel_id=1, source_target_pairs={{0,8},{4,12},{8,16},{12,20},{16,24},{20,28},{24,0},{28,4},{1,9},{5... | collective-permute-start | bytes 3145736 | tf_op jit(solution)/shard_map/ppermute | solution.py:59
  539.3 46.4 %collective-permute-start.65 = (bf16[128,1024]{0,1:T(8,128)(2,1)S(1)}, bf16[128,1024]{0,1:T(8,128)(2,1)}, u32[]{:S(2)}, u32[]{:S(2)}) collective-permute-start(bf16[128,1024]{0,1:T(8,128)(2,1)S(1)} %bitcast.332), channel_id=1, source_target_pairs={{0,4},{4,0},{8,12},{12,8},{16,20},{20,16},{24,28},{28,24},{1,5},{5... | collective-permute-start | bytes 786440 | tf_op jit(solution)/shard_map/ppermute | solution.py:54
  539.9 45.8 %collective-permute-start.66 = (bf16[512,1024]{1,0:T(8,128)(2,1)S(1)}, bf16[512,1024]{1,0:T(8,128)(2,1)}, u32[]{:S(2)}, u32[]{:S(2)}) collective-permute-start(bf16[512,1024]{1,0:T(8,128)(2,1)S(1)} %get-tuple-element.458), channel_id=1, source_target_pairs={{0,4},{4,0},{8,12},{12,8},{16,20},{20,16},{24,28},{28,24},{1,5},{5... | collective-permute-start | bytes 3145736 | tf_op jit(solution)/shard_map/ppermute | solution.py:54
  542.2 43.5 %collective-permute-start.67 = (bf16[128,1024]{0,1:T(8,128)(2,1)}, bf16[128,1024]{0,1:T(8,128)(2,1)}, u32[]{:S(2)}, u32[]{:S(2)}) collective-permute-start(bf16[128,1024]{0,1:T(8,128)(2,1)} %add_convert_fusion.8), channel_id=1, source_target_pairs={{0,8},{4,12},{8,16},{12,20},{16,24},{20,28},{24,0},{28,4},{1,9},{5... | collective-permute-start | bytes 786440 | tf_op jit(solution)/shard_map/ppermute | solution.py:59
  545.5 40.2 %collective-permute-start.68 = (bf16[512,1024]{1,0:T(8,128)(2,1)}, bf16[512,1024]{1,0:T(8,128)(2,1)}, u32[]{:S(2)}, u32[]{:S(2)}) collective-permute-start(bf16[512,1024]{1,0:T(8,128)(2,1)} %add_convert_fusion.3), channel_id=1, source_target_pairs={{0,8},{4,12},{8,16},{12,20},{16,24},{20,28},{24,0},{28,4},{1,9},{5... | collective-permute-start | bytes 3145736 | tf_op jit(solution)/shard_map/ppermute | solution.py:59
  651.9 46.5 %collective-permute-start.78 = (bf16[1040,1024]{1,0:T(8,128)(2,1)}, bf16[1040,1024]{1,0:T(8,128)(2,1)}, u32[]{:S(2)}, u32[]{:S(2)}) collective-permute-start(bf16[1040,1024]{1,0:T(8,128)(2,1)} %fusion.13), channel_id=1, source_target_pairs={{0,4},{4,0},{8,12},{12,8},{16,20},{20,16},{24,28},{28,24},{1,5},{5... | collective-permute-start | bytes 6389768 | tf_op jit(solution)/shard_map/ppermute | solution.py:54
  657.3 41.1 %collective-permute-start.79 = (bf16[1040,1024]{1,0:T(8,128)(2,1)}, bf16[1040,1024]{1,0:T(8,128)(2,1)}, u32[]{:S(2)}, u32[]{:S(2)}) collective-permute-start(bf16[1040,1024]{1,0:T(8,128)(2,1)} %add_convert_fusion.2), channel_id=1, source_target_pairs={{0,8},{4,12},{8,16},{12,20},{16,24},{20,28},{24,0},{28,4},{1,9},{5... | collective-permute-start | bytes 6389768 | tf_op jit(solution)/shard_map/ppermute | solution.py:59
  698.4 46.4 %collective-permute-start.80 = (bf16[1040,1024]{1,0:T(8,128)(2,1)}, bf16[1040,1024]{1,0:T(8,128)(2,1)}, u32[]{:S(2)}, u32[]{:S(2)}) collective-permute-start(bf16[1040,1024]{1,0:T(8,128)(2,1)} %get-tuple-element.511), channel_id=1, source_target_pairs={{0,4},{4,0},{8,12},{12,8},{16,20},{20,16},{24,28},{28,24},{1,5},{5... | collective-permute-start | bytes 6389768 | tf_op jit(solution)/shard_map/ppermute | solution.py:54
  705.4 39.4 %collective-permute-start.81 = (bf16[1040,1024]{1,0:T(8,128)(2,1)}, bf16[1040,1024]{1,0:T(8,128)(2,1)}, u32[]{:S(2)}, u32[]{:S(2)}) collective-permute-start(bf16[1040,1024]{1,0:T(8,128)(2,1)} %add_convert_fusion.1), channel_id=1, source_target_pairs={{0,8},{4,12},{8,16},{12,20},{16,24},{20,28},{24,0},{28,4},{1,9},{5... | collective-permute-start | bytes 6389768 | tf_op jit(solution)/shard_map/ppermute | solution.py:59
  744.8 44.4 %collective-permute-start.82 = (bf16[1040,1024]{1,0:T(8,128)(2,1)}, bf16[1040,1024]{1,0:T(8,128)(2,1)}, u32[]{:S(2)}, u32[]{:S(2)}) collective-permute-start(bf16[1040,1024]{1,0:T(8,128)(2,1)} %get-tuple-element.519), channel_id=1, source_target_pairs={{0,4},{4,0},{8,12},{12,8},{16,20},{20,16},{24,28},{28,24},{1,5},{5... | collective-permute-start | bytes 6389768 | tf_op jit(solution)/shard_map/ppermute | solution.py:54
  (127 other events, 2035.4 us)

commit v7 on v6

--- a/solution.py
+++ b/solution.py
@@ -404,7 +404,7 @@
     padded = outs + -outs % 128
     rows_six, rows_seven, rows_eight = w_six.shape[0], w_seven.shape[0], w_eight.shape[0]
     group_six, group_seven = features.shape[1] // rows_six, width // rows_seven
-    near_six = near_rows(rows_six, rings)
+    near_six = max(16, near_rows(rows_six, rings) - 16)
     bits = list(reversed(list(spread_bits("mp"))))
     far_bits, near_bit = bits[:-1], bits[-1]
 

time: 850 us -> 862 us (1.014)
  waiting for transfers between devices: 346 us -> 365 us
  starting transfers between devices: 82.1 us -> 68 us
  local copies, waits for them, and re-layouts: 106 us -> 115 us
    ppermute x66, waiting for transfers between devices: 303 us -> 316 us  [swap(): return lax.ppermute(value, axis, [(i, i ^ bit) for i in range(size)])]
    convert_element_type x16 -> x15, other arithmetic: 65.9 us -> 65 us  [soft_ternary(): return value.astype(jnp.bfloat16)]
  transfers between devices with their start and end apart: 90 -> 90, of which waited for: 48 -> 49; matrix products, arithmetic and copies ran while one was open for 40% -> 39% of each run, Pallas kernels for 0% -> 0%
where the time goes in v7:
time: 862 us; the launch traced here: 852 us
  waiting for transfers between devices  365 us (42%)
  other arithmetic  160 us (19%)
  matrix products  128 us (15%)
  local copies, waits for them, and re-layouts  115 us (13%)
  starting transfers between devices  68 us (8%)
  between operations  15.9 us (2%)
    ppermute x66, waiting for transfers between devices, swap(): return lax.ppermute(value, axis, [(i, i ^ bit) for i in range(size)])  316 us
    convert_element_type x15, other arithmetic, soft_ternary(): return value.astype(jnp.bfloat16)  65 us
    dynamic_update_slice x44, local copies, waits for them, and re-layouts, put(): return lax.dynamic_update_slice(whole, piece[None], (index, row, 0))  60 us
    ppermute x66, starting transfers between devices, swap(): return lax.ppermute(value, axis, [(i, i ^ bit) for i in range(size)])  53.3 us
    dot_general x3, matrix products, contract_rows(): lax.dot_general(left, right, (((0,), (0,)), ((), ())), preferred_element_...  51.5 us
    dot_general x14, matrix products, matmul(): return jnp.dot(left, right, preferred_element_type=jnp.float32)  50.1 us
    ppermute x24, waiting for transfers between devices, turn(): return lax.ppermute(value, 'dp', [(i, (i + 2) % size) for i in range(size)])  49.1 us
    convert_element_type x11, other arithmetic, narrow(): return value.astype(jnp.bfloat16)  28.7 us
  transfers between devices with their start and end apart: 90, of which 49 were waited for; matrix products, arithmetic and copies ran while one was open for 39% of the time, Pallas kernels for 0%

profile of v7, /device:TPU:0, one launch (start us, length us, event | category | flops | bytes accessed | tf_op | source)
XLA Modules:
  0.0 852.4 jit_solution(2616882126729050548)
XLA Ops:
  28.2 8.6 %collective-permute-done = bf16[576,1024]{1,0:T(8,128)(2,1)} collective-permute-done((bf16[576,1024]{1,0:T(8,128)(2,1)}, bf16[576,1024]{1,0:T(8,128)(2,1)}, u32[]{:S(2)}, u32[]{:S(2)}) %collective-permute-start) | collective-permute-done | bytes 1179680 | tf_op jit(solution)/shard_map/ppermute | solution.py:54
  54.5 7.6 collective-permute-done.5
  74.0 13.4 %collective-permute-done.3 = bf16[576,1024]{1,0:T(8,128)(2,1)} collective-permute-done((bf16[576,1024]{1,0:T(8,128)(2,1)}, bf16[576,1024]{1,0:T(8,128)(2,1)}, u32[]{:S(2)}, u32[]{:S(2)}) %collective-permute-start.3) | collective-permute-done | bytes 1179680 | tf_op jit(solution)/shard_map/ppermute | solution.py:54
  97.7 8.8 %collective-permute-done.11 = bf16[1024,2304]{1,0:T(8,128)(2,1)} collective-permute-done((bf16[1024,2304]{1,0:T(8,128)(2,1)}, bf16[1024,2304]{1,0:T(8,128)(2,1)}, u32[]{:S(2)}, u32[]{:S(2)}) %collective-permute-start.11) | collective-permute-done | bytes 4718624 | tf_op jit(solution)/shard_map/ppermute | solution.py:54
  124.0 20.9 %collective-permute-done.7 = bf16[576,1024]{1,0:T(8,128)(2,1)} collective-permute-done((bf16[576,1024]{1,0:T(8,128)(2,1)}, bf16[576,1024]{1,0:T(8,128)(2,1)}, u32[]{:S(2)}, u32[]{:S(2)}) %collective-permute-start.7) | collective-permute-done | bytes 1179680 | tf_op jit(solution)/shard_map/ppermute | solution.py:54
  148.7 9.7 %pad_maximum_fusion = bf16[1024,9216]{1,0:T(8,128)(2,1)S(1)} fusion(bf16[1024,2304]{1,0:T(8,128)(2,1)} %collective-permute-done.12, bf16[1024,2304]{1,0:T(8,128)(2,1)} %collective-permute-done.11, bf16[1024,2304]{1,0:T(8,128)(2,1)} %collective-permute-done.2, bf16[1024,2304]{1,0:T(8,128)(2,1)} %param.20), kind=kLoop, calls=%fused_computation.2 | loop fusion | flops 75497472 | bytes 37748736 | tf_op jit(solution)/shard_map/concatenate | solution.py:428
  165.6 15.7 %collective-permute-done.16 = bf16[256,1024]{1,0:T(8,128)(2,1)S(1)} collective-permute-done((bf16[256,1024]{1,0:T(8,128)(2,1)S(1)}, bf16[256,1024]{1,0:T(8,128)(2,1)S(1)}, u32[]{:S(2)}, u32[]{:S(2)}) %collective-permute-start.16) | collective-permute-done | bytes 524320 | tf_op jit(solution)/shard_map/ppermute | solution.py:54
  186.8 23.0 %fusion.117 = f32[1024,1024]{1,0:T(8,128)S(1)} fusion(bf16[1024,9216]{1,0:T(8,128)(2,1)S(1)} %pad_maximum_fusion, bf16[9216,1024]{1,0:T(8,128)(2,1)} %bitcast.20), kind=kOutput, calls=%fused_computation.289 | convolution fusion | flops 19327352832 | bytes 41943040 | tf_op jit(solution)/shard_map/dot_general | solution.py:20
  215.3 16.7 %collective-permute-done.20 = bf16[576,1024]{1,0:T(8,128)(2,1)} collective-permute-done((bf16[576,1024]{1,0:T(8,128)(2,1)S(1)}, bf16[576,1024]{1,0:T(8,128)(2,1)}, u32[]{:S(2)}, u32[]{:S(2)}) %collective-permute-start.20) | collective-permute-done | bytes 1179680 | tf_op jit(solution)/shard_map/ppermute | solution.py:54
  282.9 10.8 %collective-permute-done.28 = bf16[512,1024]{1,0:T(8,128)(2,1)S(1)} collective-permute-done((bf16[512,1024]{1,0:T(8,128)(2,1)S(1)}, bf16[512,1024]{1,0:T(8,128)(2,1)S(1)}, u32[]{:S(2)}, u32[]{:S(2)}) %collective-permute-start.28) | collective-permute-done | bytes 1048608 | tf_op jit(solution)/shard_map/ppermute | solution.py:54
  299.8 8.4 fusion.118
  348.9 9.8 %collective-permute-done.42 = f32[128,1024]{1,0:T(8,128)S(1)} collective-permute-done((f32[128,1024]{1,0:T(8,128)S(1)}, f32[128,1024]{1,0:T(8,128)S(1)}, u32[]{:S(2)}, u32[]{:S(2)}) %collective-permute-start.42) | collective-permute-done | bytes 524320 | tf_op jit(solution)/shard_map/ppermute | solution.py:54
  395.1 14.2 %abs_reduce_fusion.1 = (f32[]{:T(128)}, f32[]{:T(128)}, f32[4096,1024]{1,0:T(8,128)}) fusion(bf16[1024,1024]{1,0:T(8,128)(2,1)S(1)} %copy-done.20, bf16[512,4096]{1,0:T(8,128)(2,1)S(1)} %copy-done.13, bf16[512,4096]{1,0:T(8,128)(2,1)S(1)} %copy-done.29), kind=kOutput, calls=%fused_computation.3 | convolution fusion | flops 8623489024 | bytes 27262984 | tf_op jit(solution)/shard_map/dot_general | solution.py:24
  454.8 13.3 %collective-permute-done.51 = bf16[128,1024]{0,1:T(8,128)(2,1)} collective-permute-done((bf16[128,1024]{0,1:T(8,128)(2,1)}, bf16[128,1024]{0,1:T(8,128)(2,1)}, u32[]{:S(2)}, u32[]{:S(2)}) %collective-permute-start.51) | collective-permute-done | bytes 262176 | tf_op jit(solution)/shard_map/ppermute | solution.py:54
  488.4 10.4 %collective-permute-done.55 = bf16[128,1024]{0,1:T(8,128)(2,1)} collective-permute-done((bf16[128,1024]{0,1:T(8,128)(2,1)}, bf16[128,1024]{0,1:T(8,128)(2,1)}, u32[]{:S(2)}, u32[]{:S(2)}) %collective-permute-start.55) | collective-permute-done | bytes 262176 | tf_op jit(solution)/shard_map/ppermute | solution.py:54
  517.3 15.9 %collective-permute-done.60 = bf16[128,1024]{0,1:T(8,128)(2,1)S(1)} collective-permute-done((bf16[128,1024]{0,1:T(8,128)(2,1)}, bf16[128,1024]{0,1:T(8,128)(2,1)S(1)}, u32[]{:S(2)}, u32[]{:S(2)}) %collective-permute-start.60) | collective-permute-done | bytes 262176 | tf_op jit(solution)/shard_map/ppermute | solution.py:54
  533.2 7.5 collective-permute-done.62
  550.7 32.2 %abs_reduce_fusion = (f32[]{:T(128)}, f32[]{:T(128)}, f32[9216,1024]{1,0:T(8,128)}) fusion(bf16[1024,9216]{1,0:T(8,128)(2,1)} %copy-done.1, bf16[1024,1024]{1,0:T(8,128)(2,1)S(1)} %fusion.6), kind=kOutput, calls=%fused_computation | convolution fusion | flops 19365101568 | bytes 58720264 | tf_op jit(solution)/shard_map/dot_general | solution.py:24
  668.7 7.9 fusion.15
  676.6 33.7 %collective-permute-done.78 = bf16[1056,1024]{1,0:T(8,128)(2,1)} collective-permute-done((bf16[1056,1024]{1,0:T(8,128)(2,1)}, bf16[1056,1024]{1,0:T(8,128)(2,1)}, u32[]{:S(2)}, u32[]{:S(2)}) %collective-permute-start.78) | collective-permute-done | bytes 2162720 | tf_op jit(solution)/shard_map/ppermute | solution.py:54
  716.1 7.5 fusion.17
  723.6 33.9 %collective-permute-done.80 = bf16[1056,1024]{1,0:T(8,128)(2,1)} collective-permute-done((bf16[1056,1024]{1,0:T(8,128)(2,1)}, bf16[1056,1024]{1,0:T(8,128)(2,1)}, u32[]{:S(2)}, u32[]{:S(2)}) %collective-permute-start.80) | collective-permute-done | bytes 2162720 | tf_op jit(solution)/shard_map/ppermute | solution.py:54
  775.4 24.2 %collective-permute-done.84 = bf16[96,1024]{1,0:T(8,128)(2,1)S(1)} collective-permute-done((bf16[96,1024]{1,0:T(8,128)(2,1)}, bf16[96,1024]{1,0:T(8,128)(2,1)S(1)}, u32[]{:S(2)}, u32[]{:S(2)}) %collective-permute-start.84) | collective-permute-done | bytes 196640 | tf_op jit(solution)/shard_map/ppermute | solution.py:54
  830.6 12.8 %fusion.105 = (bf16[1152,1024]{1,0:T(8,128)(2,1)}, f32[1152,1024]{1,0:T(8,128)}, f32[1152,1024]{1,0:T(8,128)}, f32[1152,1024]{1,0:T(8,128)}) fusion(f32[1152,1024]{1,0:T(8,128)} %param.25, f32[96,1024]{1,0:T(8,128)S(1)} %convert_add_fusion.2, f32[1056,1024]{1,0:T(8,128)} %copy-done, f32[]{:T(128)} %bitcast.92, f32[]{:T(128)S(6)} %div.432, ...), kind=kLoop, calls=%fused_computation.278 | loop fusion | flops 21233664 | bytes 35389448 | tf_op jit(solution)/shard_map/convert_element_type | solution.py:723
  (451 shorter events, 469.6 us)
Async XLA Ops:
  1.2 105.3 %collective-permute-start.11 = (bf16[1024,2304]{1,0:T(8,128)(2,1)}, bf16[1024,2304]{1,0:T(8,128)(2,1)}, u32[]{:S(2)}, u32[]{:S(2)}) collective-permute-start(bf16[1024,2304]{1,0:T(8,128)(2,1)} %param.20), channel_id=1, source_target_pairs={{0,2},{1,3},{2,0},{3,1},{4,6},{5,7},{6,4},{7,5},{8,10},{9,11},{10,... | collective-permute-start | bytes 14155784 | tf_op jit(solution)/shard_map/ppermute | solution.py:54
  13.0 49.1 %collective-permute-start.5 = (bf16[576,1024]{1,0:T(8,128)(2,1)S(1)}, bf16[576,1024]{1,0:T(8,128)(2,1)}, u32[]{:S(2)}, u32[]{:S(2)}) collective-permute-start(bf16[576,1024]{1,0:T(8,128)(2,1)S(1)} %get-tuple-element.278), channel_id=1, source_target_pairs={{0,4},{4,0},{8,12},{12,8},{16,20},{20,16},{24,28},{28,24},{1,5},{5... | collective-permute-start | bytes 3538952 | tf_op jit(solution)/shard_map/ppermute | solution.py:54
  39.2 48.2 %collective-permute-start.3 = (bf16[576,1024]{1,0:T(8,128)(2,1)}, bf16[576,1024]{1,0:T(8,128)(2,1)}, u32[]{:S(2)}, u32[]{:S(2)}) collective-permute-start(bf16[576,1024]{1,0:T(8,128)(2,1)} %collective-permute-done.1), channel_id=1, source_target_pairs={{0,4},{4,0},{8,12},{12,8},{16,20},{20,16},{24,28},{28,24},{1,5},{5... | collective-permute-start | bytes 3538952 | tf_op jit(solution)/shard_map/ppermute | solution.py:54
  39.9 53.0 %collective-permute-start.4 = (bf16[576,1024]{1,0:T(8,128)(2,1)}, bf16[576,1024]{1,0:T(8,128)(2,1)}, u32[]{:S(2)}, u32[]{:S(2)}) collective-permute-start(bf16[576,1024]{1,0:T(8,128)(2,1)} %collective-permute-done.1), channel_id=1, source_target_pairs={{0,8},{4,12},{8,16},{12,20},{16,24},{20,28},{24,0},{28,4},{1,9},{5... | collective-permute-start | bytes 3538952 | tf_op jit(solution)/shard_map/ppermute | solution.py:59
  67.6 44.3 %collective-permute-start.9 = (bf16[576,1024]{1,0:T(8,128)(2,1)}, bf16[576,1024]{1,0:T(8,128)(2,1)}, u32[]{:S(2)}, u32[]{:S(2)}) collective-permute-start(bf16[576,1024]{1,0:T(8,128)(2,1)} %collective-permute-done.6), channel_id=1, source_target_pairs={{0,4},{4,0},{8,12},{12,8},{16,20},{20,16},{24,28},{28,24},{1,5},{5... | collective-permute-start | bytes 3538952 | tf_op jit(solution)/shard_map/ppermute | solution.py:54
  69.2 46.6 %collective-permute-start.10 = (bf16[576,1024]{1,0:T(8,128)(2,1)}, bf16[576,1024]{1,0:T(8,128)(2,1)}, u32[]{:S(2)}, u32[]{:S(2)}) collective-permute-start(bf16[576,1024]{1,0:T(8,128)(2,1)} %collective-permute-done.6), channel_id=1, source_target_pairs={{0,8},{4,12},{8,16},{12,20},{16,24},{20,28},{24,0},{28,4},{1,9},{5... | collective-permute-start | bytes 3538952 | tf_op jit(solution)/shard_map/ppermute | solution.py:59
  117.3 64.0 %collective-permute-start.15 = (bf16[576,1024]{1,0:T(8,128)(2,1)}, bf16[576,1024]{1,0:T(8,128)(2,1)S(1)}, u32[]{:S(2)}, u32[]{:S(2)}) collective-permute-start(bf16[576,1024]{1,0:T(8,128)(2,1)} %collective-permute-done.10), channel_id=1, source_target_pairs={{0,4},{4,0},{8,12},{12,8},{16,20},{20,16},{24,28},{28,24},{1,5},{5... | collective-permute-start | bytes 3538952 | tf_op jit(solution)/shard_map/ppermute | solution.py:54
  117.9 63.4 %collective-permute-start.17 = (bf16[576,1024]{1,0:T(8,128)(2,1)}, bf16[576,1024]{1,0:T(8,128)(2,1)S(1)}, u32[]{:S(2)}, u32[]{:S(2)}) collective-permute-start(bf16[576,1024]{1,0:T(8,128)(2,1)} %collective-permute-done.10), channel_id=1, source_target_pairs={{0,8},{4,12},{8,16},{12,20},{16,24},{20,28},{24,0},{28,4},{1,9},{5... | collective-permute-start | bytes 3538952 | tf_op jit(solution)/shard_map/ppermute | solution.py:59
  148.2 62.5 %collective-permute-start.13 = (bf16[576,1024]{1,0:T(8,128)(2,1)}, bf16[576,1024]{1,0:T(8,128)(2,1)}, u32[]{:S(2)}, u32[]{:S(2)}) collective-permute-start(bf16[576,1024]{1,0:T(8,128)(2,1)} %collective-permute-done.8), channel_id=1, source_target_pairs={{0,4},{4,0},{8,12},{12,8},{16,20},{20,16},{24,28},{28,24},{1,5},{5... | collective-permute-start | bytes 3538952 | tf_op jit(solution)/shard_map/ppermute | solution.py:54
  148.7 62.0 %collective-permute-start.14 = (bf16[384,1024]{1,0:T(8,128)(2,1)}, bf16[384,1024]{1,0:T(8,128)(2,1)}, u32[]{:S(2)}, u32[]{:S(2)}) collective-permute-start(bf16[384,1024]{1,0:T(8,128)(2,1)} %fusion.37), channel_id=1, source_target_pairs={{0,8},{4,12},{8,16},{12,20},{16,24},{20,28},{24,0},{28,4},{1,9},{5... | collective-permute-start | bytes 2359304 | tf_op jit(solution)/shard_map/ppermute | solution.py:59
  182.1 49.8 %collective-permute-start.20 = (bf16[576,1024]{1,0:T(8,128)(2,1)S(1)}, bf16[576,1024]{1,0:T(8,128)(2,1)}, u32[]{:S(2)}, u32[]{:S(2)}) collective-permute-start(bf16[576,1024]{1,0:T(8,128)(2,1)S(1)} %collective-permute-done.17), channel_id=1, source_target_pairs={{0,4},{4,0},{8,12},{12,8},{16,20},{20,16},{24,28},{28,24},{1,5},{5... | collective-permute-start | bytes 3538952 | tf_op jit(solution)/shard_map/ppermute | solution.py:54
  210.7 40.5 %collective-permute-start.18 = (bf16[384,1024]{1,0:T(8,128)(2,1)}, bf16[384,1024]{1,0:T(8,128)(2,1)S(1)}, u32[]{:S(2)}, u32[]{:S(2)}) collective-permute-start(bf16[384,1024]{1,0:T(8,128)(2,1)} %fusion.37), channel_id=1, source_target_pairs={{0,4},{4,0},{8,12},{12,8},{16,20},{20,16},{24,28},{28,24},{1,5},{5... | collective-permute-start | bytes 2359304 | tf_op jit(solution)/shard_map/ppermute | solution.py:54
  211.1 40.1 %collective-permute-start.19 = (bf16[384,1024]{1,0:T(8,128)(2,1)}, bf16[384,1024]{1,0:T(8,128)(2,1)S(1)}, u32[]{:S(2)}, u32[]{:S(2)}) collective-permute-start(bf16[384,1024]{1,0:T(8,128)(2,1)} %collective-permute-done.14), channel_id=1, source_target_pairs={{0,8},{4,12},{8,16},{12,20},{16,24},{20,28},{24,0},{28,4},{1,9},{5... | collective-permute-start | bytes 2359304 | tf_op jit(solution)/shard_map/ppermute | solution.py:59
  274.6 40.5 %collective-permute-start.32 = (bf16[512,1024]{1,0:T(8,128)(2,1)}, bf16[512,1024]{1,0:T(8,128)(2,1)S(1)}, u32[]{:S(2)}, u32[]{:S(2)}) collective-permute-start(bf16[512,1024]{1,0:T(8,128)(2,1)} %collective-permute-done.31), channel_id=1, source_target_pairs={{0,1},{1,0},{2,3},{3,2},{4,5},{5,4},{6,7},{7,6},{8,9},{9,8},{10,11... | collective-permute-start | bytes 3145736 | tf_op jit(solution)/shard_map/ppermute | solution.py:54
  274.6 38.8 %collective-permute-start.30 = (bf16[512,1024]{1,0:T(8,128)(2,1)}, bf16[512,1024]{1,0:T(8,128)(2,1)S(1)}, u32[]{:S(2)}, u32[]{:S(2)}) collective-permute-start(bf16[512,1024]{1,0:T(8,128)(2,1)} %collective-permute-done.25), channel_id=1, source_target_pairs={{0,8},{4,12},{8,16},{12,20},{16,24},{20,28},{24,0},{28,4},{1,9},{5... | collective-permute-start | bytes 3145736 | tf_op jit(solution)/shard_map/ppermute | solution.py:59
  540.8 46.3 %collective-permute-start.65 = (bf16[128,1024]{0,1:T(8,128)(2,1)S(1)}, bf16[128,1024]{0,1:T(8,128)(2,1)}, u32[]{:S(2)}, u32[]{:S(2)}) collective-permute-start(bf16[128,1024]{0,1:T(8,128)(2,1)S(1)} %bitcast.330), channel_id=1, source_target_pairs={{0,4},{4,0},{8,12},{12,8},{16,20},{20,16},{24,28},{28,24},{1,5},{5... | collective-permute-start | bytes 786440 | tf_op jit(solution)/shard_map/ppermute | solution.py:54
  541.4 45.6 %collective-permute-start.66 = (bf16[512,1024]{1,0:T(8,128)(2,1)S(1)}, bf16[512,1024]{1,0:T(8,128)(2,1)}, u32[]{:S(2)}, u32[]{:S(2)}) collective-permute-start(bf16[512,1024]{1,0:T(8,128)(2,1)S(1)} %get-tuple-element.458), channel_id=1, source_target_pairs={{0,4},{4,0},{8,12},{12,8},{16,20},{20,16},{24,28},{28,24},{1,5},{5... | collective-permute-start | bytes 3145736 | tf_op jit(solution)/shard_map/ppermute | solution.py:54
  543.7 43.4 %collective-permute-start.67 = (bf16[128,1024]{0,1:T(8,128)(2,1)}, bf16[128,1024]{0,1:T(8,128)(2,1)}, u32[]{:S(2)}, u32[]{:S(2)}) collective-permute-start(bf16[128,1024]{0,1:T(8,128)(2,1)} %add_convert_fusion.8), channel_id=1, source_target_pairs={{0,8},{4,12},{8,16},{12,20},{16,24},{20,28},{24,0},{28,4},{1,9},{5... | collective-permute-start | bytes 786440 | tf_op jit(solution)/shard_map/ppermute | solution.py:59
  546.8 40.2 %collective-permute-start.68 = (bf16[512,1024]{1,0:T(8,128)(2,1)}, bf16[512,1024]{1,0:T(8,128)(2,1)}, u32[]{:S(2)}, u32[]{:S(2)}) collective-permute-start(bf16[512,1024]{1,0:T(8,128)(2,1)} %add_convert_fusion.3), channel_id=1, source_target_pairs={{0,8},{4,12},{8,16},{12,20},{16,24},{20,28},{24,0},{28,4},{1,9},{5... | collective-permute-start | bytes 3145736 | tf_op jit(solution)/shard_map/ppermute | solution.py:59
  663.2 47.2 %collective-permute-start.78 = (bf16[1056,1024]{1,0:T(8,128)(2,1)}, bf16[1056,1024]{1,0:T(8,128)(2,1)}, u32[]{:S(2)}, u32[]{:S(2)}) collective-permute-start(bf16[1056,1024]{1,0:T(8,128)(2,1)} %fusion.13), channel_id=1, source_target_pairs={{0,4},{4,0},{8,12},{12,8},{16,20},{20,16},{24,28},{28,24},{1,5},{5... | collective-permute-start | bytes 6488072 | tf_op jit(solution)/shard_map/ppermute | solution.py:54
  667.5 42.9 %collective-permute-start.79 = (bf16[1056,1024]{1,0:T(8,128)(2,1)}, bf16[1056,1024]{1,0:T(8,128)(2,1)}, u32[]{:S(2)}, u32[]{:S(2)}) collective-permute-start(bf16[1056,1024]{1,0:T(8,128)(2,1)} %add_convert_fusion.2), channel_id=1, source_target_pairs={{0,8},{4,12},{8,16},{12,20},{16,24},{20,28},{24,0},{28,4},{1,9},{5... | collective-permute-start | bytes 6488072 | tf_op jit(solution)/shard_map/ppermute | solution.py:59
  710.4 47.1 %collective-permute-start.80 = (bf16[1056,1024]{1,0:T(8,128)(2,1)}, bf16[1056,1024]{1,0:T(8,128)(2,1)}, u32[]{:S(2)}, u32[]{:S(2)}) collective-permute-start(bf16[1056,1024]{1,0:T(8,128)(2,1)} %get-tuple-element.511), channel_id=1, source_target_pairs={{0,4},{4,0},{8,12},{12,8},{16,20},{20,16},{24,28},{28,24},{1,5},{5... | collective-permute-start | bytes 6488072 | tf_op jit(solution)/shard_map/ppermute | solution.py:54
  716.1 41.4 %collective-permute-start.81 = (bf16[1056,1024]{1,0:T(8,128)(2,1)}, bf16[1056,1024]{1,0:T(8,128)(2,1)}, u32[]{:S(2)}, u32[]{:S(2)}) collective-permute-start(bf16[1056,1024]{1,0:T(8,128)(2,1)} %add_convert_fusion.1), channel_id=1, source_target_pairs={{0,8},{4,12},{8,16},{12,20},{16,24},{20,28},{24,0},{28,4},{1,9},{5... | collective-permute-start | bytes 6488072 | tf_op jit(solution)/shard_map/ppermute | solution.py:59
  757.5 42.1 %collective-permute-start.82 = (bf16[1056,1024]{1,0:T(8,128)(2,1)}, bf16[1056,1024]{1,0:T(8,128)(2,1)}, u32[]{:S(2)}, u32[]{:S(2)}) collective-permute-start(bf16[1056,1024]{1,0:T(8,128)(2,1)} %get-tuple-element.519), channel_id=1, source_target_pairs={{0,4},{4,0},{8,12},{12,8},{16,20},{20,16},{24,28},{28,24},{1,5},{5... | collective-permute-start | bytes 6488072 | tf_op jit(solution)/shard_map/ppermute | solution.py:54
  (119 other events, 2064.6 us)
